TPU v7x, 256 devices: a whole 4x4x8 slice. The times are simulated.
256 devices in a mesh: blk: 8 (over x_lo, y), grp: 32 (over z, x_hi, core).
Axes of the slice: x: 4 (x_hi: 2, x_lo: 2; x = x_hi * 2 + x_lo), y: 4, z: 8, core: 2. Of those that a mesh axis runs over, the one named last changes fastest.
Arguments:
- batch: bfloat16 [1024, 768], P('blk'), may hold values from -6 to 6
- targets: float32 [1024, 512], P('blk'), may hold values from -6 to 6
- centers: bfloat16 [262144, 768], P(('blk', 'grp')), may hold values from -6 to 6
- weights: float32 [262144, 512], P(('blk', 'grp')), may hold values from -32 to 32
- eigvec: float32 [16384, 160], P(('blk', 'grp')), may hold values from -0.375 to 0.375
- eig_scale: float32 [160], replicated, may hold values from 0.05 to 0.95
- step: float32 [1], replicated, may hold values from 122.07031 to 366.21094
Outputs:
- predictions: float32 [1024, 512], P('blk')
- new_weights: float32 [262144, 512], P(('blk', 'grp'))
All inputs are finite; a program needn't handle non-finite values.
Results may differ from a plain program's by a relative error of at most 0.00075.
Values may be sent and summed in bfloat16 or wider, within the bound.
No kernel may reach another device: no remote copies, remote signals or barrier semaphores. Data moves between devices by JAX's collectives and lax.ppermute only.
A program may use at most 64 MiB of HBM per device.

v0:
```python
import jax
import jax.numpy as jnp
from jax import lax
from jax.sharding import PartitionSpec as P


def kernel_block(cen, rows):
    cen_sq = jnp.sum(cen.astype(jnp.float32) ** 2, axis=1)
    row_sq = jnp.sum(rows.astype(jnp.float32) ** 2, axis=1)
    cross = jnp.dot(cen, rows.T, preferred_element_type=jnp.float32)
    dist = cen_sq[:, None] + row_sq[None, :] - 2.0 * cross
    return jnp.exp(-dist * (4.0 / cen.shape[1]))


def apply_weights(kern, weights):
    return lax.dot_general(
        kern,
        weights,
        (((0,), (0,)), ((), ())),
        precision=lax.Precision.HIGHEST,
        preferred_element_type=jnp.float32,
    )


def local(batch, targets, centers, weights, eigvec, eig_scale, step):
    partial_value = apply_weights(
        kernel_block(centers, lax.all_gather(batch, "blk", axis=0, tiled=True)), weights
    )
    summed = lax.psum(partial_value, "grp")
    predictions = lax.psum_scatter(summed, "blk", scatter_dimension=0, tiled=True)
    residual = predictions - targets
    kern = kernel_block(centers, lax.all_gather(batch, "blk", axis=0, tiled=True))
    grad = jnp.dot(
        kern,
        lax.all_gather(residual.astype(jnp.bfloat16), "blk", axis=0, tiled=True).astype(
            jnp.float32
        ),
        precision=lax.Precision.HIGHEST,
        preferred_element_type=jnp.float32,
    )
    nys_rows = eigvec.shape[0]
    grad_sub = grad[:nys_rows]
    local_proj = lax.dot_general(
        eigvec,
        grad_sub,
        (((0,), (0,)), ((), ())),
        precision=lax.Precision.HIGHEST,
        preferred_element_type=jnp.float32,
    )
    proj = lax.psum(local_proj, ("blk", "grp"))
    corr = jnp.dot(
        eigvec,
        eig_scale[:, None] * proj,
        precision=lax.Precision.HIGHEST,
        preferred_element_type=jnp.float32,
    )
    precond = jnp.concatenate([grad_sub - corr, grad[nys_rows:]], axis=0)
    new_weights = weights - step[0] * precond
    return (predictions, new_weights)


def solution(mesh):
    return jax.shard_map(
        local,
        mesh=mesh,
        in_specs=(
            P("blk", None),
            P("blk", None),
            P(("blk", "grp"), None),
            P(("blk", "grp"), None),
            P(("blk", "grp"), None),
            P(),
            P(),
        ),
        out_specs=(P("blk", None), P(("blk", "grp"), None)),
        check_vma=False,
    )
```

profile of v0, /device:TPU:1, one launch (start us, length us, event | category | flops | bytes accessed | tf_op | source)
XLA Modules:
  0.0 691.8 jit_solution(12008289889637022627)
XLA Ops:
  7.2 0.0 all-gather.3.cloned.1.call-start
  7.2 0.7 all-gather.3.cloned.1.call-update
  7.9 0.0 reduce-scatter.2.cloned.1.call-start
  8.0 1.8 multiply_reduce_fusion.1
  9.8 40.8 %all-gather.3.cloned.1.call-done = bf16[1024,768]{1,0:T(8,128)(2,1)} async-done(((bf16[128,768]{1,0:T(8,128)(2,1)}), bf16[1024,768]{1,0:T(8,128)(2,1)}) %all-gather.3.cloned.1.call-update) | async-done | bytes 1572880 | tf_op jit(solution)/shard_map/all_gather | solution.py:27
  50.6 3.8 fusion.19
  54.4 0.4 multiply_reduce_fusion
  54.8 1.5 copy-done.7
  56.3 8.8 %fusion.1 = f32[1024,512]{1,0:T(8,128)} fusion(f32[1024,512]{1,0:T(8,128)S(1)} %copy-done.2, f32[1024,1024]{1,0:T(8,128)S(1)} %fusion.19, f32[1024]{0:T(1024)S(1)} %multiply_reduce_fusion, f32[1024]{0:T(1024)S(1)} %multiply_reduce_fusion.1), kind=kOutput, calls=%fused_computation.4 | convolution fusion | flops 6447693824 | bytes 8396800 | tf_op jit(solution)/shard_map/dot_general | solution.py:16
  65.2 0.0 all-reduce.5.cloned.1.call-start
  65.2 45.2 %reduce-scatter.2.cloned.1.call-done = f32[128,512]{1,0:T(8,128)} async-done(((f32[1024,512]{1,0:T(8,128)}), f32[128,512]{1,0:T(8,128)}) %reduce-scatter.2.cloned.1.call-update) | async-done | bytes 262160 | tf_op jit(solution)/shard_map/reduce_scatter | solution.py:30
  110.5 0.0 all-gather.5.cloned.1.call-start
  110.6 272.9 %all-reduce.5.cloned.1.call-done = f32[128,512]{1,0:T(8,128)} async-done(((f32[128,512]{1,0:T(8,128)}), f32[128,512]{1,0:T(8,128)}) %all-reduce.5.cloned.1.call-update) | async-done | bytes 262160 | tf_op jit(solution)/shard_map/psum | solution.py:29
  383.5 1.6 subtract_convert_fusion
  385.1 0.2 all-reduce.3.cloned.1.call-start
  385.4 35.9 %all-gather.5.cloned.1.call-done = bf16[1024,512]{1,0:T(8,128)(2,1)} async-done(((bf16[128,512]{1,0:T(8,128)(2,1)}), bf16[1024,512]{1,0:T(8,128)(2,1)}) %all-gather.5.cloned.1.call-update) | async-done | bytes 1048592 | tf_op jit(solution)/shard_map/all_gather | solution.py:35
  421.2 6.0 fusion
  427.3 1.3 copy-done.1
  428.6 1.2 convolution_bitcast_fusion
  430.5 1.7 slice.9
  432.2 247.5 %all-reduce.3.cloned.1.call-done = f32[160,512]{1,0:T(8,128)} async-done(((f32[160,512]{1,0:T(8,128)}), f32[160,512]{1,0:T(8,128)}) %all-reduce.3.cloned.1.call-update) | async-done | bytes 327696 | tf_op jit(solution)/shard_map/psum | solution.py:50
  679.7 1.4 fusion.11
  681.2 3.4 fusion.2
  684.6 0.7 copy.12
  (18 shorter events, 0.1 us)
Async XLA Ops:
  7.2 421.4 %copy-start = (f32[64,160]{1,0:T(8,128)S(1)}, f32[64,160]{1,0:T(8,128)}, u32[]{:S(2)}) copy-start(f32[64,160]{1,0:T(8,128)} %param.11) | copy-start | bytes 122884
  7.2 43.4 %all-gather.3.cloned.1.call-start = ((), (), s32[]{:S(2)}) async-start(), calls=%async_computation.1 | async-start | bytes 1769472 | tf_op jit(solution)/shard_map/all_gather | solution.py:27
  7.9 102.6 %reduce-scatter.2.cloned.1.call-start = ((), (), s32[]{:S(2)}) async-start(), calls=%async_computation.4 | async-start | bytes 2359296 | tf_op jit(solution)/shard_map/reduce_scatter | solution.py:30
  9.7 46.6 %copy-start.2 = (f32[1024,512]{1,0:T(8,128)S(1)}, f32[1024,512]{1,0:T(8,128)}, u32[]{:S(2)}) copy-start(f32[1024,512]{1,0:T(8,128)} %param.10) | copy-start | bytes 6291460
  50.6 3.8 copy-start.3
  54.4 1.9 copy-start.7
  56.3 327.1 %copy-start.5 = (f32[128,512]{1,0:T(8,128)S(1)}, f32[128,512]{1,0:T(8,128)}, u32[]{:S(2)}) copy-start(f32[128,512]{1,0:T(8,128)} %param.8) | copy-start | bytes 786436
  65.2 318.3 %all-reduce.5.cloned.1.call-start = ((), (), s32[]{:S(2)}) async-start(), calls=%async_computation.5 | async-start | bytes 524288 | tf_op jit(solution)/shard_map/psum | solution.py:29
  110.5 310.7 %all-gather.5.cloned.1.call-start = ((), (), s32[]{:S(2)}) async-start(), calls=%async_computation.2 | async-start | bytes 1179648 | tf_op jit(solution)/shard_map/all_gather | solution.py:35
  385.1 294.6 %all-reduce.3.cloned.1.call-start = ((), (), s32[]{:S(2)}) async-start(), calls=%async_computation.3 | async-start | bytes 655360 | tf_op jit(solution)/shard_map/psum | solution.py:50
  427.3 1.3 copy-start.1
  428.6 251.1 %copy-start.6 = (f32[160]{0:T(256)S(1)}, f32[160]{0:T(256)}, u32[]{:S(2)}) copy-start(f32[160]{0:T(256)} %param.12) | copy-start | bytes 1924
  681.2 3.5 copy-start.4
Sparse Core Ops, SparseCore 0:
  9.8 40.7 all-gather.2
  65.3 45.1 reduce-scatter.1
  113.1 270.3 all-reduce.4
  385.8 35.3 all-gather.4
  430.0 249.7 all-reduce.2
where the time goes:
time: 692 us
  waiting for transfers between devices  643 us (93%)
  matrix products  21.3 us (3%)
  between operations  14.5 us (2%)
  other arithmetic  7.25 us (1%)
    psum x1, waiting for transfers between devices, local(): summed = lax.psum(partial_value, 'grp')  273 us
    psum x1, waiting for transfers between devices, local(): proj = lax.psum(local_proj, ('blk', 'grp'))  248 us
    reduce_scatter x1, waiting for transfers between devices, local(): lax.psum_scatter(summed, 'blk', scatter_dimension=0, tiled=True)  45.2 us
    all_gather x1, waiting for transfers between devices, local(): lax.all_gather(batch, 'blk', axis=0, tiled=True)  40.8 us
    all_gather x1, waiting for transfers between devices, local(): lax.all_gather(residual.astype(jnp.bfloat16), 'blk', axis=0, tiled=True)  35.9 us
  transfers between devices with their start and end apart: 5, of which 5 were waited for; matrix products, arithmetic and copies ran while one was open for 1% of the time, Pallas kernels for 0%

commit v1 on v0

v1 whole, which is shorter than its diff:
```python
import jax
import jax.numpy as jnp
import numpy as np
from jax import lax
from jax.sharding import Mesh, PartitionSpec as P

AXES = ("xl", "y", "z", "xh", "c")
BLK = ("xl", "y")
RING = ("z", "xh")
ALL = P(AXES, None)


def sq_norm(rows):
    return jnp.sum(rows.astype(jnp.float32) ** 2, axis=1)


def kernel_block(cen, cen_sq, rows):
    cross = jnp.dot(cen, rows.T, preferred_element_type=jnp.float32)
    dist = cen_sq[:, None] + sq_norm(rows)[None, :] - 2.0 * cross
    return jnp.exp(-dist * (4.0 / cen.shape[1]))


def contract_rows(a, b, precision=lax.Precision.HIGH):
    return lax.dot_general(
        a, b, (((0,), (0,)), ((), ())), precision=precision, preferred_element_type=jnp.float32
    )


def swap_cores(value):
    return lax.ppermute(value, "c", [(0, 1), (1, 0)])


def spread(value, axes, size):
    return lax.all_to_all(
        jnp.broadcast_to(value[None], (size,) + value.shape), axes, 0, 0, tiled=True
    )


def local(batch, targets, centers, weights, eigvec, eig_scale, step):
    core = lax.axis_index("c")
    slot = lax.axis_index(RING)
    nys = eigvec.shape[0]
    q = eigvec.shape[1]
    c_dim = weights.shape[1]
    half = batch.shape[0] // 2

    own_rows = lax.dynamic_slice_in_dim(batch, core * half, half, 0)
    mine = spread(own_rows, BLK, 8).reshape(8 * half, -1)
    other = swap_cores(mine)
    cen_sq = sq_norm(centers)

    k_other = kernel_block(centers, cen_sq, other)
    k_mine = kernel_block(centers, cen_sq, mine)

    def terms(kern):
        value = contract_rows(kern, weights)
        coef = contract_rows(kern[:nys], eigvec)
        return jnp.concatenate([value, coef], axis=1)

    summed = terms(k_mine) + swap_cores(terms(k_other))
    wide = c_dim + q
    summed = lax.all_to_all(summed.reshape(8, half, wide), BLK, 0, 0, tiled=True).sum(0)
    part = half // 16
    pieces = summed.reshape(16, part, wide)
    pieces = lax.all_to_all(pieces, RING, 0, 0, tiled=True).sum(0)

    whole = spread(pieces, RING, 16).reshape(half, wide)
    own_pred = whole[:, :c_dim]
    other_pred = swap_cores(own_pred)
    predictions = jnp.where(
        core == 0,
        jnp.concatenate([own_pred, other_pred], axis=0),
        jnp.concatenate([other_pred, own_pred], axis=0),
    )
    own_targets = lax.dynamic_slice_in_dim(targets, core * half, half, 0)
    packed = jnp.concatenate([own_pred - own_targets, whole[:, c_dim:]], axis=1).astype(
        jnp.bfloat16
    )
    got_mine = spread(packed, BLK, 8).reshape(8 * half, wide)
    got_other = swap_cores(got_mine)

    scaled = eigvec * eig_scale[None, :]

    def gradient(kern, got):
        resid, coef = got[:, :c_dim], got[:, c_dim:]
        corr = lax.dot_general(
            scaled,
            coef.astype(jnp.float32),
            (((1,), (1,)), ((), ())),
            precision=lax.Precision.HIGH,
            preferred_element_type=jnp.float32,
        )
        kern = jnp.concatenate([kern[:nys] - corr, kern[nys:]], axis=0)
        return jnp.dot(kern.astype(jnp.bfloat16), resid, preferred_element_type=jnp.float32)

    precond = gradient(k_mine, got_mine) + gradient(k_other, got_other)
    new_weights = weights - step[0] * precond
    return (predictions, new_weights)


def solution(mesh):
    fine = Mesh(mesh.devices.reshape(2, 4, 8, 2, 2), AXES)
    return jax.shard_map(
        local,
        mesh=fine,
        in_specs=(P(BLK, None), P(BLK, None), ALL, ALL, ALL, P(), P()),
        out_specs=(P(BLK, None), ALL),
        check_vma=False,
    )
```

time: 692 us -> 132 us (0.19)
  waiting for transfers between devices: 643 us -> 5.9 us
  blocking collectives: 0 us -> 76 us
  starting transfers between devices: 0.38 us -> 15.6 us
  between operations: 14.5 us -> 1.68 us
    psum x2 -> x0, waiting for transfers between devices: 520 us -> none  [the longest x1 273 us: local(): summed = lax.psum(partial_value, 'grp')]
    all_gather x2 -> x0, waiting for transfers between devices: 76.7 us -> none  [the longest x1 40.8 us: local(): lax.all_gather(batch, 'blk', axis=0, tiled=True)]
    all_to_all x0 -> x4, blocking collectives: none -> 76 us  [the longest x2 30.6 us: spread(): lax.all_to_all(jnp.broadcast_to(value[None], (size,) + value.shape), axes...]
    reduce_scatter x1 -> x0, waiting for transfers between devices: 45.2 us -> none  [local(): lax.psum_scatter(summed, 'blk', scatter_dimension=0, tiled=True)]
    ppermute x0 -> x4, starting transfers between devices: none -> 11.7 us  [swap_cores(): return lax.ppermute(value, 'c', [(0, 1), (1, 0)])]
    dot_general x4 -> x8, matrix products: 17.5 us -> 12.1 us  [the longest x2 5.17 us: gradient(): jnp.dot(kern.astype(jnp.bfloat16), resid, preferred_element_type=jnp.floa...]
  transfers between devices with their start and end apart: 5 -> 5, of which waited for: 5 -> 2; matrix products, arithmetic and copies ran while one was open for 1% -> 10% of each run, Pallas kernels for 0% -> 0%
where the time goes in v1:
time: 132 us
  blocking collectives  76 us (58%)
  matrix products  15.7 us (12%)
  starting transfers between devices  15.6 us (12%)
  local copies, waits for them, and re-layouts  9.5 us (7%)
  other arithmetic  7.12 us (5%)
  waiting for transfers between devices  5.9 us (4%)
  between operations  1.68 us (1%)
    all_to_all x2, blocking collectives, spread(): lax.all_to_all(jnp.broadcast_to(value[None], (size,) + value.shape), axes...  30.6 us
    all_to_all x1, blocking collectives, local(): lax.all_to_all(summed.reshape(8, half, wide), BLK, 0, 0, tiled=True).sum(0)  24.6 us
    all_to_all x1, blocking collectives, local(): pieces = lax.all_to_all(pieces, RING, 0, 0, tiled=True).sum(0)  20.8 us
    ppermute x4, starting transfers between devices, swap_cores(): return lax.ppermute(value, 'c', [(0, 1), (1, 0)])  11.7 us
    dot_general x2, matrix products, gradient(): jnp.dot(kern.astype(jnp.bfloat16), resid, preferred_element_type=jnp.floa...  5.17 us
    dot_general x4, matrix products, contract_rows(): lax.dot_general(a, b, (((0,), (0,)), ((), ())), precision=precision, pref...  4.38 us
    all_to_all x1, waiting for transfers between devices, spread(): lax.all_to_all(jnp.broadcast_to(value[None], (size,) + value.shape), axes...  4.36 us
    all_to_all x1, starting transfers between devices, spread(): lax.all_to_all(jnp.broadcast_to(value[None], (size,) + value.shape), axes...  3.92 us
  transfers between devices with their start and end apart: 5, of which 2 were waited for; matrix products, arithmetic and copies ran while one was open for 10% of the time, Pallas kernels for 0%

profile of v1, /device:TPU:1, one launch (start us, length us, event | category | flops | bytes accessed | tf_op | source)
XLA Modules:
  0.0 131.5 jit_solution(15428525717554522222)
XLA Ops:
  1.6 17.4 %all_to_all.25 = bf16[8,64,768]{2,1,0:T(8,128)(2,1)S(1)} all-to-all(bf16[8,64,768]{2,1,0:T(8,128)(2,1)S(1)} %broadcast_in_dim.6), channel_id=1, replica_groups=mesh['xl'=2,'y'=4,'z'=8,'xh'=2,'c'=2] {'xl','y'}, dimensions={0} | all-to-all | bytes 1572864 | tf_op jit(solution)/shard_map/all_to_all | solution.py:34
  19.0 2.4 %collective-permute-start = (bf16[512,768]{1,0:T(8,128)(2,1)S(1)}, bf16[512,768]{1,0:T(8,128)(2,1)S(1)}, u32[]{:S(2)}, u32[]{:S(2)}) collective-permute-start(bf16[512,768]{1,0:T(8,128)(2,1)S(1)} %bitcast.35), channel_id=1, source_target_pairs={{0,1},{1,0},{2,3},{3,2},{4,5},{5,4},{6,7},{7,6},{8,9},{9,8},{10,11... | collective-permute-start | bytes 2359304 | tf_op jit(solution)/shard_map/ppermute | solution.py:30
  21.8 1.5 %collective-permute-done = bf16[512,768]{1,0:T(8,128)(2,1)S(1)} collective-permute-done((bf16[512,768]{1,0:T(8,128)(2,1)S(1)}, bf16[512,768]{1,0:T(8,128)(2,1)S(1)}, u32[]{:S(2)}, u32[]{:S(2)}) %collective-permute-start) | collective-permute-done | bytes 786464 | tf_op jit(solution)/shard_map/ppermute | solution.py:30
  23.5 1.1 fusion.2
  25.1 1.9 %fusion.30 = f32[512,512]{0,1:T(8,128)S(1)} fusion(f32[1024,512]{0,1:T(8,128)S(1)} %fusion.2, f32[1024,512]{1,0:T(8,128)S(1)} %copy-done.1), kind=kOutput, calls=%fused_computation.47 | convolution fusion | flops 1610612736 | bytes 5242880 | tf_op jit(solution)/shard_map/dot_general | solution.py:24
  27.4 1.2 pad_maximum_fusion
  29.2 2.5 %fusion.5 = f32[1024,512]{0,1:T(8,128)S(1)} fusion(bf16[512,768]{1,0:T(8,128)(2,1)S(1)} %bitcast.36, bf16[1024,768]{1,0:T(8,128)(2,1)} %param.9, f32[512]{0:T(512)S(1)} %add.38, f32[1024]{0:T(1024)S(1)} %multiply_reduce_fusion), kind=kOutput, calls=%fused_computation.10 | convolution fusion | flops 807927808 | bytes 4462592 | tf_op jit(solution)/shard_map/dot_general | solution.py:18
  32.1 1.9 %fusion.29 = f32[512,512]{0,1:T(8,128)S(1)} fusion(f32[1024,512]{0,1:T(8,128)S(1)} %fusion.5, f32[1024,512]{1,0:T(8,128)S(1)} %copy-done.1), kind=kOutput, calls=%fused_computation.46 | convolution fusion | flops 1610612736 | bytes 5242880 | tf_op jit(solution)/shard_map/dot_general | solution.py:24
  34.0 2.7 %maximum_add_fusion = f32[512,672]{0,1:T(8,128)} fusion(f32[512,672]{0,1:T(8,128)} %collective-permute-done.1, f32[512,160]{0,1:T(8,128)S(1)} %fusion.20, f32[512,512]{0,1:T(8,128)S(1)} %fusion.29), kind=kLoop, calls=%fused_computation.14 | loop fusion | flops 688128 | bytes 4128768 | tf_op jit(solution)/shard_map/add | solution.py:60
  36.7 2.9 %copy.22 = f32[512,672]{1,0:T(8,128)} copy(f32[512,672]{0,1:T(8,128)} %maximum_add_fusion) | data formatting | bytes 2752512 | tf_op jit(solution)/shard_map/add | solution.py:60
  39.7 24.6 %all_to_all.26 = f32[8,64,672]{2,1,0:T(8,128)} all-to-all(f32[8,64,672]{2,1,0:T(8,128)} %bitcast.31), channel_id=1, replica_groups=mesh['xl'=2,'y'=4,'z'=8,'xh'=2,'c'=2] {'xl','y'}, dimensions={0} | all-to-all | bytes 2752512 | tf_op jit(solution)/shard_map/all_to_all | solution.py:62
  64.3 1.5 %reduce_sum.48 = f32[64,672]{1,0:T(8,128)S(1)} reduce(f32[8,64,672]{2,1,0:T(8,128)} %all_to_all.26, f32[]{:T(128)} %constant.2.clone.1), dimensions={0}, to_apply=%region_3.0 | reduce | flops 301056 | bytes 1548292 | tf_op jit(solution)/shard_map/reduce_sum | solution.py:62
  65.9 20.8 %all_to_all.27 = f32[16,4,672]{2,1,0:T(4,128)S(1)} all-to-all(f32[16,4,672]{2,1,0:T(4,128)S(1)} %reshape.44), channel_id=1, replica_groups=mesh['xl'=2,'y'=4,'z'=8,'xh'=2,'c'=2] {'z','xh'}, dimensions={0} | all-to-all | bytes 344064 | tf_op jit(solution)/shard_map/all_to_all | solution.py:65
  86.8 13.2 %all_to_all.28 = f32[16,4,672]{2,1,0:T(4,128)S(1)} all-to-all(f32[16,4,672]{2,1,0:T(4,128)S(1)} %broadcast_in_dim.7), channel_id=1, replica_groups=mesh['xl'=2,'y'=4,'z'=8,'xh'=2,'c'=2] {'z','xh'}, dimensions={0} | all-to-all | bytes 344064 | tf_op jit(solution)/shard_map/all_to_all | solution.py:34
  101.1 3.9 %all-to-all-start.4 = ((bf16[8,64,672]{2,1,0:T(8,128)(2,1)}), bf16[8,64,672]{2,1,0:T(8,128)(2,1)S(1)}, u32[]{:S(2)}, u32[]{:S(2)}) async-start(bf16[8,64,672]{2,1,0:T(8,128)(2,1)} %broadcast_in_dim.8), calls=%async_computation.4 | async-start | bytes 1572864 | tf_op jit(solution)/shard_map/all_to_all | solution.py:34
  105.1 4.0 %collective-permute-start.2 = (f32[64,512]{1,0:T(8,128)S(1)}, f32[64,512]{1,0:T(8,128)S(1)}, u32[]{:S(2)}, u32[]{:S(2)}) collective-permute-start(f32[64,512]{1,0:T(8,128)S(1)} %get-tuple-element.3), channel_id=1, source_target_pairs={{0,1},{1,0},{2,3},{3,2},{4,5},{5,4},{6,7},{7,6},{8,9},{9,8},{10,11... | collective-permute-start | bytes 393224 | tf_op jit(solution)/shard_map/ppermute | solution.py:30
  109.0 4.4 %all-to-all-done.4 = bf16[8,64,672]{2,1,0:T(8,128)(2,1)S(1)} async-done(((bf16[8,64,672]{2,1,0:T(8,128)(2,1)}), bf16[8,64,672]{2,1,0:T(8,128)(2,1)S(1)}, u32[]{:S(2)}, u32[]{:S(2)}) %all-to-all-start.4) | async-done | bytes 688160 | tf_op jit(solution)/shard_map/all_to_all | solution.py:34
  113.4 1.1 copy.25
  114.5 4.9 %collective-permute-start.3 = (bf16[512,672]{0,1:T(8,128)(2,1)}, bf16[512,672]{0,1:T(8,128)(2,1)}, u32[]{:S(2)}, u32[]{:S(2)}) collective-permute-start(bf16[512,672]{0,1:T(8,128)(2,1)} %copy.25), channel_id=1, source_target_pairs={{0,1},{1,0},{2,3},{3,2},{4,5},{5,4},{6,7},{7,6},{8,9},{9,8},{10,11... | collective-permute-start | bytes 2064392 | tf_op jit(solution)/shard_map/ppermute | solution.py:30
  120.3 2.2 %slice.74 = bf16[960,512]{0,1:T(8,128)(2,1)S(1)} slice(f32[1024,512]{0,1:T(8,128)} %copy-done.4), slice={[64:1024], [0:512]} | slice | bytes 1966080 | tf_op jit(solution)/shard_map/slice | solution.py:93
  123.8 1.2 fusion.6
  125.0 1.4 %fusion.8 = f32[1024,512]{1,0:T(8,128)S(1)} fusion(bf16[960,512]{0,1:T(8,128)(2,1)S(1)} %slice.74, bf16[64,512]{0,1:T(8,128)(2,1)S(1)} %fusion.6, bf16[512,672]{1,0:T(8,128)(2,1)S(1)} %bitcast.34), kind=kOutput, calls=%fused_computation.20 | convolution fusion | flops 538968064 | bytes 3801088 | tf_op jit(solution)/shard_map/dot_general | solution.py:94
  126.5 1.3 fusion.7
  127.8 3.8 %multiply_subtract_fusion = f32[1024,512]{1,0:T(8,128)} fusion(f32[1024,512]{1,0:T(8,128)S(1)} %copy-done.1, f32[1024,512]{1,0:T(8,128)S(1)} %fusion.8, bf16[960,512]{0,1:T(8,128)(2,1)S(1)} %slice.73, bf16[64,512]{0,1:T(8,128)(2,1)S(1)} %fusion.7, f32[]{:T(128)} %bitcast.30, bf16[512,672]{0,1:T(8,128)(2,1)} %collective-permute-done.3), kind=kOutput, calls=%fused_computation.11 | convolution fusion | flops 540540928 | bytes 7864832 | tf_op jit(solution)/shard_map/dot_general | solution.py:94
  (40 shorter events, 5.9 us)
Async XLA Ops:
  0.6 0.9 copy-start
  1.6 19.8 %copy-start.5 = (bf16[1024,768]{1,0:T(8,128)(2,1)S(1)}, bf16[1024,768]{1,0:T(8,128)(2,1)}, u32[]{:S(2)}) copy-start(bf16[1024,768]{1,0:T(8,128)(2,1)} %param.9) | copy-start | bytes 4718596
  19.0 4.3 %collective-permute-start = (bf16[512,768]{1,0:T(8,128)(2,1)S(1)}, bf16[512,768]{1,0:T(8,128)(2,1)S(1)}, u32[]{:S(2)}, u32[]{:S(2)}) collective-permute-start(bf16[512,768]{1,0:T(8,128)(2,1)S(1)} %bitcast.35), channel_id=1, source_target_pairs={{0,1},{1,0},{2,3},{3,2},{4,5},{5,4},{6,7},{7,6},{8,9},{9,8},{10,11... | collective-permute-start | bytes 2359304 | tf_op jit(solution)/shard_map/ppermute | solution.py:30
  23.5 1.6 %copy-start.1 = (f32[1024,512]{1,0:T(8,128)S(1)}, f32[1024,512]{1,0:T(8,128)}, u32[]{:S(2)}) copy-start(f32[1024,512]{1,0:T(8,128)} %param.10) | copy-start | bytes 6291460
  25.1 1.9 %copy-start.2 = (f32[1024,512]{0,1:T(8,128)}, f32[1024,512]{0,1:T(8,128)S(1)}, u32[]{:S(2)}) copy-start(f32[1024,512]{0,1:T(8,128)S(1)} %fusion.2) | copy-start | bytes 6291460
  25.1 1.9 %copy-start.6 = (f32[64,160]{1,0:T(8,128)S(1)}, f32[64,160]{1,0:T(8,128)}, u32[]{:S(2)}) copy-start(f32[64,160]{1,0:T(8,128)} %param.11) | copy-start | bytes 122884
  28.6 5.4 %collective-permute-start.1 = (f32[512,672]{0,1:T(8,128)}, f32[512,672]{0,1:T(8,128)}, u32[]{:S(2)}, u32[]{:S(2)}) collective-permute-start(f32[512,672]{0,1:T(8,128)} %pad_maximum_fusion), channel_id=1, source_target_pairs={{0,1},{1,0},{2,3},{3,2},{4,5},{5,4},{6,7},{7,6},{8,9},{9,8},{10,11... | collective-permute-start | bytes 4128776 | tf_op jit(solution)/shard_map/ppermute | solution.py:30
  31.8 2.2 %copy-start.4 = (f32[1024,512]{0,1:T(8,128)}, f32[1024,512]{0,1:T(8,128)S(1)}, u32[]{:S(2)}) copy-start(f32[1024,512]{0,1:T(8,128)S(1)} %fusion.5) | copy-start | bytes 6291460
  64.3 35.8 %copy-start.7 = (f32[128,512]{1,0:T(8,128)S(1)}, f32[128,512]{1,0:T(8,128)}, u32[]{:S(2)}) copy-start(f32[128,512]{1,0:T(8,128)} %param.8) | copy-start | bytes 786436
  101.1 12.3 %all-to-all-start.4 = ((bf16[8,64,672]{2,1,0:T(8,128)(2,1)}), bf16[8,64,672]{2,1,0:T(8,128)(2,1)S(1)}, u32[]{:S(2)}, u32[]{:S(2)}) async-start(bf16[8,64,672]{2,1,0:T(8,128)(2,1)} %broadcast_in_dim.8), calls=%async_computation.4 | async-start | bytes 1572864 | tf_op jit(solution)/shard_map/all_to_all | solution.py:34
  105.1 18.0 %collective-permute-start.2 = (f32[64,512]{1,0:T(8,128)S(1)}, f32[64,512]{1,0:T(8,128)S(1)}, u32[]{:S(2)}, u32[]{:S(2)}) collective-permute-start(f32[64,512]{1,0:T(8,128)S(1)} %get-tuple-element.3), channel_id=1, source_target_pairs={{0,1},{1,0},{2,3},{3,2},{4,5},{5,4},{6,7},{7,6},{8,9},{9,8},{10,11... | collective-permute-start | bytes 393224 | tf_op jit(solution)/shard_map/ppermute | solution.py:30
  114.5 12.0 %collective-permute-start.3 = (bf16[512,672]{0,1:T(8,128)(2,1)}, bf16[512,672]{0,1:T(8,128)(2,1)}, u32[]{:S(2)}, u32[]{:S(2)}) collective-permute-start(bf16[512,672]{0,1:T(8,128)(2,1)} %copy.25), channel_id=1, source_target_pairs={{0,1},{1,0},{2,3},{3,2},{4,5},{5,4},{6,7},{7,6},{8,9},{9,8},{10,11... | collective-permute-start | bytes 2064392 | tf_op jit(solution)/shard_map/ppermute | solution.py:30
  119.4 3.0 %copy-start.3 = (f32[1024,512]{0,1:T(8,128)S(1)}, f32[1024,512]{0,1:T(8,128)}, u32[]{:S(2)}) copy-start(f32[1024,512]{0,1:T(8,128)} %copy-done.2) | copy-start | bytes 6291460
  120.3 3.6 %copy-start.8 = (f32[160]{0:T(256)S(1)}, f32[160]{0:T(256)}, u32[]{:S(2)}) copy-start(f32[160]{0:T(256)} %param.12) | copy-start | bytes 1924

commit v2 on v1

v2 whole, which is shorter than its diff:
```python
import math

import jax
import jax.numpy as jnp
from jax import lax
from jax.experimental import pallas as pl
from jax.experimental.pallas import tpu as pltpu
from jax.sharding import Mesh, PartitionSpec as P

AXES = ("xl", "y", "z", "xh", "c")
BLK = ("xl", "y")
RING = ("z", "xh")
ALL = P(AXES, None)
F32 = jnp.float32
BF16 = jnp.bfloat16
F16 = jnp.float16
NT = (((1,), (1,)), ((), ()))
NN = (((1,), (0,)), ((), ()))

HALF = 64
BLOCKS = 8
LANES = 128
VALUE = 4 * HALF
MAIN = VALUE + HALF
PACKED = MAIN + 16
CODED = PACKED + 16
RING_ROWS = 24
WHOLE = 16 * RING_ROWS
VMEM = 48 * 1024 * 1024


def params():
    return pltpu.CompilerParams(vmem_limit_bytes=VMEM)


def split(value):
    high = value.astype(BF16)
    return high, (value - high.astype(F32)).astype(BF16)


def dot3(a, b, dims):
    a_hi, a_lo = split(a)
    b_hi, b_lo = split(b)

    def one(x, y):
        return lax.dot_general(x, y, dims, preferred_element_type=F32)

    return one(a_hi, b_hi) + one(a_hi, b_lo) + one(a_lo, b_hi)


def lane_group(shape):
    return lax.broadcasted_iota(jnp.int32, shape, len(shape) - 1) // 32


def scale_of(features):
    return 4.0 / features * math.log2(math.e)


def terms_kernel(rows_ref, cen_ref, cs_ref, w_ref, e_ref, out_ref, acc, rs):
    i = pl.program_id(0)
    rows = rows_ref[...]
    scale = scale_of(rows.shape[1])

    @pl.when(i == 0)
    def _():
        wide = rows.astype(F32)
        rs[...] = jnp.sum(wide * wide, axis=1, keepdims=True) * scale
        acc[...] = jnp.zeros_like(acc)

    cross = lax.dot_general(rows, cen_ref[...], NT, preferred_element_type=F32)
    kern = jnp.exp2(cross * (2.0 * scale) - rs[...] - cs_ref[...])
    acc[...] += dot3(kern, w_ref[...], NN)

    @pl.when(i == 0)
    def _():
        coef = dot3(kern[:, :HALF], e_ref[...], NN)
        group = lane_group((16, LANES))
        for b in range(BLOCKS):
            block = coef[b * HALF : (b + 1) * HALF]
            out_ref[b, VALUE:MAIN, :] = block[:, :LANES]
            tail = block[:, LANES:]
            out_ref[b, MAIN:PACKED, :] = jnp.where(
                group < 2,
                jnp.where(group == 0, tail[0:16], tail[16:32]),
                jnp.where(group == 2, tail[32:48], tail[48:64]),
            )

    @pl.when(i == pl.num_programs(0) - 1)
    def _():
        for b in range(BLOCKS):
            for j in range(4):
                out_ref[b, j * HALF : (j + 1) * HALF, :] = acc[
                    b * HALF : (b + 1) * HALF, j * LANES : (j + 1) * LANES
                ]


def terms(rows, centers, cs, weights, eig):
    n, d = rows.shape
    count, c_dim = weights.shape
    tile = 256
    return pl.pallas_call(
        terms_kernel,
        grid=(count // tile,),
        in_specs=[
            pl.BlockSpec((n, d), lambda i: (0, 0)),
            pl.BlockSpec((tile, d), lambda i: (i, 0)),
            pl.BlockSpec((1, tile), lambda i: (0, i)),
            pl.BlockSpec((tile, c_dim), lambda i: (i, 0)),
            pl.BlockSpec(eig.shape, lambda i: (0, 0)),
        ],
        out_specs=pl.BlockSpec((BLOCKS, PACKED, LANES), lambda i: (0, 0, 0)),
        out_shape=jax.ShapeDtypeStruct((BLOCKS, PACKED, LANES), F32),
        scratch_shapes=[pltpu.VMEM((n, c_dim), F32), pltpu.VMEM((n, 1), F32)],
        compiler_params=params(),
        cost_estimate=pl.CostEstimate(
            flops=2 * n * count * (d + 3 * c_dim), bytes_accessed=6 << 20, transcendentals=n * count
        ),
        name="terms",
    )(rows, centers, cs, weights, eig)


def code_kernel(a_ref, b_ref, out_ref):
    for b in range(a_ref.shape[0]):
        total = a_ref[b] + b_ref[b]
        for lo, hi, at in ((0, VALUE, PACKED), (VALUE, PACKED, PACKED + 8)):
            part = total[lo:hi]
            top = jnp.max(jnp.abs(part), axis=(0, 1), keepdims=True)
            power = jnp.ceil(jnp.log2(jnp.maximum(top, 1e-30)))
            out_ref[b, lo:hi, :] = part * jnp.exp2(14.0 - power)
            out_ref[b, at : at + 8, :] = jnp.broadcast_to(power, (8, LANES))


def code(a, b):
    step = 4
    spec = pl.BlockSpec((step, PACKED, LANES), lambda i: (i, 0, 0))
    return pl.pallas_call(
        code_kernel,
        grid=(BLOCKS // step,),
        in_specs=[spec, spec],
        out_specs=pl.BlockSpec((step, CODED, LANES), lambda i: (i, 0, 0)),
        out_shape=jax.ShapeDtypeStruct((BLOCKS, CODED, LANES), F32),
        compiler_params=params(),
        name="code",
    )(a, b)


def decode_kernel(x_ref, out_ref):
    for lo, hi, at in ((0, VALUE, PACKED), (VALUE, PACKED, PACKED + 8)):
        total = jnp.zeros((hi - lo, LANES), F32)
        for b in range(BLOCKS):
            total += x_ref[b, lo:hi, :] * jnp.exp2(x_ref[b, at : at + 1, :] - 14.0)
        out_ref[lo:hi, :] = total
    out_ref[PACKED:WHOLE, :] = jnp.zeros((WHOLE - PACKED, LANES), F32)


def decode(x):
    return pl.pallas_call(
        decode_kernel,
        out_shape=jax.ShapeDtypeStruct((WHOLE, LANES), F32),
        compiler_params=params(),
        name="decode",
    )(x)


def pack_kernel(whole_ref, targets_ref, pred_ref, out_ref):
    for j in range(4):
        lanes = slice(j * LANES, (j + 1) * LANES)
        value = whole_ref[j * HALF : (j + 1) * HALF, :]
        pred_ref[:, lanes] = value
        resid = (value - targets_ref[:, lanes]).astype(BF16)
        for b in range(BLOCKS):
            out_ref[b, j * HALF : (j + 1) * HALF, :] = resid
    coef = whole_ref[VALUE:PACKED, :].astype(BF16)
    for b in range(BLOCKS):
        out_ref[b, VALUE:PACKED, :] = coef


def pack(whole, targets):
    return pl.pallas_call(
        pack_kernel,
        out_shape=(
            jax.ShapeDtypeStruct(targets.shape, F32),
            jax.ShapeDtypeStruct((BLOCKS, PACKED, LANES), BF16),
        ),
        compiler_params=params(),
        name="pack",
    )(whole, targets)


def kern_kernel(cen_ref, first_ref, second_ref, rs_ref, out_ref):
    cen = cen_ref[...]
    scale = scale_of(cen.shape[1])
    wide = cen.astype(F32)
    cs = jnp.sum(wide * wide, axis=1, keepdims=True) * scale
    n = first_ref.shape[0]
    for k, rows_ref in enumerate((first_ref, second_ref)):
        cols = slice(k * n, (k + 1) * n)
        cross = lax.dot_general(cen, rows_ref[...], NT, preferred_element_type=F32)
        out_ref[:, cols] = jnp.exp2(cross * (2.0 * scale) - cs - rs_ref[:, cols]).astype(BF16)


def kern_rows(centers, first, second, rs):
    count, d = centers.shape
    n = first.shape[0]
    tile = 256
    return pl.pallas_call(
        kern_kernel,
        grid=(count // tile,),
        in_specs=[
            pl.BlockSpec((tile, d), lambda i: (i, 0)),
            pl.BlockSpec((n, d), lambda i: (0, 0)),
            pl.BlockSpec((n, d), lambda i: (0, 0)),
            pl.BlockSpec((1, 2 * n), lambda i: (0, 0)),
        ],
        out_specs=pl.BlockSpec((tile, 2 * n), lambda i: (i, 0)),
        out_shape=jax.ShapeDtypeStruct((count, 2 * n), BF16),
        compiler_params=params(),
        cost_estimate=pl.CostEstimate(
            flops=4 * n * count * d, bytes_accessed=5 << 20, transcendentals=2 * n * count
        ),
        name="kern",
    )(centers, first, second, rs)


def step_kernel(step_ref, kern_ref, first_ref, second_ref, eig_ref, w_ref, out_ref, resid, coef):
    i = pl.program_id(0)

    @pl.when(i == 0)
    def _():
        group = lane_group((16, LANES))
        for k, got_ref in enumerate((first_ref, second_ref)):
            for b in range(BLOCKS):
                at = (k * BLOCKS + b) * HALF
                for j in range(4):
                    resid[at : at + HALF, j * LANES : (j + 1) * LANES] = got_ref[
                        b, j * HALF : (j + 1) * HALF, :
                    ]
                coef[at : at + HALF, :LANES] = got_ref[b, VALUE:MAIN, :]
                tail = got_ref[b, MAIN:PACKED, :]
                for t in range(4):
                    coef[at + 16 * t : at + 16 * (t + 1), LANES:] = jnp.where(
                        group == t, tail, jnp.zeros_like(tail)
                    )

    def update(kern):
        grad = lax.dot_general(kern, resid[...], NN, preferred_element_type=F32)
        out_ref[...] = w_ref[...] - step_ref[0] * grad

    @pl.when(i == 0)
    def _():
        e_hi, e_lo = split(eig_ref[...])
        both = coef[...]
        corr = lax.dot_general(e_hi, both, NT, preferred_element_type=F32)
        corr += lax.dot_general(e_lo, both, NT, preferred_element_type=F32)
        kern = kern_ref[...]
        sub = (kern[:HALF].astype(F32) - corr).astype(BF16)
        update(jnp.concatenate([sub, kern[HALF:]], axis=0))

    @pl.when(i > 0)
    def _():
        update(kern_ref[...])


def take_step(step, kern, first, second, eig, weights):
    count, c_dim = weights.shape
    tile = 256
    whole3 = pl.BlockSpec((BLOCKS, PACKED, LANES), lambda i: (0, 0, 0))
    return pl.pallas_call(
        step_kernel,
        grid=(count // tile,),
        in_specs=[
            pl.BlockSpec(memory_space=pltpu.SMEM),
            pl.BlockSpec((tile, kern.shape[1]), lambda i: (i, 0)),
            whole3,
            whole3,
            pl.BlockSpec(eig.shape, lambda i: (0, 0)),
            pl.BlockSpec((tile, c_dim), lambda i: (i, 0)),
        ],
        out_specs=pl.BlockSpec((tile, c_dim), lambda i: (i, 0)),
        out_shape=jax.ShapeDtypeStruct(weights.shape, F32),
        scratch_shapes=[
            pltpu.VMEM((2 * BLOCKS * HALF, c_dim), BF16),
            pltpu.VMEM((2 * BLOCKS * HALF, 2 * LANES), BF16),
        ],
        compiler_params=params(),
        cost_estimate=pl.CostEstimate(
            flops=2 * count * kern.shape[1] * c_dim, bytes_accessed=8 << 20, transcendentals=0
        ),
        name="take_step",
    )(step, kern, first, second, eig, weights)


def sq_norm(rows):
    return jnp.sum(rows.astype(F32) ** 2, axis=1) * scale_of(rows.shape[1])


def swap_cores(value):
    return lax.ppermute(value, "c", [(0, 1), (1, 0)])


def spread(value, axes, size):
    return lax.all_to_all(
        jnp.broadcast_to(value[None], (size,) + value.shape), axes, 0, 0, tiled=True
    )


def wide_eig(eig):
    return jnp.concatenate([eig[:, :LANES]] + [eig[:, LANES:]] * 4, axis=1)


def local(batch, targets, centers, weights, eigvec, eig_scale, step):
    core = lax.axis_index("c")
    d = batch.shape[1]
    cs = sq_norm(centers)[None, :]
    eig = wide_eig(eigvec)
    eig_scaled = wide_eig(eigvec * eig_scale[None, :])

    first = spread(lax.dynamic_slice_in_dim(batch, (1 - core) * HALF, HALF, 0), BLK, BLOCKS)
    first = first.reshape(BLOCKS * HALF, d)
    second = swap_cores(first)
    sent = swap_cores(terms(first, centers, cs, weights, eig))
    coded = code(terms(second, centers, cs, weights, eig), sent)
    coded, first, second = lax.optimization_barrier((coded, first, second))
    got = lax.all_to_all(coded.astype(F16), BLK, 0, 0, tiled=True)

    rs = jnp.concatenate([sq_norm(first), sq_norm(second)])[None, :]
    kern = kern_rows(centers, first, second, rs)

    summed = decode(got.astype(F32)).reshape(16, RING_ROWS, LANES)
    pieces = lax.all_to_all(summed, RING, 0, 0, tiled=True).sum(0)
    whole = spread(pieces, RING, 16).reshape(WHOLE, LANES)

    own_targets = lax.dynamic_slice_in_dim(targets, core * HALF, HALF, 0)
    own_pred, packed = pack(whole, own_targets)
    got_second = lax.all_to_all(packed, BLK, 0, 0, tiled=True)
    got_first = swap_cores(got_second)
    other_pred = swap_cores(own_pred)
    predictions = jnp.where(
        core == 0,
        jnp.concatenate([own_pred, other_pred], axis=0),
        jnp.concatenate([other_pred, own_pred], axis=0),
    )
    new_weights = take_step(step, kern, got_first, got_second, eig_scaled, weights)
    return (predictions, new_weights)


def solution(mesh):
    fine = Mesh(mesh.devices.reshape(2, 4, 8, 2, 2), AXES)
    return jax.shard_map(
        local,
        mesh=fine,
        in_specs=(P(BLK, None), P(BLK, None), ALL, ALL, ALL, P(), P()),
        out_specs=(P(BLK, None), ALL),
        check_vma=False,
    )
```

time: 132 us -> 116 us (0.88)
  blocking collectives: 76 us -> 35.1 us
  waiting for transfers between devices: 5.9 us -> 29.3 us
  Pallas kernels: 0 us -> 18.5 us
  matrix products: 15.7 us -> 0 us
  starting transfers between devices: 15.6 us -> 20.7 us
  local copies, waits for them, and re-layouts: 9.5 us -> 6.02 us
  other arithmetic: 7.12 us -> 4.45 us
    all_to_all x4 -> x2, blocking collectives: 76 us -> 35.1 us  [the longest x1 20.8 us: local(): pieces = lax.all_to_all(summed, RING, 0, 0, tiled=True).sum(0)]
    pallas_call x0 -> x7, Pallas kernels: none -> 18.5 us  [the longest x2 11.8 us: terms(): pl.pallas_call(terms_kernel, grid=(count // tile,), in_specs=[pl.BlockSpe...]
    all_to_all x1 -> x2, waiting for transfers between devices: 4.36 us -> 20.1 us  [spread(): lax.all_to_all(jnp.broadcast_to(value[None], (size,) + value.shape), axes...]
    dot_general x10 -> x0, matrix products: 15.7 us -> none  [the longest x2 5.17 us: gradient(): jnp.dot(kern.astype(jnp.bfloat16), resid, preferred_element_type=jnp.floa...]
    all_to_all x1 -> x2, starting transfers between devices: 3.92 us -> 9.6 us  [spread(): lax.all_to_all(jnp.broadcast_to(value[None], (size,) + value.shape), axes...]
    all_to_all x0 -> x1, waiting for transfers between devices: none -> 5.41 us  [local(): got_second = lax.all_to_all(packed, BLK, 0, 0, tiled=True)]
    ppermute x4, starting transfers between devices: 11.7 us -> 7.47 us  [swap_cores(): return lax.ppermute(value, 'c', [(0, 1), (1, 0)])]
    all_to_all x0 -> x1, starting transfers between devices: none -> 3.67 us  [local(): got_second = lax.all_to_all(packed, BLK, 0, 0, tiled=True)]
  transfers between devices with their start and end apart: 5 -> 7, of which waited for: 2 -> 4; matrix products, arithmetic and copies ran while one was open for 10% -> 4% of each run, Pallas kernels for 0% -> 7%
where the time goes in v2:
time: 116 us
  blocking collectives  35.1 us (30%)
  waiting for transfers between devices  29.3 us (25%)
  starting transfers between devices  20.7 us (18%)
  Pallas kernels  18.5 us (16%)
  local copies, waits for them, and re-layouts  6.02 us (5%)
  other arithmetic  4.45 us (4%)
  between operations  1.54 us (1%)
    all_to_all x1, blocking collectives, local(): pieces = lax.all_to_all(summed, RING, 0, 0, tiled=True).sum(0)  20.8 us
    all_to_all x2, waiting for transfers between devices, spread(): lax.all_to_all(jnp.broadcast_to(value[None], (size,) + value.shape), axes...  20.1 us
    all_to_all x1, blocking collectives, local(): got = lax.all_to_all(coded.astype(F16), BLK, 0, 0, tiled=True)  14.3 us
    pallas_call x2, Pallas kernels, terms(): pl.pallas_call(terms_kernel, grid=(count // tile,), in_specs=[pl.BlockSpe...  11.8 us
    all_to_all x2, starting transfers between devices, spread(): lax.all_to_all(jnp.broadcast_to(value[None], (size,) + value.shape), axes...  9.6 us
    ppermute x4, starting transfers between devices, swap_cores(): return lax.ppermute(value, 'c', [(0, 1), (1, 0)])  7.47 us
    all_to_all x1, waiting for transfers between devices, local(): got_second = lax.all_to_all(packed, BLK, 0, 0, tiled=True)  5.41 us
    ppermute x4, waiting for transfers between devices, swap_cores(): return lax.ppermute(value, 'c', [(0, 1), (1, 0)])  3.79 us
  transfers between devices with their start and end apart: 7, of which 4 were waited for; matrix products, arithmetic and copies ran while one was open for 4% of the time, Pallas kernels for 7%

profile of v2, /device:TPU:1, one launch (start us, length us, event | category | flops | bytes accessed | tf_op | source)
XLA Modules:
  0.0 115.6 jit_solution(10514337117342416021)
XLA Ops:
  0.7 0.9 constant_dynamic-slice_fusion.1
  1.6 0.9 broadcast_in_dim.6
  2.6 6.1 %all-to-all-start = ((bf16[8,64,768]{2,1,0:T(8,128)(2,1)}), bf16[8,64,768]{2,1,0:T(8,128)(2,1)S(1)}, u32[]{:S(2)}, u32[]{:S(2)}) async-start(bf16[8,64,768]{2,1,0:T(8,128)(2,1)} %broadcast_in_dim.6), calls=%async_computation | async-start | bytes 1572864 | tf_op jit(solution)/shard_map/all_to_all | solution.py:302
  8.7 1.8 %multiply_reduce_fusion = f32[1024]{0:T(1024)S(1)} fusion(bf16[1024,768]{1,0:T(8,128)(2,1)} %cen_ref.5), kind=kLoop, calls=%fused_computation | loop fusion | flops 2358272 | bytes 1576960 | tf_op jit(solution)/shard_map/reduce_sum | solution.py:294
  10.5 9.5 %all-to-all-done = bf16[8,64,768]{2,1,0:T(8,128)(2,1)S(1)} async-done(((bf16[8,64,768]{2,1,0:T(8,128)(2,1)}), bf16[8,64,768]{2,1,0:T(8,128)(2,1)S(1)}, u32[]{:S(2)}, u32[]{:S(2)}) %all-to-all-start) | async-done | bytes 786464 | tf_op jit(solution)/shard_map/all_to_all | solution.py:302
  20.0 1.4 %copy-done.3 = bf16[1024,768]{1,0:T(8,128)(2,1)S(1)} copy-done((bf16[1024,768]{1,0:T(8,128)(2,1)S(1)}, bf16[1024,768]{1,0:T(8,128)(2,1)}, u32[]{:S(2)}) %copy-start.3) | copy-done | bytes 1572888
  21.4 5.9 %terms.3 = f32[8,336,128]{2,1,0:T(8,128)S(1)} custom-call(bf16[512,768]{1,0:T(8,128)(2,1)S(1)} %bitcast.5, bf16[1024,768]{1,0:T(8,128)(2,1)S(1)} %copy-done.3, f32[1,1024]{1,0:T(1,128)S(1)} %bitcast.11, f32[1024,512]{1,0:T(8,128)S(1)} %copy-done.1, f32[64,256]{1,0:T(8,128)S(1)} %pad_maximum_fusion.e_ref), custom_call_target="tpu_custom_call" | custom-call | flops 2415919104 | bytes 6291456 | tf_op jit(solution)/shard_map/terms/pallas_call | solution.py:101
  27.4 1.7 %collective-permute-start.1 = (f32[8,336,128]{2,1,0:T(8,128)S(1)}, f32[8,336,128]{2,1,0:T(8,128)S(1)}, u32[]{:S(2)}, u32[]{:S(2)}) collective-permute-start(f32[8,336,128]{2,1,0:T(8,128)S(1)} %terms.3), channel_id=1, source_target_pairs={{0,1},{1,0},{2,3},{3,2},{4,5},{5,4},{6,7},{7,6},{8,9},{9,8},{10,11... | collective-permute-start | bytes 4128776 | tf_op jit(solution)/shard_map/ppermute | solution.py:298
  29.1 3.8 %collective-permute-done.rows_ref.second_ref = bf16[512,768]{1,0:T(8,128)(2,1)S(1)} collective-permute-done((bf16[512,768]{1,0:T(8,128)(2,1)S(1)}, bf16[512,768]{1,0:T(8,128)(2,1)S(1)}, u32[]{:S(2)}, u32[]{:S(2)}) %collective-permute-start) | collective-permute-done | bytes 786464 | tf_op jit(solution)/shard_map/ppermute | solution.py:298
  32.9 5.9 %terms.2.a_ref = f32[8,336,128]{2,1,0:T(8,128)S(1)} custom-call(bf16[512,768]{1,0:T(8,128)(2,1)S(1)} %collective-permute-done.rows_ref.second_ref, bf16[1024,768]{1,0:T(8,128)(2,1)S(1)} %copy-done.3, f32[1,1024]{1,0:T(1,128)S(1)} %bitcast.12, f32[1024,512]{1,0:T(8,128)S(1)} %copy-done.1, f32[64,256]{1,0:T(8,128)S(1)} %pad_maximum_fusion.e_ref), custom_call_target="tpu_custom_call" | custom-call | flops 2415919104 | bytes 6291456 | tf_op jit(solution)/shard_map/terms/pallas_call | solution.py:101
  39.5 14.3 %all_to_all.25 = f16[8,352,128]{2,1,0:T(8,128)(2,1)S(1)} all-to-all(f16[8,352,128]{2,1,0:T(8,128)(2,1)S(1)} %convert_element_type.16), channel_id=1, replica_groups=mesh['xl'=2,'y'=4,'z'=8,'xh'=2,'c'=2] {'xl','y'}, dimensions={0} | all-to-all | bytes 1441792 | tf_op jit(solution)/shard_map/all_to_all | solution.py:324
  54.0 20.8 %all_to_all.26 = f32[16,24,128]{2,1,0:T(8,128)S(1)} all-to-all(f32[16,24,128]{2,1,0:T(8,128)S(1)} %bitcast.9), channel_id=1, replica_groups=mesh['xl'=2,'y'=4,'z'=8,'xh'=2,'c'=2] {'z','xh'}, dimensions={0} | all-to-all | bytes 393216 | tf_op jit(solution)/shard_map/all_to_all | solution.py:330
  74.8 0.7 broadcast_in_dim.7
  75.5 3.5 %all-to-all-start.3 = ((f32[16,24,128]{2,1,0:T(8,128)}), f32[16,24,128]{2,1,0:T(8,128)S(1)}, u32[]{:S(2)}, u32[]{:S(2)}) async-start(f32[16,24,128]{2,1,0:T(8,128)} %broadcast_in_dim.7), calls=%async_computation.3 | async-start | bytes 393216 | tf_op jit(solution)/shard_map/all_to_all | solution.py:302
  79.1 10.6 %all-to-all-done.3 = f32[16,24,128]{2,1,0:T(8,128)S(1)} async-done(((f32[16,24,128]{2,1,0:T(8,128)}), f32[16,24,128]{2,1,0:T(8,128)S(1)}, u32[]{:S(2)}, u32[]{:S(2)}) %all-to-all-start.3) | async-done | bytes 196640 | tf_op jit(solution)/shard_map/all_to_all | solution.py:302
  89.8 0.8 copy-done.7
  90.6 3.7 %all-to-all-start.4 = ((bf16[8,336,128]{2,1,0:T(8,128)(2,1)}), bf16[8,336,128]{2,1,0:T(8,128)(2,1)S(1)}, u32[]{:S(2)}, u32[]{:S(2)}) async-start(bf16[8,336,128]{2,1,0:T(8,128)(2,1)} %copy-done.7), calls=%async_computation.4 | async-start | bytes 1376256 | tf_op jit(solution)/shard_map/all_to_all | solution.py:335
  95.1 1.5 %multiply_reduce_fusion.1 = (f32[512]{0:T(512)S(1)}, f32[512]{0:T(512)S(1)}) fusion(bf16[512,768]{1,0:T(8,128)(2,1)} %copy-done.5, bf16[512,768]{1,0:T(8,128)(2,1)S(1)} %bitcast.7), kind=kLoop, calls=%fused_computation.1 | loop fusion | flops 2358272 | bytes 1576960 | tf_op jit(solution)/shard_map/reduce_sum | solution.py:294
  96.6 5.4 %all-to-all-done.4.second_ref = bf16[8,336,128]{2,1,0:T(8,128)(2,1)S(1)} async-done(((bf16[8,336,128]{2,1,0:T(8,128)(2,1)}), bf16[8,336,128]{2,1,0:T(8,128)(2,1)S(1)}, u32[]{:S(2)}, u32[]{:S(2)}) %all-to-all-start.4) | async-done | bytes 688160 | tf_op jit(solution)/shard_map/all_to_all | solution.py:335
  102.0 5.6 %collective-permute-start.3 = (bf16[8,336,128]{2,1,0:T(8,128)(2,1)S(1)}, bf16[8,336,128]{2,1,0:T(8,128)(2,1)S(1)}, u32[]{:S(2)}, u32[]{:S(2)}) collective-permute-start(bf16[8,336,128]{2,1,0:T(8,128)(2,1)S(1)} %all-to-all-done.4.second_ref), channel_id=1, source_target_pairs={{0,1},{1,0},{2,3},{3,2},{4,5},{5,4},{6,7},{7,6},{8,9},{9,8},{10,11... | collective-permute-start | bytes 2064392 | tf_op jit(solution)/shard_map/ppermute | solution.py:298
  107.8 1.1 copy-done.6
  108.9 2.7 %kern.1.kern_ref = bf16[1024,1024]{1,0:T(8,128)(2,1)S(1)} custom-call(bf16[1024,768]{1,0:T(8,128)(2,1)S(1)} %copy-done.4, bf16[512,768]{1,0:T(8,128)(2,1)S(1)} %bitcast.8, bf16[512,768]{1,0:T(8,128)(2,1)S(1)} %copy-done.6, f32[1,1024]{1,0:T(1,128)S(1)} %bitcast.13), custom_call_target="tpu_custom_call" | custom-call | flops 1610612736 | bytes 5242880 | tf_op jit(solution)/shard_map/kern/pallas_call | solution.py:206
  111.6 0.7 maximum_select_fusion
  112.4 3.3 %take_step.1 = f32[1024,512]{1,0:T(8,128)} custom-call(f32[1]{0:T(128)S(6)} %copy.9.step_ref, bf16[1024,1024]{1,0:T(8,128)(2,1)S(1)} %kern.1.kern_ref, bf16[8,336,128]{2,1,0:T(8,128)(2,1)S(1)} %collective-permute-done.3.first_ref, bf16[8,336,128]{2,1,0:T(8,128)(2,1)S(1)} %all-to-all-done.4.second_ref, f32[64,256]{1,0:T(8,128)S(1)} %pad_maximum_fusion.1.eig_ref, ...), custom_call_target="tpu_custom_call" | custom-call | flops 1073741824 | bytes 8388608 | tf_op jit(solution)/shard_map/take_step/pallas_call | solution.py:268
  (39 shorter events, 1.4 us)
Async XLA Ops:
  0.6 78.4 %copy-start = (f32[128,512]{1,0:T(8,128)S(1)}, f32[128,512]{1,0:T(8,128)}, u32[]{:S(2)}) copy-start(f32[128,512]{1,0:T(8,128)} %param.8) | copy-start | bytes 786436
  0.6 8.0 %copy-start.8 = (f32[64,160]{1,0:T(8,128)S(1)}, f32[64,160]{1,0:T(8,128)}, u32[]{:S(2)}) copy-start(f32[64,160]{1,0:T(8,128)} %param.11) | copy-start | bytes 122884
  0.7 8.0 %slice-start = ((f32[64,160]{1,0:T(8,128)}), f32[64,32]{1,0:T(8,128)S(1)}, s32[]{:S(2)}) async-start(f32[64,160]{1,0:T(8,128)} %param.11), calls=%async_computation.5 | async-start | bytes 65536 | tf_op jit(solution)/shard_map/slice | solution.py:308
  2.6 17.5 %copy-start.1 = (f32[1024,512]{1,0:T(8,128)S(1)}, f32[1024,512]{1,0:T(8,128)}, u32[]{:S(2)}) copy-start(f32[1024,512]{1,0:T(8,128)} %w_ref.5) | copy-start | bytes 6291460
  2.6 17.5 %all-to-all-start = ((bf16[8,64,768]{2,1,0:T(8,128)(2,1)}), bf16[8,64,768]{2,1,0:T(8,128)(2,1)S(1)}, u32[]{:S(2)}, u32[]{:S(2)}) async-start(bf16[8,64,768]{2,1,0:T(8,128)(2,1)} %broadcast_in_dim.6), calls=%async_computation | async-start | bytes 1572864 | tf_op jit(solution)/shard_map/all_to_all | solution.py:302
  20.0 1.4 %copy-start.3 = (bf16[1024,768]{1,0:T(8,128)(2,1)S(1)}, bf16[1024,768]{1,0:T(8,128)(2,1)}, u32[]{:S(2)}) copy-start(bf16[1024,768]{1,0:T(8,128)(2,1)} %cen_ref.5) | copy-start | bytes 4718596
  27.4 11.5 %collective-permute-start.1 = (f32[8,336,128]{2,1,0:T(8,128)S(1)}, f32[8,336,128]{2,1,0:T(8,128)S(1)}, u32[]{:S(2)}, u32[]{:S(2)}) collective-permute-start(f32[8,336,128]{2,1,0:T(8,128)S(1)} %terms.3), channel_id=1, source_target_pairs={{0,1},{1,0},{2,3},{3,2},{4,5},{5,4},{6,7},{7,6},{8,9},{9,8},{10,11... | collective-permute-start | bytes 4128776 | tf_op jit(solution)/shard_map/ppermute | solution.py:298
  29.0 3.9 %collective-permute-start = (bf16[512,768]{1,0:T(8,128)(2,1)S(1)}, bf16[512,768]{1,0:T(8,128)(2,1)S(1)}, u32[]{:S(2)}, u32[]{:S(2)}) collective-permute-start(bf16[512,768]{1,0:T(8,128)(2,1)S(1)} %bitcast.6), channel_id=1, source_target_pairs={{0,1},{1,0},{2,3},{3,2},{4,5},{5,4},{6,7},{7,6},{8,9},{9,8},{10,11... | collective-permute-start | bytes 2359304 | tf_op jit(solution)/shard_map/ppermute | solution.py:298
  32.9 5.9 %copy-start.5 = (bf16[512,768]{1,0:T(8,128)(2,1)}, bf16[512,768]{1,0:T(8,128)(2,1)S(1)}, u32[]{:S(2)}) copy-start(bf16[512,768]{1,0:T(8,128)(2,1)S(1)} %collective-permute-done.rows_ref.second_ref) | copy-start | bytes 2359300
  54.0 40.3 %copy-start.9 = (f32[160]{0:T(256)S(1)}, f32[160]{0:T(256)}, u32[]{:S(2)}) copy-start(f32[160]{0:T(256)} %param.12) | copy-start | bytes 1924
  75.5 14.2 %all-to-all-start.3 = ((f32[16,24,128]{2,1,0:T(8,128)}), f32[16,24,128]{2,1,0:T(8,128)S(1)}, u32[]{:S(2)}, u32[]{:S(2)}) async-start(f32[16,24,128]{2,1,0:T(8,128)} %broadcast_in_dim.7), calls=%async_computation.3 | async-start | bytes 393216 | tf_op jit(solution)/shard_map/all_to_all | solution.py:302
  89.8 0.9 copy-start.7
  90.6 17.1 %copy-start.4 = (bf16[1024,768]{1,0:T(8,128)(2,1)S(1)}, bf16[1024,768]{1,0:T(8,128)(2,1)}, u32[]{:S(2)}) copy-start(bf16[1024,768]{1,0:T(8,128)(2,1)} %cen_ref.5) | copy-start | bytes 4718596
  90.6 11.4 %all-to-all-start.4 = ((bf16[8,336,128]{2,1,0:T(8,128)(2,1)}), bf16[8,336,128]{2,1,0:T(8,128)(2,1)S(1)}, u32[]{:S(2)}, u32[]{:S(2)}) async-start(bf16[8,336,128]{2,1,0:T(8,128)(2,1)} %copy-done.7), calls=%async_computation.4 | async-start | bytes 1376256 | tf_op jit(solution)/shard_map/all_to_all | solution.py:335
  102.0 10.3 %collective-permute-start.3 = (bf16[8,336,128]{2,1,0:T(8,128)(2,1)S(1)}, bf16[8,336,128]{2,1,0:T(8,128)(2,1)S(1)}, u32[]{:S(2)}, u32[]{:S(2)}) collective-permute-start(bf16[8,336,128]{2,1,0:T(8,128)(2,1)S(1)} %all-to-all-done.4.second_ref), channel_id=1, source_target_pairs={{0,1},{1,0},{2,3},{3,2},{4,5},{5,4},{6,7},{7,6},{8,9},{9,8},{10,11... | collective-permute-start | bytes 2064392 | tf_op jit(solution)/shard_map/ppermute | solution.py:298
  107.7 4.0 %collective-permute-start.2 = (f32[64,512]{1,0:T(8,128)S(1)}, f32[64,512]{1,0:T(8,128)S(1)}, u32[]{:S(2)}, u32[]{:S(2)}) collective-permute-start(f32[64,512]{1,0:T(8,128)S(1)} %get-tuple-element.8), channel_id=1, source_target_pairs={{0,1},{1,0},{2,3},{3,2},{4,5},{5,4},{6,7},{7,6},{8,9},{9,8},{10,11... | collective-permute-start | bytes 393224 | tf_op jit(solution)/shard_map/ppermute | solution.py:298
  107.8 1.1 copy-start.6
  108.9 3.5 %copy-start.2 = (f32[1024,512]{1,0:T(8,128)S(1)}, f32[1024,512]{1,0:T(8,128)}, u32[]{:S(2)}) copy-start(f32[1024,512]{1,0:T(8,128)} %w_ref.5) | copy-start | bytes 6291460

commit v3 on v1

v3 whole, which is shorter than its diff:
```python
import math

import jax
import jax.numpy as jnp
from jax import lax
from jax.experimental import pallas as pl
from jax.experimental.pallas import tpu as pltpu
from jax.sharding import Mesh, PartitionSpec as P

AXES = ("xl", "y", "z", "xh", "c")
BLK = ("xl", "y")
RING = ("z", "xh")
ALL = P(AXES, None)
F32 = jnp.float32
BF16 = jnp.bfloat16
F16 = jnp.float16
NT = (((1,), (1,)), ((), ()))
NN = (((1,), (0,)), ((), ()))
TN = (((0,), (0,)), ((), ()))

HALF = 64
BLOCKS = 8
LANES = 128
VALUE = 4 * HALF
MAIN = VALUE + HALF
PACKED = MAIN + 16
CODED = PACKED + 16
RING_ROWS = 24
WHOLE = 16 * RING_ROWS
def params(mib):
    return pltpu.CompilerParams(vmem_limit_bytes=mib << 20)


def split(value):
    high = value.astype(BF16)
    return high, (value - high.astype(F32)).astype(BF16)


def dot3(a, b, dims):
    a_hi, a_lo = split(a)
    b_hi, b_lo = split(b)

    def one(x, y):
        return lax.dot_general(x, y, dims, preferred_element_type=F32)

    return one(a_hi, b_hi) + one(a_hi, b_lo) + one(a_lo, b_hi)


def widen(eig):
    return jnp.concatenate([eig[:, :LANES]] + [eig[:, LANES:]] * 4, axis=1)


def lane_group(shape):
    return lax.broadcasted_iota(jnp.int32, shape, len(shape) - 1) // 32


def scale_of(features):
    return 4.0 / features * math.log2(math.e)


def fan_kernel(core_ref, rows_ref, out_ref):
    rows = rows_ref[...]
    for b in range(BLOCKS):
        out_ref[b] = rows


def fan(batch, core):
    d = batch.shape[1]
    return pl.pallas_call(
        fan_kernel,
        grid_spec=pltpu.PrefetchScalarGridSpec(
            num_scalar_prefetch=1,
            grid=(1,),
            in_specs=[pl.BlockSpec((HALF, d), lambda i, core: (1 - core[0], 0))],
            out_specs=pl.BlockSpec((BLOCKS, HALF, d), lambda i, core: (0, 0, 0)),
        ),
        out_shape=jax.ShapeDtypeStruct((BLOCKS, HALF, d), batch.dtype),
        compiler_params=params(8),
        name="fan",
    )(core, batch)


def weights_kernel(w_ref, out_ref):
    count = w_ref.shape[0]
    high, low = split(w_ref[...])
    out_ref[:count] = high
    out_ref[count : 2 * count] = low
    out_ref[2 * count :] = high


def split_weights(weights):
    count, c_dim = weights.shape
    return pl.pallas_call(
        weights_kernel,
        out_shape=jax.ShapeDtypeStruct((3 * count, c_dim), BF16),
        compiler_params=params(12),
        cost_estimate=pl.CostEstimate(flops=0, bytes_accessed=5 << 20, transcendentals=0),
        name="split_weights",
    )(weights)


def terms_kernel(rows_ref, cen_ref, cs_ref, w_ref, e_ref, out_ref, kern_ref, kern3):
    n, d = rows_ref.shape
    count = cen_ref.shape[0]
    tile = 512
    scale = scale_of(d)
    rows = rows_ref[...]
    wide = rows.astype(F32)
    rs = jnp.sum(wide * wide, axis=1, keepdims=True) * scale
    for at in range(0, count, tile):
        cols = slice(at, at + tile)
        cross = lax.dot_general(rows, cen_ref[cols, :], NT, preferred_element_type=F32)
        kern = jnp.exp2(cross * (2.0 * scale) - rs - cs_ref[:, cols])
        high, low = split(kern)
        kern3[:, at : at + tile] = high
        kern3[:, count + at : count + at + tile] = high
        kern_ref[:, cols] = high
        kern3[:, 2 * count + at : 2 * count + at + tile] = low
        if at == 0:
            coef = dot3(kern[:, :HALF], widen(e_ref[...]), NN)
            group = lane_group((16, LANES))
            for b in range(BLOCKS):
                block = coef[b * HALF : (b + 1) * HALF]
                out_ref[b, VALUE:MAIN, :] = block[:, :LANES]
                tail = block[:, LANES:]
                out_ref[b, MAIN:PACKED, :] = jnp.where(
                    group < 2,
                    jnp.where(group == 0, tail[0:16], tail[16:32]),
                    jnp.where(group == 2, tail[32:48], tail[48:64]),
                )
    value = lax.dot_general(kern3[...], w_ref[...], NN, preferred_element_type=F32)
    for b in range(BLOCKS):
        for j in range(4):
            out_ref[b, j * HALF : (j + 1) * HALF, :] = value[
                b * HALF : (b + 1) * HALF, j * LANES : (j + 1) * LANES
            ]


def terms(rows, centers, cs, weights3, eig):
    n, d = rows.shape
    count = centers.shape[0]
    c_dim = weights3.shape[1]
    return pl.pallas_call(
        terms_kernel,
        out_shape=(
            jax.ShapeDtypeStruct((BLOCKS, PACKED, LANES), F32),
            jax.ShapeDtypeStruct((n, count), BF16),
        ),
        scratch_shapes=[pltpu.VMEM((n, 3 * count), BF16)],
        compiler_params=params(24),
        cost_estimate=pl.CostEstimate(
            flops=20 * n * count * (d + 3 * c_dim), bytes_accessed=6 << 20, transcendentals=n * count
        ),
        name="terms",
    )(rows, centers, cs, weights3, eig)


def code_kernel(a_ref, b_ref, out_ref):
    for b in range(a_ref.shape[0]):
        total = a_ref[b] + b_ref[b]
        for lo, hi, at in ((0, VALUE, PACKED), (VALUE, PACKED, PACKED + 8)):
            part = total[lo:hi]
            top = jnp.max(jnp.abs(part), axis=(0, 1), keepdims=True)
            power = jnp.ceil(jnp.log2(jnp.maximum(top, 1e-30)))
            out_ref[b, lo:hi, :] = part * jnp.exp2(14.0 - power)
            out_ref[b, at : at + 8, :] = jnp.broadcast_to(power, (8, LANES))


def code(a, b):
    step = 4
    spec = pl.BlockSpec((step, PACKED, LANES), lambda i: (i, 0, 0))
    return pl.pallas_call(
        code_kernel,
        grid=(BLOCKS // step,),
        in_specs=[spec, spec],
        out_specs=pl.BlockSpec((step, CODED, LANES), lambda i: (i, 0, 0)),
        out_shape=jax.ShapeDtypeStruct((BLOCKS, CODED, LANES), F32),
        compiler_params=params(12),
        name="code",
    )(a, b)


def decode_kernel(x_ref, out_ref):
    for lo, hi, at in ((0, VALUE, PACKED), (VALUE, PACKED, PACKED + 8)):
        total = jnp.zeros((hi - lo, LANES), F32)
        for b in range(BLOCKS):
            total += x_ref[b, lo:hi, :] * jnp.exp2(x_ref[b, at : at + 1, :] - 14.0)
        out_ref[lo:hi, :] = total
    out_ref[PACKED:WHOLE, :] = jnp.zeros((WHOLE - PACKED, LANES), F32)


def decode(x):
    return pl.pallas_call(
        decode_kernel,
        out_shape=jax.ShapeDtypeStruct((WHOLE, LANES), F32),
        compiler_params=params(12),
        name="decode",
    )(x)


def pack_kernel(core_ref, whole_ref, targets_ref, pred_ref, out_ref):
    for j in range(4):
        lanes = slice(j * LANES, (j + 1) * LANES)
        value = whole_ref[j * HALF : (j + 1) * HALF, :]
        pred_ref[:, lanes] = value
        resid = (value - targets_ref[:, lanes]).astype(BF16)
        for b in range(BLOCKS):
            out_ref[b, j * HALF : (j + 1) * HALF, :] = resid
    coef = whole_ref[VALUE:PACKED, :].astype(BF16)
    for b in range(BLOCKS):
        out_ref[b, VALUE:PACKED, :] = coef


def pack(whole, targets, core):
    c_dim = targets.shape[1]
    return pl.pallas_call(
        pack_kernel,
        grid_spec=pltpu.PrefetchScalarGridSpec(
            num_scalar_prefetch=1,
            grid=(1,),
            in_specs=[
                pl.BlockSpec((WHOLE, LANES), lambda i, core: (0, 0)),
                pl.BlockSpec((HALF, c_dim), lambda i, core: (core[0], 0)),
            ],
            out_specs=(
                pl.BlockSpec((HALF, c_dim), lambda i, core: (0, 0)),
                pl.BlockSpec((BLOCKS, PACKED, LANES), lambda i, core: (0, 0, 0)),
            ),
        ),
        out_shape=(
            jax.ShapeDtypeStruct((HALF, c_dim), F32),
            jax.ShapeDtypeStruct((BLOCKS, PACKED, LANES), BF16),
        ),
        compiler_params=params(8),
        name="pack",
    )(core, whole, targets)


def gradient(kern_ref, got_ref, eig_ref, scale_ref, resid, head, tile, add):
    count = kern_ref.shape[1]
    group = lane_group((16, LANES))
    coefs = []
    for b in range(BLOCKS):
        at = b * HALF
        for j in range(4):
            resid[at : at + HALF, j * LANES : (j + 1) * LANES] = got_ref[
                b, j * HALF : (j + 1) * HALF, :
            ]
        tail = got_ref[b, MAIN:PACKED, :]
        zero = jnp.zeros_like(tail)
        tails = [jnp.where(group == t, tail, zero) for t in range(4)]
        coefs.append(
            jnp.concatenate(
                [got_ref[b, VALUE:MAIN, :], jnp.concatenate(tails, axis=0)], axis=1
            )
        )
    coef = jnp.concatenate(coefs, axis=0)
    corr = jnp.zeros((coef.shape[0], HALF), F32)
    for part in split(widen(eig_ref[...] * scale_ref[...])):
        corr += lax.dot_general(coef, part, NT, preferred_element_type=F32)
    head[...] = kern_ref[:, :LANES]
    head[:, :HALF] = (kern_ref[:, :HALF].astype(F32) - corr).astype(BF16)
    for at in range(0, count, tile):
        if at == 0:
            kern = jnp.concatenate([head[...], kern_ref[:, LANES:tile]], axis=1)
        else:
            kern = kern_ref[:, at : at + tile]
        add(
            slice(at, at + tile),
            lax.dot_general(kern, resid[...], TN, preferred_element_type=F32),
        )


def half_kernel(kern_ref, got_ref, eig_ref, scale_ref, out_ref, resid, head):
    def add(rows, product):
        out_ref[rows, :] = product

    gradient(kern_ref, got_ref, eig_ref, scale_ref, resid, head, 512, add)


def half_scratch(n, c_dim):
    return [pltpu.VMEM((n, c_dim), BF16), pltpu.VMEM((n, LANES), BF16)]


def half_gradient(kern, got, eig, scale, c_dim):
    n, count = kern.shape
    return pl.pallas_call(
        half_kernel,
        out_shape=jax.ShapeDtypeStruct((count, c_dim), F32),
        scratch_shapes=half_scratch(n, c_dim),
        compiler_params=params(16),
        cost_estimate=pl.CostEstimate(
            flops=20 * n * count * c_dim, bytes_accessed=4 << 20, transcendentals=0
        ),
        name="half_gradient",
    )(kern, got, eig, scale)


def step_kernel(
    step_ref,
    core_ref,
    kern_ref,
    got_ref,
    eig_ref,
    scale_ref,
    grad_ref,
    w_ref,
    own_ref,
    other_ref,
    pred_ref,
    out_ref,
    resid,
    head,
    new,
    sem,
    pred_sem,
):
    step = step_ref[0]
    core = core_ref[0]
    copies = []
    own_copy = pltpu.make_async_copy(
        own_ref, pred_ref.at[pl.ds(pl.multiple_of(core * HALF, HALF), HALF)], pred_sem.at[0]
    )
    other_copy = pltpu.make_async_copy(
        other_ref,
        pred_ref.at[pl.ds(pl.multiple_of((1 - core) * HALF, HALF), HALF)],
        pred_sem.at[1],
    )
    own_copy.start()
    other_copy.start()

    def add(rows, product):
        new[rows, :] = w_ref[rows, :] - step * (grad_ref[rows, :] + product)
        k = len(copies)
        copies.append(pltpu.make_async_copy(new.at[rows], out_ref.at[rows], sem.at[k]))
        copies[k].start()

    gradient(kern_ref, got_ref, eig_ref, scale_ref, resid, head, 256, add)
    own_copy.wait()
    other_copy.wait()
    for copy in copies:
        copy.wait()


def take_step(step, core, kern, got, eig, scale, grad, weights, own, other):
    n, count = kern.shape
    c_dim = weights.shape[1]
    smem = pl.BlockSpec(memory_space=pltpu.SMEM)
    vmem = pl.BlockSpec(memory_space=pltpu.VMEM)
    return pl.pallas_call(
        step_kernel,
        in_specs=[smem] * 2 + [vmem] * 8,
        out_specs=[pl.BlockSpec(memory_space=pltpu.HBM)] * 2,
        out_shape=(
            jax.ShapeDtypeStruct((2 * HALF, c_dim), F32),
            jax.ShapeDtypeStruct(weights.shape, F32),
        ),
        scratch_shapes=half_scratch(n, c_dim)
        + [
            pltpu.VMEM(weights.shape, F32),
            pltpu.SemaphoreType.DMA((4,)),
            pltpu.SemaphoreType.DMA((2,)),
        ],
        compiler_params=params(16),
        cost_estimate=pl.CostEstimate(
            flops=2 * n * count * c_dim, bytes_accessed=8 << 20, transcendentals=0
        ),
        name="take_step",
    )(step, core, kern, got, eig, scale, grad, weights, own, other)


def sq_norm(rows):
    return jnp.sum(rows.astype(F32) ** 2, axis=1) * scale_of(rows.shape[1])


def swap_cores(value):
    return lax.ppermute(value, "c", [(0, 1), (1, 0)])


def spread(value, axes, size):
    return lax.all_to_all(
        jnp.broadcast_to(value[None], (size,) + value.shape), axes, 0, 0, tiled=True
    )


def local(batch, targets, centers, weights, eigvec, eig_scale, step):
    core = lax.axis_index("c")
    half = core.reshape(1)
    n, d = BLOCKS * HALF, batch.shape[1]
    c_dim = weights.shape[1]

    first = lax.all_to_all(fan(batch, half), BLK, 0, 0, tiled=True).reshape(n, d)
    first, held, to_split = lax.optimization_barrier((first, centers, weights))
    second = swap_cores(first)
    cs = sq_norm(held)[None, :]
    weights3 = split_weights(to_split)
    sent, kern_first = terms(first, held, cs, weights3, eigvec)
    kept, kern_second = terms(second, held, cs, weights3, eigvec)
    coded = code(kept, swap_cores(sent)).astype(F16)

    got = lax.all_to_all(coded, BLK, 0, 0, tiled=True)
    summed = decode(got.astype(F32)).reshape(16, RING_ROWS, LANES)
    pieces = lax.all_to_all(summed, RING, 0, 0, tiled=True).sum(0)
    whole = spread(pieces, RING, 16).reshape(WHOLE, LANES)

    own_pred, packed = pack(whole, targets, half)
    got_second = lax.all_to_all(packed, BLK, 0, 0, tiled=True)
    got_second, own_pred = lax.optimization_barrier((got_second, own_pred))
    got_first = swap_cores(got_second)
    other_pred = swap_cores(own_pred)
    scale = eig_scale[None, :]
    grad = half_gradient(kern_second, got_second, eigvec, scale, c_dim)
    return take_step(
        step, half, kern_first, got_first, eigvec, scale, grad, weights, own_pred, other_pred
    )


def solution(mesh):
    fine = Mesh(mesh.devices.reshape(2, 4, 8, 2, 2), AXES)
    return jax.shard_map(
        local,
        mesh=fine,
        in_specs=(P(BLK, None), P(BLK, None), ALL, ALL, ALL, P(), P()),
        out_specs=(P(BLK, None), ALL),
        check_vma=False,
    )
```

time: 132 us -> 101 us (0.77)
  matrix products: 15.7 us -> 0 us
  Pallas kernels: 0 us -> 10.5 us
  local copies, waits for them, and re-layouts: 9.5 us -> 1.52 us
  starting transfers between devices: 15.6 us -> 7.78 us
  waiting for transfers between devices: 5.9 us -> 0.23 us
  other arithmetic: 7.12 us -> 1.52 us
  blocking collectives: 76 us -> 77.4 us
    all_to_all x2 -> x4, blocking collectives: 45.4 us -> 64 us  [the longest x1 20.9 us: local(): pieces = lax.all_to_all(summed, RING, 0, 0, tiled=True).sum(0)]
    all_to_all x2 -> x1, blocking collectives: 30.6 us -> 13.4 us  [spread(): lax.all_to_all(jnp.broadcast_to(value[None], (size,) + value.shape), axes...]
    dot_general x10 -> x0, matrix products: 15.7 us -> none  [the longest x2 5.17 us: gradient(): jnp.dot(kern.astype(jnp.bfloat16), resid, preferred_element_type=jnp.floa...]
    pallas_call x0 -> x9, Pallas kernels: none -> 10.5 us  [the longest x2 5.95 us: terms(): pl.pallas_call(terms_kernel, out_shape=(jax.ShapeDtypeStruct((BLOCKS, PAC...]
    all_to_all x1 -> x0, waiting for transfers between devices: 4.36 us -> none  [spread(): lax.all_to_all(jnp.broadcast_to(value[None], (size,) + value.shape), axes...]
    all_to_all x1 -> x0, starting transfers between devices: 3.92 us -> none  [spread(): lax.all_to_all(jnp.broadcast_to(value[None], (size,) + value.shape), axes...]
    ppermute x4, starting transfers between devices: 11.7 us -> 7.78 us  [swap_cores(): return lax.ppermute(value, 'c', [(0, 1), (1, 0)])]
    add x2 -> x0, local copies, waits for them, and re-layouts: 3.03 us -> none  [the longest x1 2.95 us: local(): summed = terms(k_mine) + swap_cores(terms(k_other))]
  transfers between devices with their start and end apart: 5 -> 4, of which waited for: 2 -> 1; matrix products, arithmetic and copies ran while one was open for 10% -> 0% of each run, Pallas kernels for 0% -> 7%
where the time goes in v3:
time: 101 us; the launch traced here: 100 us
  blocking collectives  77.4 us (77%)
  Pallas kernels  10.5 us (10%)
  starting transfers between devices  7.78 us (8%)
  local copies, waits for them, and re-layouts  1.52 us (2%)
  other arithmetic  1.52 us (2%)
  between operations  1.47 us (1%)
    all_to_all x1, blocking collectives, local(): pieces = lax.all_to_all(summed, RING, 0, 0, tiled=True).sum(0)  20.9 us
    all_to_all x1, blocking collectives, local(): lax.all_to_all(fan(batch, half), BLK, 0, 0, tiled=True).reshape(n, d)  17.4 us
    all_to_all x1, blocking collectives, local(): got = lax.all_to_all(coded, BLK, 0, 0, tiled=True)  13.7 us
    all_to_all x1, blocking collectives, spread(): lax.all_to_all(jnp.broadcast_to(value[None], (size,) + value.shape), axes...  13.4 us
    all_to_all x1, blocking collectives, local(): got_second = lax.all_to_all(packed, BLK, 0, 0, tiled=True)  12.1 us
    ppermute x4, starting transfers between devices, swap_cores(): return lax.ppermute(value, 'c', [(0, 1), (1, 0)])  7.78 us
    pallas_call x2, Pallas kernels, terms(): pl.pallas_call(terms_kernel, out_shape=(jax.ShapeDtypeStruct((BLOCKS, PAC...  5.95 us
    pallas_call x1, Pallas kernels, take_step(): pl.pallas_call(step_kernel, in_specs=[smem] * 2 + [vmem] * 8, out_specs=[...  2.38 us
  transfers between devices with their start and end apart: 4, of which 1 were waited for; matrix products, arithmetic and copies ran while one was open for 0% of the time, Pallas kernels for 7%

profile of v3, /device:TPU:1, one launch (start us, length us, event | category | flops | bytes accessed | tf_op | source)
XLA Modules:
  0.0 100.4 jit_solution(3471505423336391803)
XLA Ops:
  0.7 1.0 %copy-done.3 = bf16[128,768]{1,0:T(8,128)(2,1)S(1)} copy-done((bf16[128,768]{1,0:T(8,128)(2,1)S(1)}, bf16[128,768]{1,0:T(8,128)(2,1)}, u32[]{:S(2)}) %copy-start.3) | copy-done | bytes 196632
  1.8 17.4 %all_to_all.25 = bf16[8,64,768]{2,1,0:T(8,128)(2,1)S(1)} all-to-all(bf16[8,64,768]{2,1,0:T(8,128)(2,1)S(1)} %fan.1), channel_id=1, replica_groups=mesh['xl'=2,'y'=4,'z'=8,'xh'=2,'c'=2] {'xl','y'}, dimensions={0} | all-to-all | bytes 1572864 | tf_op jit(solution)/shard_map/all_to_all | solution.py:392
  19.1 0.4 multiply_reduce_fusion
  19.5 0.3 split_weights.1.w_ref
  19.9 2.5 %collective-permute-start = (bf16[512,768]{1,0:T(8,128)(2,1)S(1)}, bf16[512,768]{1,0:T(8,128)(2,1)S(1)}, u32[]{:S(2)}, u32[]{:S(2)}) collective-permute-start(bf16[512,768]{1,0:T(8,128)(2,1)S(1)} %bitcast.7), channel_id=1, source_target_pairs={{0,1},{1,0},{2,3},{3,2},{4,5},{5,4},{6,7},{7,6},{8,9},{9,8},{10,11... | collective-permute-start | bytes 2359304 | tf_op jit(solution)/shard_map/ppermute | solution.py:377
  22.4 3.0 %terms.2 = (f32[8,336,128]{2,1,0:T(8,128)S(1)}, bf16[512,1024]{1,0:T(8,128)(2,1)S(1)}) custom-call(bf16[512,768]{1,0:T(8,128)(2,1)S(1)} %bitcast.8, bf16[1024,768]{1,0:T(8,128)(2,1)S(1)} %copy-done.1, f32[1,1024]{1,0:T(1,128)S(1)} %bitcast.10, bf16[3072,512]{1,0:T(8,128)(2,1)S(1)} %split_weights.1.w_ref, f32[64,160]{1,0:T(8,128)S(1)} %copy-done.4), custom_call_target="tpu_custom_call" | custom-call | flops 24159191040 | bytes 6291456 | tf_op jit(solution)/shard_map/terms/pallas_call | solution.py:143
  25.3 0.5 collective-permute-start.1
  25.8 3.0 %terms.3 = (f32[8,336,128]{2,1,0:T(8,128)S(1)}, bf16[512,1024]{1,0:T(8,128)(2,1)S(1)}) custom-call(bf16[512,768]{1,0:T(8,128)(2,1)S(1)} %collective-permute-done.rows_ref, bf16[1024,768]{1,0:T(8,128)(2,1)S(1)} %copy-done.1, f32[1,1024]{1,0:T(1,128)S(1)} %bitcast.11, bf16[3072,512]{1,0:T(8,128)(2,1)S(1)} %split_weights.1.w_ref, f32[64,160]{1,0:T(8,128)S(1)} %copy-done.4), custom_call_target="tpu_custom_call" | custom-call | flops 24159191040 | bytes 6291456 | tf_op jit(solution)/shard_map/terms/pallas_call | solution.py:143
  28.8 0.5 code.1
  29.3 0.4 copy-done.6
  29.8 0.1 convert_element_type.10
  29.9 13.7 %all_to_all.26 = f16[8,352,128]{2,1,0:T(8,128)(2,1)S(1)} all-to-all(f16[8,352,128]{2,1,0:T(8,128)(2,1)S(1)} %convert_element_type.10), channel_id=1, replica_groups=mesh['xl'=2,'y'=4,'z'=8,'xh'=2,'c'=2] {'xl','y'}, dimensions={0} | all-to-all | bytes 1441792 | tf_op jit(solution)/shard_map/all_to_all | solution.py:401
  43.6 0.1 convert_element_type.11.x_ref
  43.7 0.1 decode.1
  43.8 20.9 %all_to_all.27 = f32[16,24,128]{2,1,0:T(8,128)} all-to-all(f32[16,24,128]{2,1,0:T(8,128)S(1)} %bitcast.6), channel_id=1, replica_groups=mesh['xl'=2,'y'=4,'z'=8,'xh'=2,'c'=2] {'z','xh'}, dimensions={0} | all-to-all | bytes 393216 | tf_op jit(solution)/shard_map/all_to_all | solution.py:403
  64.7 0.9 reduce_sum.19
  65.7 13.4 %all_to_all.28 = f32[16,24,128]{2,1,0:T(8,128)S(1)} all-to-all(f32[16,24,128]{2,1,0:T(8,128)S(1)} %broadcast_in_dim.4), channel_id=1, replica_groups=mesh['xl'=2,'y'=4,'z'=8,'xh'=2,'c'=2] {'z','xh'}, dimensions={0} | all-to-all | bytes 393216 | tf_op jit(solution)/shard_map/all_to_all | solution.py:381
  79.1 0.1 pack.1
  79.1 12.1 %all_to_all.29.got_ref = bf16[8,336,128]{2,1,0:T(8,128)(2,1)S(1)} all-to-all(bf16[8,336,128]{2,1,0:T(8,128)(2,1)S(1)} %get-tuple-element.19), channel_id=1, replica_groups=mesh['xl'=2,'y'=4,'z'=8,'xh'=2,'c'=2] {'xl','y'}, dimensions={0} | all-to-all | bytes 1376256 | tf_op jit(solution)/shard_map/all_to_all | solution.py:407
  91.2 4.7 %collective-permute-start.2 = (bf16[8,336,128]{2,1,0:T(8,128)(2,1)S(1)}, bf16[8,336,128]{2,1,0:T(8,128)(2,1)S(1)}, u32[]{:S(2)}, u32[]{:S(2)}) collective-permute-start(bf16[8,336,128]{2,1,0:T(8,128)(2,1)S(1)} %all_to_all.29.got_ref), channel_id=1, source_target_pairs={{0,1},{1,0},{2,3},{3,2},{4,5},{5,4},{6,7},{7,6},{8,9},{9,8},{10,11... | collective-permute-start | bytes 2064392 | tf_op jit(solution)/shard_map/ppermute | solution.py:377
  96.6 0.1 collective-permute-start.3
  96.7 1.1 %half_gradient.1.grad_ref = f32[1024,512]{1,0:T(8,128)S(1)} custom-call(bf16[512,1024]{1,0:T(8,128)(2,1)S(1)} %copy-done.7, bf16[8,336,128]{2,1,0:T(8,128)(2,1)S(1)} %all_to_all.29.got_ref, f32[64,160]{1,0:T(8,128)S(1)} %copy-done.4, f32[1,160]{1,0:T(1,128)S(1)} %bitcast.12), custom_call_target="tpu_custom_call" | custom-call | flops 5368709120 | bytes 4194304 | tf_op jit(solution)/shard_map/half_gradient/pallas_call | solution.py:287
  97.8 0.2 collective-permute-done.3.other_ref
  98.0 2.4 %take_step.1 = (f32[128,512]{1,0:T(8,128)}, f32[1024,512]{1,0:T(8,128)}) custom-call(f32[1]{0:T(128)S(6)} %copy.9.step_ref, s32[1]{0:T(128)} %bitcast.core_ref, bf16[512,1024]{1,0:T(8,128)(2,1)S(1)} %get-tuple-element.16.kern_ref, bf16[8,336,128]{2,1,0:T(8,128)(2,1)S(1)} %collective-permute-done.2.got_ref, f32[64,160]{1,0:T(8,128)S(1)} %copy-done.4, ...), custom_call_target="tpu_custom_call" | custom-call | flops 536870912 | bytes 8388608 | tf_op jit(solution)/shard_map/take_step/pallas_call | solution.py:350
  (20 shorter events, 0.1 us)
Async XLA Ops:
  0.6 18.5 %copy-start.1 = (bf16[1024,768]{1,0:T(8,128)(2,1)S(1)}, bf16[1024,768]{1,0:T(8,128)(2,1)}, u32[]{:S(2)}) copy-start(bf16[1024,768]{1,0:T(8,128)(2,1)} %cen_ref.1) | copy-start | bytes 4718596
  0.6 1.0 %copy-start.3 = (bf16[128,768]{1,0:T(8,128)(2,1)S(1)}, bf16[128,768]{1,0:T(8,128)(2,1)}, u32[]{:S(2)}) copy-start(bf16[128,768]{1,0:T(8,128)(2,1)} %rows_ref.1) | copy-start | bytes 589828
  1.7 17.8 %copy-start = (f32[1024,512]{1,0:T(8,128)S(1)}, f32[1024,512]{1,0:T(8,128)}, u32[]{:S(2)}) copy-start(f32[1024,512]{1,0:T(8,128)} %w_ref.2) | copy-start | bytes 6291460
  19.5 2.9 %copy-start.4 = (f32[64,160]{1,0:T(8,128)S(1)}, f32[64,160]{1,0:T(8,128)}, u32[]{:S(2)}) copy-start(f32[64,160]{1,0:T(8,128)} %eig_ref.3) | copy-start | bytes 122884
  19.9 5.9 %collective-permute-start = (bf16[512,768]{1,0:T(8,128)(2,1)S(1)}, bf16[512,768]{1,0:T(8,128)(2,1)S(1)}, u32[]{:S(2)}, u32[]{:S(2)}) collective-permute-start(bf16[512,768]{1,0:T(8,128)(2,1)S(1)} %bitcast.7), channel_id=1, source_target_pairs={{0,1},{1,0},{2,3},{3,2},{4,5},{5,4},{6,7},{7,6},{8,9},{9,8},{10,11... | collective-permute-start | bytes 2359304 | tf_op jit(solution)/shard_map/ppermute | solution.py:377
  25.3 3.5 %collective-permute-start.1 = (f32[8,336,128]{2,1,0:T(8,128)S(1)}, f32[8,336,128]{2,1,0:T(8,128)S(1)}, u32[]{:S(2)}, u32[]{:S(2)}) collective-permute-start(f32[8,336,128]{2,1,0:T(8,128)S(1)} %get-tuple-element.18), channel_id=1, source_target_pairs={{0,1},{1,0},{2,3},{3,2},{4,5},{5,4},{6,7},{7,6},{8,9},{9,8},{10,11... | collective-permute-start | bytes 4128776 | tf_op jit(solution)/shard_map/ppermute | solution.py:377
  28.8 1.0 copy-start.6
  43.7 35.4 %copy-start.2 = (f32[128,512]{1,0:T(8,128)S(1)}, f32[128,512]{1,0:T(8,128)}, u32[]{:S(2)}) copy-start(f32[128,512]{1,0:T(8,128)} %targets_ref.1) | copy-start | bytes 786436
  43.8 52.9 %copy-start.5 = (f32[160]{0:T(256)S(1)}, f32[160]{0:T(256)}, u32[]{:S(2)}) copy-start(f32[160]{0:T(256)} %param.12) | copy-start | bytes 1924
  65.7 31.0 %copy-start.7 = (bf16[512,1024]{1,0:T(8,128)(2,1)S(1)}, bf16[512,1024]{1,0:T(8,128)(2,1)}, u32[]{:S(2)}) copy-start(bf16[512,1024]{1,0:T(8,128)(2,1)} %copy-done.6) | copy-start | bytes 3145732
  91.2 6.8 %collective-permute-start.2 = (bf16[8,336,128]{2,1,0:T(8,128)(2,1)S(1)}, bf16[8,336,128]{2,1,0:T(8,128)(2,1)S(1)}, u32[]{:S(2)}, u32[]{:S(2)}) collective-permute-start(bf16[8,336,128]{2,1,0:T(8,128)(2,1)S(1)} %all_to_all.29.got_ref), channel_id=1, source_target_pairs={{0,1},{1,0},{2,3},{3,2},{4,5},{5,4},{6,7},{7,6},{8,9},{9,8},{10,11... | collective-permute-start | bytes 2064392 | tf_op jit(solution)/shard_map/ppermute | solution.py:377
  96.6 1.4 %collective-permute-start.3 = (f32[64,512]{1,0:T(8,128)S(1)}, f32[64,512]{1,0:T(8,128)S(1)}, u32[]{:S(2)}, u32[]{:S(2)}) collective-permute-start(f32[64,512]{1,0:T(8,128)S(1)} %get-tuple-element.23.own_ref), channel_id=1, source_target_pairs={{0,1},{1,0},{2,3},{3,2},{4,5},{5,4},{6,7},{7,6},{8,9},{9,8},{10,11... | collective-permute-start | bytes 393224 | tf_op jit(solution)/shard_map/ppermute | solution.py:377

commit v4 on v3

--- a/solution.py
+++ b/solution.py
@@ -9,7 +9,8 @@
 
 AXES = ("xl", "y", "z", "xh", "c")
 BLK = ("xl", "y")
-RING = ("z", "xh")
+PLANE = ("xl", "y", "xh")
+RING = ("xh", "z")
 ALL = P(AXES, None)
 F32 = jnp.float32
 BF16 = jnp.bfloat16
@@ -20,13 +21,21 @@
 
 HALF = 64
 BLOCKS = 8
+SUB = 32
+SUBS = 16
 LANES = 128
-VALUE = 4 * HALF
-MAIN = VALUE + HALF
-PACKED = MAIN + 16
-CODED = PACKED + 16
+VALUE = 4 * SUB
+MAIN = VALUE + SUB
+PACKED = MAIN + 8
+CODED = PACKED + 8
 RING_ROWS = 24
-WHOLE = 16 * RING_ROWS
+RING_SIZE = 8
+WHOLE = RING_SIZE * RING_ROWS
+BACK_VALUE = 2 * VALUE
+BACK_MAIN = 2 * MAIN
+BACK = 2 * PACKED
+
+
 def params(mib):
     return pltpu.CompilerParams(vmem_limit_bytes=mib << 20)
 
@@ -64,7 +73,7 @@
         out_ref[b] = rows
 
 
-def fan(batch, core):
+def fan(core, batch):
     d = batch.shape[1]
     return pl.pallas_call(
         fan_kernel,
@@ -118,21 +127,21 @@
         kern3[:, 2 * count + at : 2 * count + at + tile] = low
         if at == 0:
             coef = dot3(kern[:, :HALF], widen(e_ref[...]), NN)
-            group = lane_group((16, LANES))
-            for b in range(BLOCKS):
-                block = coef[b * HALF : (b + 1) * HALF]
+            group = lane_group((8, LANES))
+            for b in range(SUBS):
+                block = coef[b * SUB : (b + 1) * SUB]
                 out_ref[b, VALUE:MAIN, :] = block[:, :LANES]
                 tail = block[:, LANES:]
                 out_ref[b, MAIN:PACKED, :] = jnp.where(
                     group < 2,
-                    jnp.where(group == 0, tail[0:16], tail[16:32]),
-                    jnp.where(group == 2, tail[32:48], tail[48:64]),
+                    jnp.where(group == 0, tail[0:8], tail[8:16]),
+                    jnp.where(group == 2, tail[16:24], tail[24:32]),
                 )
     value = lax.dot_general(kern3[...], w_ref[...], NN, preferred_element_type=F32)
-    for b in range(BLOCKS):
+    for b in range(SUBS):
         for j in range(4):
-            out_ref[b, j * HALF : (j + 1) * HALF, :] = value[
-                b * HALF : (b + 1) * HALF, j * LANES : (j + 1) * LANES
+            out_ref[b, j * SUB : (j + 1) * SUB, :] = value[
+                b * SUB : (b + 1) * SUB, j * LANES : (j + 1) * LANES
             ]
 
 
@@ -143,7 +152,7 @@
     return pl.pallas_call(
         terms_kernel,
         out_shape=(
-            jax.ShapeDtypeStruct((BLOCKS, PACKED, LANES), F32),
+            jax.ShapeDtypeStruct((SUBS, PACKED, LANES), F32),
             jax.ShapeDtypeStruct((n, count), BF16),
         ),
         scratch_shapes=[pltpu.VMEM((n, 3 * count), BF16)],
@@ -156,34 +165,37 @@
 
 
 def code_kernel(a_ref, b_ref, out_ref):
+    upper = lax.broadcasted_iota(jnp.int32, (8, LANES), 0) < 4
     for b in range(a_ref.shape[0]):
         total = a_ref[b] + b_ref[b]
-        for lo, hi, at in ((0, VALUE, PACKED), (VALUE, PACKED, PACKED + 8)):
+        powers = []
+        for lo, hi in ((0, VALUE), (VALUE, PACKED)):
             part = total[lo:hi]
             top = jnp.max(jnp.abs(part), axis=(0, 1), keepdims=True)
             power = jnp.ceil(jnp.log2(jnp.maximum(top, 1e-30)))
             out_ref[b, lo:hi, :] = part * jnp.exp2(14.0 - power)
-            out_ref[b, at : at + 8, :] = jnp.broadcast_to(power, (8, LANES))
+            powers.append(jnp.broadcast_to(power, (8, LANES)))
+        out_ref[b, PACKED:CODED, :] = jnp.where(upper, powers[0], powers[1])
 
 
 def code(a, b):
-    step = 4
+    step = 8
     spec = pl.BlockSpec((step, PACKED, LANES), lambda i: (i, 0, 0))
     return pl.pallas_call(
         code_kernel,
-        grid=(BLOCKS // step,),
+        grid=(SUBS // step,),
         in_specs=[spec, spec],
         out_specs=pl.BlockSpec((step, CODED, LANES), lambda i: (i, 0, 0)),
-        out_shape=jax.ShapeDtypeStruct((BLOCKS, CODED, LANES), F32),
+        out_shape=jax.ShapeDtypeStruct((SUBS, CODED, LANES), F32),
         compiler_params=params(12),
         name="code",
     )(a, b)
 
 
 def decode_kernel(x_ref, out_ref):
-    for lo, hi, at in ((0, VALUE, PACKED), (VALUE, PACKED, PACKED + 8)):
+    for lo, hi, at in ((0, VALUE, PACKED), (VALUE, PACKED, PACKED + 4)):
         total = jnp.zeros((hi - lo, LANES), F32)
-        for b in range(BLOCKS):
+        for b in range(SUBS):
             total += x_ref[b, lo:hi, :] * jnp.exp2(x_ref[b, at : at + 1, :] - 14.0)
         out_ref[lo:hi, :] = total
     out_ref[PACKED:WHOLE, :] = jnp.zeros((WHOLE - PACKED, LANES), F32)
@@ -198,17 +210,42 @@
     )(x)
 
 
+def ring_kernel(x_ref, out_ref):
+    total = x_ref[0]
+    for z in range(1, RING_SIZE):
+        total += x_ref[z]
+    for k in range(2 * RING_SIZE):
+        out_ref[k] = total
+
+
+def ring_fan(x):
+    return pl.pallas_call(
+        ring_kernel,
+        out_shape=jax.ShapeDtypeStruct((2 * RING_SIZE, RING_ROWS, LANES), F32),
+        compiler_params=params(8),
+        name="ring_fan",
+    )(x)
+
+
 def pack_kernel(core_ref, whole_ref, targets_ref, pred_ref, out_ref):
-    for j in range(4):
-        lanes = slice(j * LANES, (j + 1) * LANES)
-        value = whole_ref[j * HALF : (j + 1) * HALF, :]
-        pred_ref[:, lanes] = value
-        resid = (value - targets_ref[:, lanes]).astype(BF16)
+    for h in range(2):
+        rows = slice(h * SUB, (h + 1) * SUB)
+        for j in range(4):
+            lanes = slice(j * LANES, (j + 1) * LANES)
+            value = whole_ref[h, j * SUB : (j + 1) * SUB, :]
+            pred_ref[rows, lanes] = value
+            resid = (value - targets_ref[rows, lanes]).astype(BF16)
+            at = j * HALF + h * SUB
+            for b in range(BLOCKS):
+                out_ref[b, at : at + SUB, :] = resid
+        coef = whole_ref[h, VALUE:MAIN, :].astype(BF16)
+        at = BACK_VALUE + h * SUB
         for b in range(BLOCKS):
-            out_ref[b, j * HALF : (j + 1) * HALF, :] = resid
-    coef = whole_ref[VALUE:PACKED, :].astype(BF16)
+            out_ref[b, at : at + SUB, :] = coef
+    tails = [whole_ref[h, MAIN:PACKED, :] for h in range(2)]
+    tail = jnp.concatenate(tails, axis=0).astype(BF16)
     for b in range(BLOCKS):
-        out_ref[b, VALUE:PACKED, :] = coef
+        out_ref[b, BACK_MAIN:BACK, :] = tail
 
 
 def pack(whole, targets, core):
@@ -219,17 +256,17 @@
             num_scalar_prefetch=1,
             grid=(1,),
             in_specs=[
-                pl.BlockSpec((WHOLE, LANES), lambda i, core: (0, 0)),
+                pl.BlockSpec((2, WHOLE, LANES), lambda i, core: (0, 0, 0)),
                 pl.BlockSpec((HALF, c_dim), lambda i, core: (core[0], 0)),
             ],
             out_specs=(
                 pl.BlockSpec((HALF, c_dim), lambda i, core: (0, 0)),
-                pl.BlockSpec((BLOCKS, PACKED, LANES), lambda i, core: (0, 0, 0)),
+                pl.BlockSpec((BLOCKS, BACK, LANES), lambda i, core: (0, 0, 0)),
             ),
         ),
         out_shape=(
             jax.ShapeDtypeStruct((HALF, c_dim), F32),
-            jax.ShapeDtypeStruct((BLOCKS, PACKED, LANES), BF16),
+            jax.ShapeDtypeStruct((BLOCKS, BACK, LANES), BF16),
         ),
         compiler_params=params(8),
         name="pack",
@@ -238,7 +275,7 @@
 
 def gradient(kern_ref, got_ref, eig_ref, scale_ref, resid, head, tile, add):
     count = kern_ref.shape[1]
-    group = lane_group((16, LANES))
+    group = lane_group((8, LANES))
     coefs = []
     for b in range(BLOCKS):
         at = b * HALF
@@ -246,12 +283,14 @@
             resid[at : at + HALF, j * LANES : (j + 1) * LANES] = got_ref[
                 b, j * HALF : (j + 1) * HALF, :
             ]
-        tail = got_ref[b, MAIN:PACKED, :]
-        zero = jnp.zeros_like(tail)
-        tails = [jnp.where(group == t, tail, zero) for t in range(4)]
+        tail = got_ref[b, BACK_MAIN:BACK, :].astype(F32)
+        tails = [
+            jnp.where(group == t, tail[8 * h : 8 * h + 8], 0.0) for h in range(2) for t in range(4)
+        ]
         coefs.append(
             jnp.concatenate(
-                [got_ref[b, VALUE:MAIN, :], jnp.concatenate(tails, axis=0)], axis=1
+                [got_ref[b, BACK_VALUE:BACK_MAIN, :], jnp.concatenate(tails, axis=0).astype(BF16)],
+                axis=1,
             )
         )
     coef = jnp.concatenate(coefs, axis=0)
@@ -271,6 +310,10 @@
         )
 
 
+def gradient_scratch(n, c_dim):
+    return [pltpu.VMEM((n, c_dim), BF16), pltpu.VMEM((n, LANES), BF16)]
+
+
 def half_kernel(kern_ref, got_ref, eig_ref, scale_ref, out_ref, resid, head):
     def add(rows, product):
         out_ref[rows, :] = product
@@ -278,16 +321,12 @@
     gradient(kern_ref, got_ref, eig_ref, scale_ref, resid, head, 512, add)
 
 
-def half_scratch(n, c_dim):
-    return [pltpu.VMEM((n, c_dim), BF16), pltpu.VMEM((n, LANES), BF16)]
-
-
 def half_gradient(kern, got, eig, scale, c_dim):
     n, count = kern.shape
     return pl.pallas_call(
         half_kernel,
         out_shape=jax.ShapeDtypeStruct((count, c_dim), F32),
-        scratch_shapes=half_scratch(n, c_dim),
+        scratch_shapes=gradient_scratch(n, c_dim),
         compiler_params=params(16),
         cost_estimate=pl.CostEstimate(
             flops=20 * n * count * c_dim, bytes_accessed=4 << 20, transcendentals=0
@@ -297,12 +336,12 @@
 
 
 def step_kernel(
-    step_ref,
     core_ref,
     kern_ref,
     got_ref,
     eig_ref,
     scale_ref,
+    step_ref,
     grad_ref,
     w_ref,
     own_ref,
@@ -315,9 +354,7 @@
     sem,
     pred_sem,
 ):
-    step = step_ref[0]
     core = core_ref[0]
-    copies = []
     own_copy = pltpu.make_async_copy(
         own_ref, pred_ref.at[pl.ds(pl.multiple_of(core * HALF, HALF), HALF)], pred_sem.at[0]
     )
@@ -328,6 +365,8 @@
     )
     own_copy.start()
     other_copy.start()
+    step = step_ref[...]
+    copies = []
 
     def add(rows, product):
         new[rows, :] = w_ref[rows, :] - step * (grad_ref[rows, :] + product)
@@ -342,20 +381,21 @@
         copy.wait()
 
 
-def take_step(step, core, kern, got, eig, scale, grad, weights, own, other):
+def take_step(core, kern, got, eig, scale, step, grad, weights, own, other):
     n, count = kern.shape
     c_dim = weights.shape[1]
     smem = pl.BlockSpec(memory_space=pltpu.SMEM)
     vmem = pl.BlockSpec(memory_space=pltpu.VMEM)
+    hbm = pl.BlockSpec(memory_space=pltpu.HBM)
     return pl.pallas_call(
         step_kernel,
-        in_specs=[smem] * 2 + [vmem] * 8,
-        out_specs=[pl.BlockSpec(memory_space=pltpu.HBM)] * 2,
+        in_specs=[smem] + [vmem] * 9,
+        out_specs=[hbm] * 2,
         out_shape=(
             jax.ShapeDtypeStruct((2 * HALF, c_dim), F32),
             jax.ShapeDtypeStruct(weights.shape, F32),
         ),
-        scratch_shapes=half_scratch(n, c_dim)
+        scratch_shapes=gradient_scratch(n, c_dim)
         + [
             pltpu.VMEM(weights.shape, F32),
             pltpu.SemaphoreType.DMA((4,)),
@@ -366,7 +406,7 @@
             flops=2 * n * count * c_dim, bytes_accessed=8 << 20, transcendentals=0
         ),
         name="take_step",
-    )(step, core, kern, got, eig, scale, grad, weights, own, other)
+    )(core, kern, got, eig, scale, step, grad, weights, own, other)
 
 
 def sq_norm(rows):
@@ -375,12 +415,6 @@
 
 def swap_cores(value):
     return lax.ppermute(value, "c", [(0, 1), (1, 0)])
-
-
-def spread(value, axes, size):
-    return lax.all_to_all(
-        jnp.broadcast_to(value[None], (size,) + value.shape), axes, 0, 0, tiled=True
-    )
 
 
 def local(batch, targets, centers, weights, eigvec, eig_scale, step):
@@ -389,7 +423,7 @@
     n, d = BLOCKS * HALF, batch.shape[1]
     c_dim = weights.shape[1]
 
-    first = lax.all_to_all(fan(batch, half), BLK, 0, 0, tiled=True).reshape(n, d)
+    first = lax.all_to_all(fan(half, batch), BLK, 0, 0, tiled=True).reshape(n, d)
     first, held, to_split = lax.optimization_barrier((first, centers, weights))
     second = swap_cores(first)
     cs = sq_norm(held)[None, :]
@@ -398,10 +432,10 @@
     kept, kern_second = terms(second, held, cs, weights3, eigvec)
     coded = code(kept, swap_cores(sent)).astype(F16)
 
-    got = lax.all_to_all(coded, BLK, 0, 0, tiled=True)
-    summed = decode(got.astype(F32)).reshape(16, RING_ROWS, LANES)
-    pieces = lax.all_to_all(summed, RING, 0, 0, tiled=True).sum(0)
-    whole = spread(pieces, RING, 16).reshape(WHOLE, LANES)
+    got = lax.all_to_all(coded, PLANE, 0, 0, tiled=True)
+    summed = decode(got.astype(F32)).reshape(RING_SIZE, RING_ROWS, LANES)
+    pieces = ring_fan(lax.all_to_all(summed, "z", 0, 0, tiled=True))
+    whole = lax.all_to_all(pieces, RING, 0, 0, tiled=True).reshape(2, WHOLE, LANES)
 
     own_pred, packed = pack(whole, targets, half)
     got_second = lax.all_to_all(packed, BLK, 0, 0, tiled=True)
@@ -411,7 +445,16 @@
     scale = eig_scale[None, :]
     grad = half_gradient(kern_second, got_second, eigvec, scale, c_dim)
     return take_step(
-        step, half, kern_first, got_first, eigvec, scale, grad, weights, own_pred, other_pred
+        half,
+        kern_first,
+        got_first,
+        eigvec,
+        scale,
+        step[None, :],
+        grad,
+        weights,
+        own_pred,
+        other_pred,
     )
 
 

time: 101 us -> 95.3 us (0.944)
  blocking collectives: 77.4 us -> 72.4 us
    all_to_all x4, blocking collectives: 65.3 us -> 61.6 us  [the longest x1 17.4 us: local(): lax.all_to_all(fan(half, batch), BLK, 0, 0, tiled=True).reshape(n, d)]
    all_to_all x1, blocking collectives: 12.1 us -> 10.8 us  [local(): got_second = lax.all_to_all(packed, BLK, 0, 0, tiled=True)]
    pallas_call x4 -> x5, Pallas kernels: 8.84 us -> 9.04 us  [the longest x2 5.97 us: terms(): pl.pallas_call(terms_kernel, out_shape=(jax.ShapeDtypeStruct((SUBS, PACKE...]
where the time goes in v4:
time: 95.3 us; the launch traced here: 94.9 us
  blocking collectives  72.4 us (76%)
  Pallas kernels  10.7 us (11%)
  starting transfers between devices  8.54 us (9%)
  between operations  1.43 us (2%)
  local copies, waits for them, and re-layouts  1.07 us (1%)
    all_to_all x1, blocking collectives, local(): lax.all_to_all(fan(half, batch), BLK, 0, 0, tiled=True).reshape(n, d)  17.4 us
    all_to_all x1, blocking collectives, local(): got = lax.all_to_all(coded, PLANE, 0, 0, tiled=True)  16.8 us
    all_to_all x1, blocking collectives, local(): pieces = ring_fan(lax.all_to_all(summed, 'z', 0, 0, tiled=True))  15.7 us
    all_to_all x1, blocking collectives, local(): lax.all_to_all(pieces, RING, 0, 0, tiled=True).reshape(2, WHOLE, LANES)  11.7 us
    all_to_all x1, blocking collectives, local(): got_second = lax.all_to_all(packed, BLK, 0, 0, tiled=True)  10.8 us
    ppermute x4, starting transfers between devices, swap_cores(): return lax.ppermute(value, 'c', [(0, 1), (1, 0)])  8.54 us
    pallas_call x2, Pallas kernels, terms(): pl.pallas_call(terms_kernel, out_shape=(jax.ShapeDtypeStruct((SUBS, PACKE...  5.97 us
    pallas_call x1, Pallas kernels, take_step(): pl.pallas_call(step_kernel, in_specs=[smem] + [vmem] * 9, out_specs=[hbm]...  2.54 us
  transfers between devices with their start and end apart: 4, of which 1 were waited for; matrix products, arithmetic and copies ran while one was open for 0% of the time, Pallas kernels for 7%

profile of v4, /device:TPU:1, one launch (start us, length us, event | category | flops | bytes accessed | tf_op | source)
XLA Modules:
  0.0 94.9 jit_solution(6130386754520645294)
XLA Ops:
  0.7 1.0 %copy-done.3 = bf16[128,768]{1,0:T(8,128)(2,1)S(1)} copy-done((bf16[128,768]{1,0:T(8,128)(2,1)S(1)}, bf16[128,768]{1,0:T(8,128)(2,1)}, u32[]{:S(2)}) %copy-start.3) | copy-done | bytes 196632
  1.7 0.1 fan.1
  1.8 17.4 %all_to_all.25 = bf16[8,64,768]{2,1,0:T(8,128)(2,1)S(1)} all-to-all(bf16[8,64,768]{2,1,0:T(8,128)(2,1)S(1)} %fan.1), channel_id=1, replica_groups=mesh['xl'=2,'y'=4,'z'=8,'xh'=2,'c'=2] {'xl','y'}, dimensions={0} | all-to-all | bytes 1572864 | tf_op jit(solution)/shard_map/all_to_all | solution.py:426
  19.1 0.4 multiply_reduce_fusion
  19.5 0.4 split_weights.1.w_ref
  19.9 2.5 %collective-permute-start = (bf16[512,768]{1,0:T(8,128)(2,1)S(1)}, bf16[512,768]{1,0:T(8,128)(2,1)S(1)}, u32[]{:S(2)}, u32[]{:S(2)}) collective-permute-start(bf16[512,768]{1,0:T(8,128)(2,1)S(1)} %bitcast.8), channel_id=1, source_target_pairs={{0,1},{1,0},{2,3},{3,2},{4,5},{5,4},{6,7},{7,6},{8,9},{9,8},{10,11... | collective-permute-start | bytes 2359304 | tf_op jit(solution)/shard_map/ppermute | solution.py:417
  22.4 3.0 %terms.2 = (f32[16,168,128]{2,1,0:T(8,128)S(1)}, bf16[512,1024]{1,0:T(8,128)(2,1)S(1)}) custom-call(bf16[512,768]{1,0:T(8,128)(2,1)S(1)} %bitcast.9, bf16[1024,768]{1,0:T(8,128)(2,1)S(1)} %copy-done.1, f32[1,1024]{1,0:T(1,128)S(1)} %bitcast.12, bf16[3072,512]{1,0:T(8,128)(2,1)S(1)} %split_weights.1.w_ref, f32[64,160]{1,0:T(8,128)S(1)} %copy-done.4), custom_call_target="tpu_custom_call" | custom-call | flops 24159191040 | bytes 6291456 | tf_op jit(solution)/shard_map/terms/pallas_call | solution.py:152
  25.4 0.5 collective-permute-start.1
  25.8 3.0 %terms.3 = (f32[16,168,128]{2,1,0:T(8,128)S(1)}, bf16[512,1024]{1,0:T(8,128)(2,1)S(1)}) custom-call(bf16[512,768]{1,0:T(8,128)(2,1)S(1)} %collective-permute-done.rows_ref, bf16[1024,768]{1,0:T(8,128)(2,1)S(1)} %copy-done.1, f32[1,1024]{1,0:T(1,128)S(1)} %bitcast.13, bf16[3072,512]{1,0:T(8,128)(2,1)S(1)} %split_weights.1.w_ref, f32[64,160]{1,0:T(8,128)S(1)} %copy-done.4), custom_call_target="tpu_custom_call" | custom-call | flops 24159191040 | bytes 6291456 | tf_op jit(solution)/shard_map/terms/pallas_call | solution.py:152
  28.8 0.5 code.1
  29.4 0.1 convert_element_type.10
  29.5 16.8 %all_to_all.26 = f16[16,176,128]{2,1,0:T(8,128)(2,1)S(1)} all-to-all(f16[16,176,128]{2,1,0:T(8,128)(2,1)S(1)} %convert_element_type.10), channel_id=1, replica_groups=mesh['xl'=2,'y'=4,'z'=8,'xh'=2,'c'=2] {'xl','y','xh'}, dimensions={0} | all-to-all | bytes 1441792 | tf_op jit(solution)/shard_map/all_to_all | solution.py:435
  46.3 0.1 convert_element_type.11.x_ref
  46.4 0.0 copy-start.2
  46.4 0.1 decode.1
  46.5 15.7 %all_to_all.27.x_ref = f32[8,24,128]{2,1,0:T(8,128)S(1)} all-to-all(f32[8,24,128]{2,1,0:T(8,128)S(1)} %bitcast.11), channel_id=1, replica_groups=mesh['xl'=2,'y'=4,'z'=8,'xh'=2,'c'=2] {'z'}, dimensions={0} | all-to-all | bytes 196608 | tf_op jit(solution)/shard_map/all_to_all | solution.py:437
  62.2 11.7 %all_to_all.28 = f32[16,24,128]{2,1,0:T(8,128)S(1)} all-to-all(f32[16,24,128]{2,1,0:T(8,128)S(1)} %ring_fan.1), channel_id=1, replica_groups=mesh['xl'=2,'y'=4,'z'=8,'xh'=2,'c'=2] {'xh','z'}, dimensions={0} | all-to-all | bytes 393216 | tf_op jit(solution)/shard_map/all_to_all | solution.py:438
  73.9 0.1 pack.1
  74.0 10.8 %all_to_all.29.got_ref = bf16[8,336,128]{2,1,0:T(8,128)(2,1)S(1)} all-to-all(bf16[8,336,128]{2,1,0:T(8,128)(2,1)S(1)} %get-tuple-element.19), channel_id=1, replica_groups=mesh['xl'=2,'y'=4,'z'=8,'xh'=2,'c'=2] {'xl','y'}, dimensions={0} | all-to-all | bytes 1376256 | tf_op jit(solution)/shard_map/all_to_all | solution.py:441
  84.8 5.5 %collective-permute-start.2 = (bf16[8,336,128]{2,1,0:T(8,128)(2,1)S(1)}, bf16[8,336,128]{2,1,0:T(8,128)(2,1)S(1)}, u32[]{:S(2)}, u32[]{:S(2)}) collective-permute-start(bf16[8,336,128]{2,1,0:T(8,128)(2,1)S(1)} %all_to_all.29.got_ref), channel_id=1, source_target_pairs={{0,1},{1,0},{2,3},{3,2},{4,5},{5,4},{6,7},{7,6},{8,9},{9,8},{10,11... | collective-permute-start | bytes 2064392 | tf_op jit(solution)/shard_map/ppermute | solution.py:417
  91.0 0.1 collective-permute-start.3
  91.1 1.1 %half_gradient.1.grad_ref = f32[1024,512]{1,0:T(8,128)S(1)} custom-call(bf16[512,1024]{1,0:T(8,128)(2,1)S(1)} %get-tuple-element.22.kern_ref, bf16[8,336,128]{2,1,0:T(8,128)(2,1)S(1)} %all_to_all.29.got_ref, f32[64,160]{1,0:T(8,128)S(1)} %copy-done.4, f32[1,160]{1,0:T(1,128)S(1)} %bitcast.14), custom_call_target="tpu_custom_call" | custom-call | flops 5368709120 | bytes 4194304 | tf_op jit(solution)/shard_map/half_gradient/pallas_call | solution.py:326
  92.2 0.2 collective-permute-done.3.other_ref
  92.4 2.5 %take_step.1 = (f32[128,512]{1,0:T(8,128)}, f32[1024,512]{1,0:T(8,128)}) custom-call(s32[1]{0:T(128)} %bitcast.core_ref, bf16[512,1024]{1,0:T(8,128)(2,1)S(1)} %get-tuple-element.16.kern_ref, bf16[8,336,128]{2,1,0:T(8,128)(2,1)S(1)} %collective-permute-done.2.got_ref, f32[64,160]{1,0:T(8,128)S(1)} %copy-done.4, f32[1,160]{1,0:T(1,128)S(1)} %bitcast.15, ...), custom_call_target="tpu_custom_call" | custom-call | flops 536870912 | bytes 8388608 | tf_op jit(solution)/shard_map/take_step/pallas_call | solution.py:390
  (15 shorter events, 0.1 us)
Async XLA Ops:
  0.6 18.5 %copy-start.1 = (bf16[1024,768]{1,0:T(8,128)(2,1)S(1)}, bf16[1024,768]{1,0:T(8,128)(2,1)}, u32[]{:S(2)}) copy-start(bf16[1024,768]{1,0:T(8,128)(2,1)} %cen_ref.1) | copy-start | bytes 4718596
  0.6 1.0 %copy-start.3 = (bf16[128,768]{1,0:T(8,128)(2,1)S(1)}, bf16[128,768]{1,0:T(8,128)(2,1)}, u32[]{:S(2)}) copy-start(bf16[128,768]{1,0:T(8,128)(2,1)} %rows_ref.1) | copy-start | bytes 589828
  1.7 17.8 %copy-start = (f32[1024,512]{1,0:T(8,128)S(1)}, f32[1024,512]{1,0:T(8,128)}, u32[]{:S(2)}) copy-start(f32[1024,512]{1,0:T(8,128)} %w_ref.2) | copy-start | bytes 6291460
  19.5 2.9 %copy-start.4 = (f32[64,160]{1,0:T(8,128)S(1)}, f32[64,160]{1,0:T(8,128)}, u32[]{:S(2)}) copy-start(f32[64,160]{1,0:T(8,128)} %eig_ref.3) | copy-start | bytes 122884
  19.9 5.9 %collective-permute-start = (bf16[512,768]{1,0:T(8,128)(2,1)S(1)}, bf16[512,768]{1,0:T(8,128)(2,1)S(1)}, u32[]{:S(2)}, u32[]{:S(2)}) collective-permute-start(bf16[512,768]{1,0:T(8,128)(2,1)S(1)} %bitcast.8), channel_id=1, source_target_pairs={{0,1},{1,0},{2,3},{3,2},{4,5},{5,4},{6,7},{7,6},{8,9},{9,8},{10,11... | collective-permute-start | bytes 2359304 | tf_op jit(solution)/shard_map/ppermute | solution.py:417
  25.4 3.4 %collective-permute-start.1 = (f32[16,168,128]{2,1,0:T(8,128)S(1)}, f32[16,168,128]{2,1,0:T(8,128)S(1)}, u32[]{:S(2)}, u32[]{:S(2)}) collective-permute-start(f32[16,168,128]{2,1,0:T(8,128)S(1)} %get-tuple-element.18), channel_id=1, source_target_pairs={{0,1},{1,0},{2,3},{3,2},{4,5},{5,4},{6,7},{7,6},{8,9},{9,8},{10,11... | collective-permute-start | bytes 4128776 | tf_op jit(solution)/shard_map/ppermute | solution.py:417
  46.4 27.6 %copy-start.2 = (f32[128,512]{1,0:T(8,128)S(1)}, f32[128,512]{1,0:T(8,128)}, u32[]{:S(2)}) copy-start(f32[128,512]{1,0:T(8,128)} %targets_ref.1) | copy-start | bytes 786436
  46.5 44.6 %copy-start.5 = (f32[160]{0:T(256)S(1)}, f32[160]{0:T(256)}, u32[]{:S(2)}) copy-start(f32[160]{0:T(256)} %param.12) | copy-start | bytes 1924
  84.8 7.6 %collective-permute-start.2 = (bf16[8,336,128]{2,1,0:T(8,128)(2,1)S(1)}, bf16[8,336,128]{2,1,0:T(8,128)(2,1)S(1)}, u32[]{:S(2)}, u32[]{:S(2)}) collective-permute-start(bf16[8,336,128]{2,1,0:T(8,128)(2,1)S(1)} %all_to_all.29.got_ref), channel_id=1, source_target_pairs={{0,1},{1,0},{2,3},{3,2},{4,5},{5,4},{6,7},{7,6},{8,9},{9,8},{10,11... | collective-permute-start | bytes 2064392 | tf_op jit(solution)/shard_map/ppermute | solution.py:417
  91.0 1.4 %collective-permute-start.3 = (f32[64,512]{1,0:T(8,128)S(1)}, f32[64,512]{1,0:T(8,128)S(1)}, u32[]{:S(2)}, u32[]{:S(2)}) collective-permute-start(f32[64,512]{1,0:T(8,128)S(1)} %get-tuple-element.23.own_ref), channel_id=1, source_target_pairs={{0,1},{1,0},{2,3},{3,2},{4,5},{5,4},{6,7},{7,6},{8,9},{9,8},{10,11... | collective-permute-start | bytes 393224 | tf_op jit(solution)/shard_map/ppermute | solution.py:417

commit v5 on v4

v5 whole, which is shorter than its diff:
```python
import math

import jax
import jax.numpy as jnp
from jax import lax
from jax.experimental import pallas as pl
from jax.experimental.pallas import tpu as pltpu
from jax.sharding import Mesh, PartitionSpec as P

AXES = ("xl", "y", "z", "xh", "c")
BLK = ("xl", "y")
PLANE = ("xl", "y", "xh")
ALL = P(AXES, None)
F32 = jnp.float32
BF16 = jnp.bfloat16
F16 = jnp.float16
NT = (((1,), (1,)), ((), ()))
NN = (((1,), (0,)), ((), ()))
TN = (((0,), (0,)), ((), ()))

HALF = 64
BLOCKS = 8
SUB = 32
SUBS = 16
LANES = 128
VALUE = 4 * SUB
MAIN = VALUE + SUB
PACKED = MAIN + 8
CODED = PACKED + 8
RING_SIZE = 8


def params(mib):
    return pltpu.CompilerParams(vmem_limit_bytes=mib << 20)


def split(value):
    high = value.astype(BF16)
    return high, (value - high.astype(F32)).astype(BF16)


def dot3(a, b, dims):
    a_hi, a_lo = split(a)
    b_hi, b_lo = split(b)

    def one(x, y):
        return lax.dot_general(x, y, dims, preferred_element_type=F32)

    return one(a_hi, b_hi) + one(a_hi, b_lo) + one(a_lo, b_hi)


def widen(eig):
    return jnp.concatenate([eig[:, :LANES]] + [eig[:, LANES:]] * 4, axis=1)


def lane_group(shape):
    return lax.broadcasted_iota(jnp.int32, shape, len(shape) - 1) // 32


def scale_of(features):
    return 4.0 / features * math.log2(math.e)


def fan_kernel(core_ref, hi_ref, blk_ref, rows_ref, out_ref):
    rows = rows_ref[...]
    for b in range(BLOCKS):
        out_ref[b] = rows


def fan(core, hi, blk, batch):
    d = batch.shape[1]
    return pl.pallas_call(
        fan_kernel,
        grid_spec=pltpu.PrefetchScalarGridSpec(
            num_scalar_prefetch=3,
            grid=(1,),
            in_specs=[pl.BlockSpec((HALF, d), lambda i, core, hi, blk: (1 - core[0], 0))],
            out_specs=pl.BlockSpec((BLOCKS, HALF, d), lambda i, core, hi, blk: (0, 0, 0)),
        ),
        out_shape=jax.ShapeDtypeStruct((BLOCKS, HALF, d), batch.dtype),
        compiler_params=params(8),
        name="fan",
    )(core, hi, blk, batch)


def weights_kernel(w_ref, out_ref):
    count = w_ref.shape[0]
    high, low = split(w_ref[...])
    out_ref[:count] = high
    out_ref[count : 2 * count] = low
    out_ref[2 * count :] = high


def split_weights(weights):
    count, c_dim = weights.shape
    return pl.pallas_call(
        weights_kernel,
        out_shape=jax.ShapeDtypeStruct((3 * count, c_dim), BF16),
        compiler_params=params(12),
        cost_estimate=pl.CostEstimate(flops=0, bytes_accessed=5 << 20, transcendentals=0),
        name="split_weights",
    )(weights)


def terms_kernel(rows_ref, cen_ref, cs_ref, w_ref, e_ref, out_ref, kern_ref, kern3):
    n, d = rows_ref.shape
    count = cen_ref.shape[0]
    tile = 512
    scale = scale_of(d)
    rows = rows_ref[...]
    wide = rows.astype(F32)
    rs = jnp.sum(wide * wide, axis=1, keepdims=True) * scale
    for at in range(0, count, tile):
        cols = slice(at, at + tile)
        cross = lax.dot_general(rows, cen_ref[cols, :], NT, preferred_element_type=F32)
        kern = jnp.exp2(cross * (2.0 * scale) - rs - cs_ref[:, cols])
        high, low = split(kern)
        kern3[:, at : at + tile] = high
        kern3[:, count + at : count + at + tile] = high
        kern_ref[:, cols] = high
        kern3[:, 2 * count + at : 2 * count + at + tile] = low
        if at == 0:
            coef = dot3(kern[:, :HALF], widen(e_ref[...]), NN)
            group = lane_group((8, LANES))
            for b in range(SUBS):
                block = coef[b * SUB : (b + 1) * SUB]
                out_ref[b, VALUE:MAIN, :] = block[:, :LANES]
                tail = block[:, LANES:]
                out_ref[b, MAIN:PACKED, :] = jnp.where(
                    group < 2,
                    jnp.where(group == 0, tail[0:8], tail[8:16]),
                    jnp.where(group == 2, tail[16:24], tail[24:32]),
                )
    value = lax.dot_general(kern3[...], w_ref[...], NN, preferred_element_type=F32)
    for b in range(SUBS):
        for j in range(4):
            out_ref[b, j * SUB : (j + 1) * SUB, :] = value[
                b * SUB : (b + 1) * SUB, j * LANES : (j + 1) * LANES
            ]


def terms(rows, centers, cs, weights3, eig):
    n, d = rows.shape
    count = centers.shape[0]
    c_dim = weights3.shape[1]
    return pl.pallas_call(
        terms_kernel,
        out_shape=(
            jax.ShapeDtypeStruct((SUBS, PACKED, LANES), F32),
            jax.ShapeDtypeStruct((n, count), BF16),
        ),
        scratch_shapes=[pltpu.VMEM((n, 3 * count), BF16)],
        compiler_params=params(24),
        cost_estimate=pl.CostEstimate(
            flops=20 * n * count * (d + 3 * c_dim), bytes_accessed=6 << 20, transcendentals=n * count
        ),
        name="terms",
    )(rows, centers, cs, weights3, eig)


def scaled(part):
    top = jnp.max(jnp.abs(part), axis=(0, 1), keepdims=True)
    power = jnp.ceil(jnp.log2(jnp.maximum(top, 1e-30)))
    return part * jnp.exp2(14.0 - power), power


def powers_tile(value_power, coef_power):
    upper = lax.broadcasted_iota(jnp.int32, (8, LANES), 0) < 4
    return jnp.where(upper, value_power, coef_power)


def unscale(ref, b):
    value = jnp.exp2(ref[b, PACKED : PACKED + 1, :] - 14.0)
    coef = jnp.exp2(ref[b, PACKED + 4 : PACKED + 5, :] - 14.0)
    return value, coef


def sum_blocks(ref):
    value = jnp.zeros((VALUE, LANES), F32)
    coef = jnp.zeros((PACKED - VALUE, LANES), F32)
    for b in range(ref.shape[0]):
        value_scale, coef_scale = unscale(ref, b)
        value += ref[b, :VALUE, :] * value_scale
        coef += ref[b, VALUE:PACKED, :] * coef_scale
    return value, coef


def code_kernel(a_ref, b_ref, out_ref):
    for b in range(a_ref.shape[0]):
        total = a_ref[b] + b_ref[b]
        value, value_power = scaled(total[:VALUE])
        coef, coef_power = scaled(total[VALUE:])
        out_ref[b, :VALUE, :] = value
        out_ref[b, VALUE:PACKED, :] = coef
        out_ref[b, PACKED:CODED, :] = powers_tile(value_power, coef_power)


def code(a, b):
    step = 8
    spec = pl.BlockSpec((step, PACKED, LANES), lambda i: (i, 0, 0))
    return pl.pallas_call(
        code_kernel,
        grid=(SUBS // step,),
        in_specs=[spec, spec],
        out_specs=pl.BlockSpec((step, CODED, LANES), lambda i: (i, 0, 0)),
        out_shape=jax.ShapeDtypeStruct((SUBS, CODED, LANES), F32),
        compiler_params=params(12),
        name="code",
    )(a, b)


def recode_kernel(x_ref, out_ref):
    value, coef = sum_blocks(x_ref)
    value, value_power = scaled(value)
    coef, coef_power = scaled(coef)
    out_ref[:VALUE, :] = value
    out_ref[VALUE:PACKED, :] = coef
    out_ref[PACKED:CODED, :] = powers_tile(value_power, coef_power)


def recode(x):
    return pl.pallas_call(
        recode_kernel,
        out_shape=jax.ShapeDtypeStruct((CODED, LANES), F32),
        compiler_params=params(12),
        name="recode",
    )(x)


def pack_kernel(core_ref, hi_ref, blk_ref, x_ref, targets_ref, out_ref):
    value, coef = sum_blocks(x_ref)
    row = pl.multiple_of(core_ref[0] * HALF + hi_ref[0] * SUB, SUB)
    resid = []
    for j in range(4):
        target = targets_ref[pl.ds(row, SUB), j * LANES : (j + 1) * LANES]
        resid.append(value[j * SUB : (j + 1) * SUB] - target)
    resid, resid_power = scaled(jnp.concatenate(resid, axis=0))
    value, value_power = scaled(value)
    coef, coef_power = scaled(coef)
    resid_tile = powers_tile(resid_power, coef_power)
    value_tile = powers_tile(value_power, coef_power)
    for b in range(SUBS):
        out_ref[b, :VALUE, :] = resid
        out_ref[b, VALUE:PACKED, :] = coef
        out_ref[b, PACKED:CODED, :] = resid_tile
    for h in range(2):
        b = blk_ref[0] * 2 + h
        out_ref[b, :VALUE, :] = value
        out_ref[b, PACKED:CODED, :] = value_tile


def pack(core, hi, blk, x, targets):
    smem = pl.BlockSpec(memory_space=pltpu.SMEM)
    vmem = pl.BlockSpec(memory_space=pltpu.VMEM)
    return pl.pallas_call(
        pack_kernel,
        in_specs=[smem] * 3 + [vmem] * 2,
        out_shape=jax.ShapeDtypeStruct((SUBS, CODED, LANES), F32),
        compiler_params=params(12),
        name="pack",
    )(core, hi, blk, x, targets)


def gradient(
    half, blk, kern_ref, got_ref, eig_ref, scale_ref, targets_ref, pred_ref, resid, head, tile, add
):
    count = kern_ref.shape[1]
    group = lane_group((8, LANES))
    coefs = []
    for b in range(SUBS):
        value_scale, coef_scale = unscale(got_ref, b)
        for j in range(4):
            resid[b * SUB : (b + 1) * SUB, j * LANES : (j + 1) * LANES] = (
                got_ref[b, j * SUB : (j + 1) * SUB, :] * value_scale
            ).astype(BF16)
        main = got_ref[b, VALUE:MAIN, :] * coef_scale
        tail = got_ref[b, MAIN:PACKED, :] * coef_scale
        tails = [jnp.where(group == t, tail, 0.0) for t in range(4)]
        coefs.append(jnp.concatenate([main, jnp.concatenate(tails, axis=0)], axis=1).astype(BF16))
    for h in range(2):
        b = blk * 2 + h
        value_scale, _ = unscale(got_ref, b)
        row = pl.multiple_of(half * HALF + h * SUB, SUB)
        for j in range(4):
            lanes = slice(j * LANES, (j + 1) * LANES)
            value = got_ref[b, j * SUB : (j + 1) * SUB, :] * value_scale
            pred_ref[h * SUB : (h + 1) * SUB, lanes] = value
            target = targets_ref[pl.ds(row, SUB), lanes]
            resid[pl.ds(pl.multiple_of(b * SUB, SUB), SUB), lanes] = (value - target).astype(BF16)
    coef = jnp.concatenate(coefs, axis=0)
    corr = jnp.zeros((coef.shape[0], HALF), F32)
    for part in split(widen(eig_ref[...] * scale_ref[...])):
        corr += lax.dot_general(coef, part, NT, preferred_element_type=F32)
    head[...] = kern_ref[:, :LANES]
    head[:, :HALF] = (kern_ref[:, :HALF].astype(F32) - corr).astype(BF16)
    for at in range(0, count, tile):
        if at == 0:
            kern = jnp.concatenate([head[...], kern_ref[:, LANES:tile]], axis=1)
        else:
            kern = kern_ref[:, at : at + tile]
        add(
            slice(at, at + tile),
            lax.dot_general(kern, resid[...], TN, preferred_element_type=F32),
        )


def gradient_scratch(n, c_dim):
    return [pltpu.VMEM((n, c_dim), BF16), pltpu.VMEM((n, LANES), BF16)]


def half_kernel(
    core_ref,
    blk_ref,
    kern_ref,
    got_ref,
    eig_ref,
    scale_ref,
    targets_ref,
    pred_ref,
    out_ref,
    resid,
    head,
):
    def add(rows, product):
        out_ref[rows, :] = product

    gradient(
        core_ref[0],
        blk_ref[0],
        kern_ref,
        got_ref,
        eig_ref,
        scale_ref,
        targets_ref,
        pred_ref,
        resid,
        head,
        512,
        add,
    )


def half_gradient(core, blk, kern, got, eig, scale, targets):
    n, count = kern.shape
    c_dim = targets.shape[1]
    smem = pl.BlockSpec(memory_space=pltpu.SMEM)
    vmem = pl.BlockSpec(memory_space=pltpu.VMEM)
    return pl.pallas_call(
        half_kernel,
        in_specs=[smem] * 2 + [vmem] * 5,
        out_shape=(
            jax.ShapeDtypeStruct((HALF, c_dim), F32),
            jax.ShapeDtypeStruct((count, c_dim), F32),
        ),
        scratch_shapes=gradient_scratch(n, c_dim),
        compiler_params=params(16),
        cost_estimate=pl.CostEstimate(
            flops=20 * n * count * c_dim, bytes_accessed=4 << 20, transcendentals=0
        ),
        name="half_gradient",
    )(core, blk, kern, got, eig, scale, targets)


def step_kernel(
    core_ref,
    blk_ref,
    kern_ref,
    got_ref,
    eig_ref,
    scale_ref,
    targets_ref,
    step_ref,
    grad_ref,
    w_ref,
    own_ref,
    pred_ref,
    out_ref,
    resid,
    head,
    other,
    new,
    sem,
    pred_sem,
):
    core = core_ref[0]
    own_copy = pltpu.make_async_copy(
        own_ref, pred_ref.at[pl.ds(pl.multiple_of(core * HALF, HALF), HALF)], pred_sem.at[0]
    )
    own_copy.start()
    step = step_ref[...]
    copies = []

    def add(rows, product):
        new[rows, :] = w_ref[rows, :] - step * (grad_ref[rows, :] + product)
        k = len(copies)
        copies.append(pltpu.make_async_copy(new.at[rows], out_ref.at[rows], sem.at[k]))
        copies[k].start()

    gradient(
        1 - core,
        blk_ref[0],
        kern_ref,
        got_ref,
        eig_ref,
        scale_ref,
        targets_ref,
        other,
        resid,
        head,
        256,
        add,
    )
    other_copy = pltpu.make_async_copy(
        other, pred_ref.at[pl.ds(pl.multiple_of((1 - core) * HALF, HALF), HALF)], pred_sem.at[1]
    )
    other_copy.start()
    own_copy.wait()
    for copy in copies:
        copy.wait()
    other_copy.wait()


def take_step(core, blk, kern, got, eig, scale, targets, step, grad, weights, own):
    n, count = kern.shape
    c_dim = weights.shape[1]
    smem = pl.BlockSpec(memory_space=pltpu.SMEM)
    vmem = pl.BlockSpec(memory_space=pltpu.VMEM)
    hbm = pl.BlockSpec(memory_space=pltpu.HBM)
    return pl.pallas_call(
        step_kernel,
        in_specs=[smem] * 2 + [vmem] * 9,
        out_specs=[hbm] * 2,
        out_shape=(
            jax.ShapeDtypeStruct(targets.shape, F32),
            jax.ShapeDtypeStruct(weights.shape, F32),
        ),
        scratch_shapes=gradient_scratch(n, c_dim)
        + [
            pltpu.VMEM((HALF, c_dim), F32),
            pltpu.VMEM(weights.shape, F32),
            pltpu.SemaphoreType.DMA((4,)),
            pltpu.SemaphoreType.DMA((2,)),
        ],
        compiler_params=params(16),
        cost_estimate=pl.CostEstimate(
            flops=2 * n * count * c_dim, bytes_accessed=8 << 20, transcendentals=0
        ),
        name="take_step",
    )(core, blk, kern, got, eig, scale, targets, step, grad, weights, own)


def sq_norm(rows):
    return jnp.sum(rows.astype(F32) ** 2, axis=1) * scale_of(rows.shape[1])


def swap_cores(value):
    return lax.ppermute(value, "c", [(0, 1), (1, 0)])


def local(batch, targets, centers, weights, eigvec, eig_scale, step):
    core = lax.axis_index("c").reshape(1)
    hi = lax.axis_index("xh").reshape(1)
    blk = lax.axis_index(BLK).reshape(1)
    n, d = BLOCKS * HALF, batch.shape[1]

    first = lax.all_to_all(fan(core, hi, blk, batch), BLK, 0, 0, tiled=True).reshape(n, d)
    first, held, to_split = lax.optimization_barrier((first, centers, weights))
    second = swap_cores(first)
    cs = sq_norm(held)[None, :]
    weights3 = split_weights(to_split)
    sent, kern_first = terms(first, held, cs, weights3, eigvec)
    kept, kern_second = terms(second, held, cs, weights3, eigvec)
    coded = code(kept, swap_cores(sent)).astype(F16)

    got = lax.all_to_all(coded, PLANE, 0, 0, tiled=True).astype(F32)
    partial = recode(got).astype(F16)
    partial = jnp.broadcast_to(partial[None], (RING_SIZE,) + partial.shape)
    ring = lax.all_to_all(partial, "z", 0, 0, tiled=True).astype(F32)

    packed = pack(core, hi, blk, ring, targets).astype(F16)
    got_second = lax.all_to_all(packed, PLANE, 0, 0, tiled=True)
    got_first = swap_cores(got_second)
    scale = eig_scale[None, :]
    own, grad = half_gradient(
        core, blk, kern_second, got_second.astype(F32), eigvec, scale, targets
    )
    return take_step(
        core,
        blk,
        kern_first,
        got_first.astype(F32),
        eigvec,
        scale,
        targets,
        step[None, :],
        grad,
        weights,
        own,
    )


def solution(mesh):
    fine = Mesh(mesh.devices.reshape(2, 4, 8, 2, 2), AXES)
    return jax.shard_map(
        local,
        mesh=fine,
        in_specs=(P(BLK, None), P(BLK, None), ALL, ALL, ALL, P(), P()),
        out_specs=(P(BLK, None), ALL),
        check_vma=False,
    )
```

time: 95.3 us -> 89.8 us (0.942)
  blocking collectives: 72.4 us -> 67.6 us
  starting transfers between devices: 8.54 us -> 7.26 us
    all_to_all x5 -> x4, blocking collectives: 72.4 us -> 67.6 us  [the longest x1 19.1 us: local(): ring = lax.all_to_all(partial, 'z', 0, 0, tiled=True).astype(F32)]
    ppermute x4 -> x3, starting transfers between devices: 8.54 us -> 7.26 us  [swap_cores(): return lax.ppermute(value, 'c', [(0, 1), (1, 0)])]
    pallas_call x5 -> x4, Pallas kernels: 3.82 us -> 4.22 us  [the longest x1 2.57 us: take_step(): pl.pallas_call(step_kernel, in_specs=[smem] * 2 + [vmem] * 9, out_specs=[...]
  transfers between devices with their start and end apart: 4 -> 3, of which waited for: 1 -> 0; matrix products, arithmetic and copies ran while one was open for 0% -> 0% of each run, Pallas kernels for 7% -> 8%
where the time goes in v5:
time: 89.8 us; the launch traced here: 89.5 us
  blocking collectives  67.6 us (75%)
  Pallas kernels  11.1 us (12%)
  starting transfers between devices  7.26 us (8%)
  between operations  1.49 us (2%)
  local copies, waits for them, and re-layouts  1.12 us (1%)
  other arithmetic  0.92 us (1%)
    all_to_all x1, blocking collectives, local(): ring = lax.all_to_all(partial, 'z', 0, 0, tiled=True).astype(F32)  19.1 us
    all_to_all x1, blocking collectives, local(): lax.all_to_all(fan(core, hi, blk, batch), BLK, 0, 0, tiled=True)  17.4 us
    all_to_all x1, blocking collectives, local(): got = lax.all_to_all(coded, PLANE, 0, 0, tiled=True).astype(F32)  16.8 us
    all_to_all x1, blocking collectives, local(): got_second = lax.all_to_all(packed, PLANE, 0, 0, tiled=True)  14.3 us
    ppermute x3, starting transfers between devices, swap_cores(): return lax.ppermute(value, 'c', [(0, 1), (1, 0)])  7.26 us
    pallas_call x2, Pallas kernels, terms(): pl.pallas_call(terms_kernel, out_shape=(jax.ShapeDtypeStruct((SUBS, PACKE...  5.96 us
    pallas_call x1, Pallas kernels, take_step(): pl.pallas_call(step_kernel, in_specs=[smem] * 2 + [vmem] * 9, out_specs=[...  2.57 us
  transfers between devices with their start and end apart: 3, of which 0 were waited for; matrix products, arithmetic and copies ran while one was open for 0% of the time, Pallas kernels for 8%

profile of v5, /device:TPU:1, one launch (start us, length us, event | category | flops | bytes accessed | tf_op | source)
XLA Modules:
  0.0 89.5 jit_solution(7291516899151600371)
XLA Ops:
  0.7 1.0 %copy-done.3 = bf16[128,768]{1,0:T(8,128)(2,1)S(1)} copy-done((bf16[128,768]{1,0:T(8,128)(2,1)S(1)}, bf16[128,768]{1,0:T(8,128)(2,1)}, u32[]{:S(2)}) %copy-start.3) | copy-done | bytes 196632
  1.7 0.1 fan.1
  1.8 17.4 %all_to_all.20 = bf16[8,64,768]{2,1,0:T(8,128)(2,1)S(1)} all-to-all(bf16[8,64,768]{2,1,0:T(8,128)(2,1)S(1)} %fan.1), channel_id=1, replica_groups=mesh['xl'=2,'y'=4,'z'=8,'xh'=2,'c'=2] {'xl','y'}, dimensions={0} | all-to-all | bytes 1572864 | tf_op jit(solution)/shard_map/all_to_all | solution.py:466
  19.1 0.4 multiply_reduce_fusion
  19.5 0.4 split_weights.1.w_ref
  19.9 2.5 %collective-permute-start = (bf16[512,768]{1,0:T(8,128)(2,1)S(1)}, bf16[512,768]{1,0:T(8,128)(2,1)S(1)}, u32[]{:S(2)}, u32[]{:S(2)}) collective-permute-start(bf16[512,768]{1,0:T(8,128)(2,1)S(1)} %bitcast.8), channel_id=1, source_target_pairs={{0,1},{1,0},{2,3},{3,2},{4,5},{5,4},{6,7},{7,6},{8,9},{9,8},{10,11... | collective-permute-start | bytes 2359304 | tf_op jit(solution)/shard_map/ppermute | solution.py:457
  22.4 3.0 %terms.2 = (f32[16,168,128]{2,1,0:T(8,128)S(1)}, bf16[512,1024]{1,0:T(8,128)(2,1)S(1)}) custom-call(bf16[512,768]{1,0:T(8,128)(2,1)S(1)} %bitcast.9, bf16[1024,768]{1,0:T(8,128)(2,1)S(1)} %copy-done.1, f32[1,1024]{1,0:T(1,128)S(1)} %bitcast.10, bf16[3072,512]{1,0:T(8,128)(2,1)S(1)} %split_weights.1.w_ref, f32[64,160]{1,0:T(8,128)S(1)} %copy-done.4), custom_call_target="tpu_custom_call" | custom-call | flops 24159191040 | bytes 6291456 | tf_op jit(solution)/shard_map/terms/pallas_call | solution.py:146
  25.4 0.5 collective-permute-start.1
  25.8 3.0 %terms.3 = (f32[16,168,128]{2,1,0:T(8,128)S(1)}, bf16[512,1024]{1,0:T(8,128)(2,1)S(1)}) custom-call(bf16[512,768]{1,0:T(8,128)(2,1)S(1)} %collective-permute-done.rows_ref, bf16[1024,768]{1,0:T(8,128)(2,1)S(1)} %copy-done.1, f32[1,1024]{1,0:T(1,128)S(1)} %bitcast.11, bf16[3072,512]{1,0:T(8,128)(2,1)S(1)} %split_weights.1.w_ref, f32[64,160]{1,0:T(8,128)S(1)} %copy-done.4), custom_call_target="tpu_custom_call" | custom-call | flops 24159191040 | bytes 6291456 | tf_op jit(solution)/shard_map/terms/pallas_call | solution.py:146
  28.8 0.5 code.1
  29.3 0.1 convert_element_type.25
  29.5 16.8 %all_to_all.21 = f16[16,176,128]{2,1,0:T(8,128)(2,1)S(1)} all-to-all(f16[16,176,128]{2,1,0:T(8,128)(2,1)S(1)} %convert_element_type.25), channel_id=1, replica_groups=mesh['xl'=2,'y'=4,'z'=8,'xh'=2,'c'=2] {'xl','y','xh'}, dimensions={0} | all-to-all | bytes 1441792 | tf_op jit(solution)/shard_map/all_to_all | solution.py:475
  46.3 0.1 convert_element_type.26.x_ref
  46.4 0.2 recode.1
  46.7 0.1 broadcast_in_dim.6
  46.7 19.1 %all_to_all.22 = f16[8,176,128]{2,1,0:T(8,128)(2,1)S(1)} all-to-all(f16[8,176,128]{2,1,0:T(8,128)(2,1)S(1)} %broadcast_in_dim.6), channel_id=1, replica_groups=mesh['xl'=2,'y'=4,'z'=8,'xh'=2,'c'=2] {'z'}, dimensions={0} | all-to-all | bytes 720896 | tf_op jit(solution)/shard_map/all_to_all | solution.py:478
  65.9 0.3 pack.1
  66.2 0.1 convert_element_type.29
  66.3 14.3 %all_to_all.23 = f16[16,176,128]{2,1,0:T(8,128)(2,1)S(1)} all-to-all(f16[16,176,128]{2,1,0:T(8,128)(2,1)S(1)} %convert_element_type.29), channel_id=1, replica_groups=mesh['xl'=2,'y'=4,'z'=8,'xh'=2,'c'=2] {'xl','y','xh'}, dimensions={0} | all-to-all | bytes 1441792 | tf_op jit(solution)/shard_map/all_to_all | solution.py:481
  80.6 4.3 %collective-permute-start.2 = (f16[16,176,128]{2,1,0:T(8,128)(2,1)S(1)}, f16[16,176,128]{2,1,0:T(8,128)(2,1)S(1)}, u32[]{:S(2)}, u32[]{:S(2)}) collective-permute-start(f16[16,176,128]{2,1,0:T(8,128)(2,1)S(1)} %all_to_all.23), channel_id=1, source_target_pairs={{0,1},{1,0},{2,3},{3,2},{4,5},{5,4},{6,7},{7,6},{8,9},{9,8},{10,11... | collective-permute-start | bytes 2162696 | tf_op jit(solution)/shard_map/ppermute | solution.py:457
  85.6 0.1 convert_element_type.31.got_ref
  85.7 1.1 %half_gradient.1 = (f32[64,512]{1,0:T(8,128)S(1)}, f32[1024,512]{1,0:T(8,128)S(1)}) custom-call(s32[1]{0:T(128)} %bitcast.core_ref, s32[1]{0:T(128)} %bitcast.1.blk_ref, bf16[512,1024]{1,0:T(8,128)(2,1)S(1)} %get-tuple-element.17.kern_ref, f32[16,176,128]{2,1,0:T(8,128)S(1)} %convert_element_type.31.got_ref, f32[64,160]{1,0:T(8,128)S(1)} %copy-done.4, ...), custom_call_target="tpu_custom_call" | custom-call | flops 5368709120 | bytes 4194304 | tf_op jit(solution)/shard_map/half_gradient/pallas_call | solution.py:348
  86.8 0.1 convert_element_type.30.got_ref
  86.9 2.6 %take_step.1 = (f32[128,512]{1,0:T(8,128)}, f32[1024,512]{1,0:T(8,128)}) custom-call(s32[1]{0:T(128)} %bitcast.core_ref, s32[1]{0:T(128)} %bitcast.1.blk_ref, bf16[512,1024]{1,0:T(8,128)(2,1)S(1)} %get-tuple-element.14.kern_ref, f32[16,176,128]{2,1,0:T(8,128)S(1)} %convert_element_type.30.got_ref, f32[64,160]{1,0:T(8,128)S(1)} %copy-done.4, ...), custom_call_target="tpu_custom_call" | custom-call | flops 536870912 | bytes 8388608 | tf_op jit(solution)/shard_map/take_step/pallas_call | solution.py:429
  (17 shorter events, 0.1 us)
Async XLA Ops:
  0.6 18.5 %copy-start.1 = (bf16[1024,768]{1,0:T(8,128)(2,1)S(1)}, bf16[1024,768]{1,0:T(8,128)(2,1)}, u32[]{:S(2)}) copy-start(bf16[1024,768]{1,0:T(8,128)(2,1)} %cen_ref.1) | copy-start | bytes 4718596
  0.6 1.0 %copy-start.3 = (bf16[128,768]{1,0:T(8,128)(2,1)S(1)}, bf16[128,768]{1,0:T(8,128)(2,1)}, u32[]{:S(2)}) copy-start(bf16[128,768]{1,0:T(8,128)(2,1)} %rows_ref.1) | copy-start | bytes 589828
  1.7 17.8 %copy-start = (f32[1024,512]{1,0:T(8,128)S(1)}, f32[1024,512]{1,0:T(8,128)}, u32[]{:S(2)}) copy-start(f32[1024,512]{1,0:T(8,128)} %w_ref.2) | copy-start | bytes 6291460
  19.5 2.9 %copy-start.4 = (f32[64,160]{1,0:T(8,128)S(1)}, f32[64,160]{1,0:T(8,128)}, u32[]{:S(2)}) copy-start(f32[64,160]{1,0:T(8,128)} %eig_ref.3) | copy-start | bytes 122884
  19.9 5.9 %collective-permute-start = (bf16[512,768]{1,0:T(8,128)(2,1)S(1)}, bf16[512,768]{1,0:T(8,128)(2,1)S(1)}, u32[]{:S(2)}, u32[]{:S(2)}) collective-permute-start(bf16[512,768]{1,0:T(8,128)(2,1)S(1)} %bitcast.8), channel_id=1, source_target_pairs={{0,1},{1,0},{2,3},{3,2},{4,5},{5,4},{6,7},{7,6},{8,9},{9,8},{10,11... | collective-permute-start | bytes 2359304 | tf_op jit(solution)/shard_map/ppermute | solution.py:457
  25.4 3.4 %collective-permute-start.1 = (f32[16,168,128]{2,1,0:T(8,128)S(1)}, f32[16,168,128]{2,1,0:T(8,128)S(1)}, u32[]{:S(2)}, u32[]{:S(2)}) collective-permute-start(f32[16,168,128]{2,1,0:T(8,128)S(1)} %get-tuple-element.16), channel_id=1, source_target_pairs={{0,1},{1,0},{2,3},{3,2},{4,5},{5,4},{6,7},{7,6},{8,9},{9,8},{10,11... | collective-permute-start | bytes 4128776 | tf_op jit(solution)/shard_map/ppermute | solution.py:457
  46.4 19.5 %copy-start.2 = (f32[128,512]{1,0:T(8,128)S(1)}, f32[128,512]{1,0:T(8,128)}, u32[]{:S(2)}) copy-start(f32[128,512]{1,0:T(8,128)} %targets_ref.5) | copy-start | bytes 786436
  66.3 19.4 %copy-start.5 = (f32[160]{0:T(256)S(1)}, f32[160]{0:T(256)}, u32[]{:S(2)}) copy-start(f32[160]{0:T(256)} %param.12) | copy-start | bytes 1924
  80.6 6.2 %collective-permute-start.2 = (f16[16,176,128]{2,1,0:T(8,128)(2,1)S(1)}, f16[16,176,128]{2,1,0:T(8,128)(2,1)S(1)}, u32[]{:S(2)}, u32[]{:S(2)}) collective-permute-start(f16[16,176,128]{2,1,0:T(8,128)(2,1)S(1)} %all_to_all.23), channel_id=1, source_target_pairs={{0,1},{1,0},{2,3},{3,2},{4,5},{5,4},{6,7},{7,6},{8,9},{9,8},{10,11... | collective-permute-start | bytes 2162696 | tf_op jit(solution)/shard_map/ppermute | solution.py:457

commit v6 on v5

v6 whole, which is shorter than its diff:
```python
import math

import jax
import jax.numpy as jnp
from jax import lax
from jax.experimental import pallas as pl
from jax.experimental.pallas import tpu as pltpu
from jax.sharding import Mesh, PartitionSpec as P

AXES = ("xl", "y", "zh", "zl", "xh", "c")
BLK = ("xl", "y")
SUB_AXES = ("xh", "zl")
NEAR = BLK + SUB_AXES
FAR = "zh"
ALL = P(AXES, None)
F32 = jnp.float32
BF16 = jnp.bfloat16
F16 = jnp.float16
NT = (((1,), (1,)), ((), ()))
NN = (((1,), (0,)), ((), ()))
TN = (((0,), (0,)), ((), ()))

HALF = 64
BLOCKS = 8
SUB = 16
SUBS = 32
PER_BLOCK = HALF // SUB
LANES = 128
VALUE = 4 * SUB
MAIN = VALUE + SUB
CODED = MAIN + 8
FAR_SIZE = 4


def params(mib):
    return pltpu.CompilerParams(vmem_limit_bytes=mib << 20)


def split(value):
    high = value.astype(BF16)
    return high, (value - high.astype(F32)).astype(BF16)


def dot3(a, b, dims):
    a_hi, a_lo = split(a)
    b_hi, b_lo = split(b)

    def one(x, y):
        return lax.dot_general(x, y, dims, preferred_element_type=F32)

    return one(a_hi, b_hi) + one(a_hi, b_lo) + one(a_lo, b_hi)


def widen(eig):
    return jnp.concatenate([eig[:, :LANES]] + [eig[:, LANES:]] * 4, axis=1)


def lane_group(shape):
    return lax.broadcasted_iota(jnp.int32, shape, len(shape) - 1) // 32


def scale_of(features):
    return 4.0 / features * math.log2(math.e)


def fan_kernel(core_ref, sub_ref, blk_ref, rows_ref, out_ref):
    rows = rows_ref[...]
    for b in range(BLOCKS):
        out_ref[b] = rows


def fan(core, sub, blk, batch):
    d = batch.shape[1]
    return pl.pallas_call(
        fan_kernel,
        grid_spec=pltpu.PrefetchScalarGridSpec(
            num_scalar_prefetch=3,
            grid=(1,),
            in_specs=[pl.BlockSpec((HALF, d), lambda i, core, sub, blk: (1 - core[0], 0))],
            out_specs=pl.BlockSpec((BLOCKS, HALF, d), lambda i, core, sub, blk: (0, 0, 0)),
        ),
        out_shape=jax.ShapeDtypeStruct((BLOCKS, HALF, d), batch.dtype),
        compiler_params=params(8),
        name="fan",
    )(core, sub, blk, batch)


def weights_kernel(w_ref, e_ref, out_ref, e_out):
    count = w_ref.shape[0]
    e_out[...] = widen(e_ref[...])
    high, low = split(w_ref[...])
    out_ref[:count] = high
    out_ref[count : 2 * count] = low
    out_ref[2 * count :] = high


def split_weights(weights, eig):
    count, c_dim = weights.shape
    return pl.pallas_call(
        weights_kernel,
        out_shape=(
            jax.ShapeDtypeStruct((3 * count, c_dim), BF16),
            jax.ShapeDtypeStruct((HALF, 2 * LANES), F32),
        ),
        compiler_params=params(12),
        cost_estimate=pl.CostEstimate(flops=0, bytes_accessed=5 << 20, transcendentals=0),
        name="split_weights",
    )(weights, eig)


def terms_kernel(rows_ref, cen_ref, cs_ref, w_ref, e_ref, out_ref, kern_ref, kern3):
    n, d = rows_ref.shape
    count = cen_ref.shape[0]
    tile = 512
    scale = scale_of(d)
    rows = rows_ref[...]
    wide = rows.astype(F32)
    rs = jnp.sum(wide * wide, axis=1, keepdims=True) * scale
    for at in range(0, count, tile):
        cols = slice(at, at + tile)
        cross = lax.dot_general(rows, cen_ref[cols, :], NT, preferred_element_type=F32)
        kern = jnp.exp2(cross * (2.0 * scale) - rs - cs_ref[:, cols])
        high, low = split(kern)
        kern3[:, at : at + tile] = high
        kern3[:, count + at : count + at + tile] = high
        kern_ref[:, cols] = high
        kern3[:, 2 * count + at : 2 * count + at + tile] = low
        if at == 0:
            coef = dot3(kern[:, :HALF], e_ref[...], NN)
            group = lane_group((8, LANES))
            for b in range(SUBS):
                block = coef[b * SUB : (b + 1) * SUB]
                out_ref[b, VALUE:MAIN, :] = block[:, :LANES]
                tail = block[:, LANES:]
                out_ref[b, MAIN:CODED, :] = jnp.where(
                    group == 0, tail[:8], jnp.where(group == 1, tail[8:], 0.0)
                )
    value = lax.dot_general(kern3[...], w_ref[...], NN, preferred_element_type=F32)
    for b in range(SUBS):
        for j in range(4):
            out_ref[b, j * SUB : (j + 1) * SUB, :] = value[
                b * SUB : (b + 1) * SUB, j * LANES : (j + 1) * LANES
            ]


def terms(rows, centers, cs, weights3, eig):
    n, d = rows.shape
    count = centers.shape[0]
    c_dim = weights3.shape[1]
    return pl.pallas_call(
        terms_kernel,
        out_shape=(
            jax.ShapeDtypeStruct((SUBS, CODED, LANES), F32),
            jax.ShapeDtypeStruct((n, count), BF16),
        ),
        scratch_shapes=[pltpu.VMEM((n, 3 * count), BF16)],
        compiler_params=params(24),
        cost_estimate=pl.CostEstimate(
            flops=20 * n * count * (d + 3 * c_dim), bytes_accessed=6 << 20, transcendentals=n * count
        ),
        name="terms",
    )(rows, centers, cs, weights3, eig)


def scaled(part):
    top = jnp.max(jnp.abs(part), axis=(0, 1), keepdims=True)
    power = jnp.ceil(jnp.log2(jnp.maximum(top, 1e-30)))
    return part * jnp.exp2(14.0 - power), power


def with_powers(coef, value_power, coef_power):
    group = lane_group((8, LANES))
    powers = jnp.where(group == 2, value_power, coef_power)
    tile = jnp.where(group < 2, coef[SUB:], powers)
    return coef[:SUB], tile


def unscale(ref, b):
    value = jnp.exp2(ref[b, MAIN : MAIN + 1, 64:65] - 14.0)
    coef = jnp.exp2(ref[b, MAIN : MAIN + 1, 96:97] - 14.0)
    return value, coef


def sum_blocks(ref):
    value = jnp.zeros((VALUE, LANES), F32)
    main = jnp.zeros((SUB, LANES), F32)
    tile = jnp.zeros((8, LANES), F32)
    for b in range(ref.shape[0]):
        value_scale, coef_scale = unscale(ref, b)
        value += ref[b, :VALUE, :] * value_scale
        main += ref[b, VALUE:MAIN, :] * coef_scale
        tile += ref[b, MAIN:CODED, :] * coef_scale
    tile = jnp.where(lane_group((8, LANES)) < 2, tile, 0.0)
    return value, jnp.concatenate([main, tile], axis=0)


def code_kernel(a_ref, b_ref, out_ref):
    for b in range(SUBS):
        total = a_ref[b] + b_ref[b]
        value, value_power = scaled(total[:VALUE])
        coef, coef_power = scaled(total[VALUE:])
        main, tile = with_powers(coef, value_power, coef_power)
        out_ref[b, :VALUE, :] = value
        out_ref[b, VALUE:MAIN, :] = main
        out_ref[b, MAIN:CODED, :] = tile


def code(a, b):
    return pl.pallas_call(
        code_kernel,
        out_shape=jax.ShapeDtypeStruct((SUBS, CODED, LANES), F32),
        compiler_params=params(12),
        name="code",
    )(a, b)


def recode_kernel(x_ref, out_ref):
    value, coef = sum_blocks(x_ref)
    value, value_power = scaled(value)
    coef, coef_power = scaled(coef)
    main, tile = with_powers(coef, value_power, coef_power)
    out_ref[:VALUE, :] = value
    out_ref[VALUE:MAIN, :] = main
    out_ref[MAIN:CODED, :] = tile


def recode(x):
    return pl.pallas_call(
        recode_kernel,
        out_shape=jax.ShapeDtypeStruct((CODED, LANES), F32),
        compiler_params=params(12),
        name="recode",
    )(x)


def pack_kernel(core_ref, sub_ref, blk_ref, x_ref, targets_ref, out_ref):
    value, coef = sum_blocks(x_ref)
    row = pl.multiple_of(core_ref[0] * HALF + sub_ref[0] * SUB, SUB)
    resid = []
    for j in range(4):
        target = targets_ref[pl.ds(row, SUB), j * LANES : (j + 1) * LANES]
        resid.append(value[j * SUB : (j + 1) * SUB] - target)
    resid, resid_power = scaled(jnp.concatenate(resid, axis=0))
    value, value_power = scaled(value)
    coef, coef_power = scaled(coef)
    main, tile = with_powers(coef, resid_power, coef_power)
    for b in range(SUBS):
        out_ref[b, :VALUE, :] = resid
        out_ref[b, VALUE:MAIN, :] = main
        out_ref[b, MAIN:CODED, :] = tile
    _, tile = with_powers(coef, value_power, coef_power)
    for h in range(PER_BLOCK):
        b = blk_ref[0] * PER_BLOCK + h
        out_ref[b, :VALUE, :] = value
        out_ref[b, MAIN:CODED, :] = tile


def pack(core, sub, blk, x, targets):
    smem = pl.BlockSpec(memory_space=pltpu.SMEM)
    vmem = pl.BlockSpec(memory_space=pltpu.VMEM)
    return pl.pallas_call(
        pack_kernel,
        in_specs=[smem] * 3 + [vmem] * 2,
        out_shape=jax.ShapeDtypeStruct((SUBS, CODED, LANES), F32),
        compiler_params=params(12),
        name="pack",
    )(core, sub, blk, x, targets)


def gradient(
    half, blk, kern_ref, got_ref, eig_ref, scale_ref, targets_ref, pred_ref, resid, head, tile, add
):
    count = kern_ref.shape[1]
    group = lane_group((8, LANES))
    coefs = []
    for b in range(SUBS):
        value_scale, coef_scale = unscale(got_ref, b)
        for j in range(4):
            resid[b * SUB : (b + 1) * SUB, j * LANES : (j + 1) * LANES] = (
                got_ref[b, j * SUB : (j + 1) * SUB, :] * value_scale
            ).astype(BF16)
        main = got_ref[b, VALUE:MAIN, :] * coef_scale
        tile_rows = got_ref[b, MAIN:CODED, :] * coef_scale
        tails = [jnp.where(group == t, tile_rows, 0.0) for t in range(2)]
        coefs.append(jnp.concatenate([main, jnp.concatenate(tails, axis=0)], axis=1).astype(BF16))
    for h in range(PER_BLOCK):
        b = blk * PER_BLOCK + h
        value_scale, _ = unscale(got_ref, b)
        row = pl.multiple_of(half * HALF + h * SUB, SUB)
        for j in range(4):
            lanes = slice(j * LANES, (j + 1) * LANES)
            value = got_ref[b, j * SUB : (j + 1) * SUB, :] * value_scale
            pred_ref[h * SUB : (h + 1) * SUB, lanes] = value
            target = targets_ref[pl.ds(row, SUB), lanes]
            resid[pl.ds(pl.multiple_of(b * SUB, SUB), SUB), lanes] = (value - target).astype(BF16)
    coef = jnp.concatenate(coefs, axis=0)
    corr = jnp.zeros((coef.shape[0], HALF), F32)
    for part in split(eig_ref[...] * widen(scale_ref[:, : LANES + 32])):
        corr += lax.dot_general(coef, part, NT, preferred_element_type=F32)
    head[...] = kern_ref[:, :LANES]
    head[:, :HALF] = (kern_ref[:, :HALF].astype(F32) - corr).astype(BF16)
    for at in [*range(tile, count, tile), 0]:
        if at == 0:
            kern = jnp.concatenate([head[...], kern_ref[:, LANES:tile]], axis=1)
        else:
            kern = kern_ref[:, at : at + tile]
        add(
            slice(at, at + tile),
            lax.dot_general(kern, resid[...], TN, preferred_element_type=F32),
        )


def gradient_scratch(n, c_dim):
    return [pltpu.VMEM((n, c_dim), BF16), pltpu.VMEM((n, LANES), BF16)]


def half_kernel(
    core_ref,
    blk_ref,
    kern_ref,
    got_ref,
    eig_ref,
    scale_ref,
    targets_ref,
    w_ref,
    pred_ref,
    out_ref,
    resid,
    head,
):
    step = scale_ref[:, LANES + 32 :]

    def add(rows, product):
        out_ref[rows, :] = w_ref[rows, :] - step * product

    gradient(
        core_ref[0],
        blk_ref[0],
        kern_ref,
        got_ref,
        eig_ref,
        scale_ref,
        targets_ref,
        pred_ref,
        resid,
        head,
        512,
        add,
    )


def half_step(core, blk, kern, got, eig, scale, targets, weights):
    n, count = kern.shape
    c_dim = targets.shape[1]
    smem = pl.BlockSpec(memory_space=pltpu.SMEM)
    vmem = pl.BlockSpec(memory_space=pltpu.VMEM)
    return pl.pallas_call(
        half_kernel,
        in_specs=[smem] * 2 + [vmem] * 6,
        out_shape=(
            jax.ShapeDtypeStruct((HALF, c_dim), F32),
            jax.ShapeDtypeStruct((count, c_dim), F32),
        ),
        scratch_shapes=gradient_scratch(n, c_dim),
        compiler_params=params(16),
        cost_estimate=pl.CostEstimate(
            flops=20 * n * count * c_dim, bytes_accessed=4 << 20, transcendentals=0
        ),
        name="half_step",
    )(core, blk, kern, got, eig, scale, targets, weights)


def step_kernel(
    core_ref,
    blk_ref,
    kern_ref,
    got_ref,
    eig_ref,
    scale_ref,
    targets_ref,
    base_ref,
    own_ref,
    pred_ref,
    out_ref,
    resid,
    head,
    other,
    new,
    sem,
    pred_sem,
):
    core = core_ref[0]
    own_copy = pltpu.make_async_copy(
        own_ref, pred_ref.at[pl.ds(pl.multiple_of(core * HALF, HALF), HALF)], pred_sem.at[0]
    )
    own_copy.start()
    step = scale_ref[:, LANES + 32 :]
    copies = []

    def add(rows, product):
        new[rows, :] = base_ref[rows, :] - step * product
        k = len(copies)
        copies.append(pltpu.make_async_copy(new.at[rows], out_ref.at[rows], sem.at[k]))
        copies[k].start()

    gradient(
        1 - core,
        blk_ref[0],
        kern_ref,
        got_ref,
        eig_ref,
        scale_ref,
        targets_ref,
        other,
        resid,
        head,
        256,
        add,
    )
    other_copy = pltpu.make_async_copy(
        other, pred_ref.at[pl.ds(pl.multiple_of((1 - core) * HALF, HALF), HALF)], pred_sem.at[1]
    )
    other_copy.start()
    own_copy.wait()
    for copy in copies:
        copy.wait()
    other_copy.wait()


def take_step(core, blk, kern, got, eig, scale, targets, base, own):
    n, count = kern.shape
    c_dim = base.shape[1]
    smem = pl.BlockSpec(memory_space=pltpu.SMEM)
    vmem = pl.BlockSpec(memory_space=pltpu.VMEM)
    hbm = pl.BlockSpec(memory_space=pltpu.HBM)
    return pl.pallas_call(
        step_kernel,
        in_specs=[smem] * 2 + [vmem] * 7,
        out_specs=[hbm] * 2,
        out_shape=(
            jax.ShapeDtypeStruct(targets.shape, F32),
            jax.ShapeDtypeStruct(base.shape, F32),
        ),
        scratch_shapes=gradient_scratch(n, c_dim)
        + [
            pltpu.VMEM((HALF, c_dim), F32),
            pltpu.VMEM(base.shape, F32),
            pltpu.SemaphoreType.DMA((4,)),
            pltpu.SemaphoreType.DMA((2,)),
        ],
        compiler_params=params(16),
        cost_estimate=pl.CostEstimate(
            flops=2 * n * count * c_dim, bytes_accessed=8 << 20, transcendentals=0
        ),
        name="take_step",
    )(core, blk, kern, got, eig, scale, targets, base, own)


def sq_norm(rows):
    return jnp.sum(rows.astype(F32) ** 2, axis=1) * scale_of(rows.shape[1])


def swap_cores(value):
    return lax.ppermute(value, "c", [(0, 1), (1, 0)])


def local(batch, targets, centers, weights, eigvec, eig_scale, step):
    core = lax.axis_index("c").reshape(1)
    sub = lax.axis_index(SUB_AXES).reshape(1)
    blk = lax.axis_index(BLK).reshape(1)
    n, d = BLOCKS * HALF, batch.shape[1]

    first = lax.all_to_all(fan(core, sub, blk, batch), BLK, 0, 0, tiled=True).reshape(n, d)
    first, held, to_split = lax.optimization_barrier((first, centers, weights))
    second = swap_cores(first)
    cs = sq_norm(held)[None, :]
    weights3, eig = split_weights(to_split, eigvec)
    sent, kern_first = terms(first, held, cs, weights3, eig)
    kept, kern_second = terms(second, held, cs, weights3, eig)
    coded = code(kept, swap_cores(sent)).astype(F16)

    got = lax.all_to_all(coded, NEAR, 0, 0, tiled=True).astype(F32)
    partial = recode(got).astype(F16)
    partial = jnp.broadcast_to(partial[None], (FAR_SIZE,) + partial.shape)
    far = lax.all_to_all(partial, FAR, 0, 0, tiled=True).astype(F32)

    packed = pack(core, sub, blk, far, targets).astype(F16)
    got_second = lax.all_to_all(packed, NEAR, 0, 0, tiled=True)
    got_first = swap_cores(got_second)
    scale = jnp.concatenate([eig_scale, step])[None, :]
    own, base = half_step(
        core, blk, kern_second, got_second.astype(F32), eig, scale, targets, weights
    )
    return take_step(
        core, blk, kern_first, got_first.astype(F32), eig, scale, targets, base, own
    )


def solution(mesh):
    fine = Mesh(mesh.devices.reshape(2, 4, 4, 2, 2, 2), AXES)
    return jax.shard_map(
        local,
        mesh=fine,
        in_specs=(P(BLK, None), P(BLK, None), ALL, ALL, ALL, P(), P()),
        out_specs=(P(BLK, None), ALL),
        check_vma=False,
    )
```

time: 89.8 us -> 86.9 us (0.968)
  blocking collectives: 67.6 us -> 64.7 us
    all_to_all x4, blocking collectives: 67.6 us -> 64.7 us  [the longest x1 19 us: local(): got = lax.all_to_all(coded, NEAR, 0, 0, tiled=True).astype(F32)]
  transfers between devices with their start and end apart: 3 -> 3, of which waited for: 0 -> 1; matrix products, arithmetic and copies ran while one was open for 0% -> 0% of each run, Pallas kernels for 8% -> 9%
where the time goes in v6:
time: 86.9 us; the launch traced here: 86.6 us
  blocking collectives  64.7 us (74%)
  Pallas kernels  11.1 us (13%)
  starting transfers between devices  7.05 us (8%)
  between operations  1.48 us (2%)
  local copies, waits for them, and re-layouts  1.08 us (1%)
  other arithmetic  0.95 us (1%)
    all_to_all x1, blocking collectives, local(): got = lax.all_to_all(coded, NEAR, 0, 0, tiled=True).astype(F32)  19 us
    all_to_all x1, blocking collectives, local(): lax.all_to_all(fan(core, sub, blk, batch), BLK, 0, 0, tiled=True)  17.4 us
    all_to_all x1, blocking collectives, local(): got_second = lax.all_to_all(packed, NEAR, 0, 0, tiled=True)  14.2 us
    all_to_all x1, blocking collectives, local(): far = lax.all_to_all(partial, FAR, 0, 0, tiled=True).astype(F32)  14.1 us
    ppermute x3, starting transfers between devices, swap_cores(): return lax.ppermute(value, 'c', [(0, 1), (1, 0)])  7.05 us
    pallas_call x2, Pallas kernels, terms(): pl.pallas_call(terms_kernel, out_shape=(jax.ShapeDtypeStruct((SUBS, CODED...  5.94 us
    pallas_call x1, Pallas kernels, take_step(): pl.pallas_call(step_kernel, in_specs=[smem] * 2 + [vmem] * 7, out_specs=[...  2.36 us
  transfers between devices with their start and end apart: 3, of which 1 were waited for; matrix products, arithmetic and copies ran while one was open for 0% of the time, Pallas kernels for 9%

profile of v6, /device:TPU:1, one launch (start us, length us, event | category | flops | bytes accessed | tf_op | source)
XLA Modules:
  0.0 86.6 jit_solution(5077798493728987784)
XLA Ops:
  0.7 1.0 %copy-done.3 = bf16[128,768]{1,0:T(8,128)(2,1)S(1)} copy-done((bf16[128,768]{1,0:T(8,128)(2,1)S(1)}, bf16[128,768]{1,0:T(8,128)(2,1)}, u32[]{:S(2)}) %copy-start.3) | copy-done | bytes 196632
  1.8 17.4 %all_to_all.20 = bf16[8,64,768]{2,1,0:T(8,128)(2,1)S(1)} all-to-all(bf16[8,64,768]{2,1,0:T(8,128)(2,1)S(1)} %fan.1), channel_id=1, replica_groups=mesh['xl'=2,'y'=4,'zh'=4,'zl'=2,'xh'=2,'c'=2] {'xl','y'}, dimensions={0} | all-to-all | bytes 1572864 | tf_op jit(solution)/shard_map/all_to_all | solution.py:473
  19.1 0.4 multiply_reduce_fusion
  19.5 2.5 %collective-permute-start = (bf16[512,768]{1,0:T(8,128)(2,1)S(1)}, bf16[512,768]{1,0:T(8,128)(2,1)S(1)}, u32[]{:S(2)}, u32[]{:S(2)}) collective-permute-start(bf16[512,768]{1,0:T(8,128)(2,1)S(1)} %bitcast.6), channel_id=1, source_target_pairs={{0,1},{1,0},{2,3},{3,2},{4,5},{5,4},{6,7},{7,6},{8,9},{9,8},{10,11... | collective-permute-start | bytes 2359304 | tf_op jit(solution)/shard_map/ppermute | solution.py:464
  22.0 0.6 split_weights.1
  22.6 3.0 %terms.2 = (f32[32,88,128]{2,1,0:T(8,128)S(1)}, bf16[512,1024]{1,0:T(8,128)(2,1)S(1)}) custom-call(bf16[512,768]{1,0:T(8,128)(2,1)S(1)} %bitcast.7, bf16[1024,768]{1,0:T(8,128)(2,1)S(1)} %copy-done.1, f32[1,1024]{1,0:T(1,128)S(1)} %bitcast.10, bf16[3072,512]{1,0:T(8,128)(2,1)S(1)} %get-tuple-element.16.w_ref, f32[64,256]{1,0:T(8,128)S(1)} %get-tuple-element.17.e_ref.eig_ref), custom_call_target="tpu_custom_call" | custom-call | flops 24159191040 | bytes 6291456 | tf_op jit(solution)/shard_map/terms/pallas_call | solution.py:150
  25.6 0.1 collective-permute-start.1
  25.7 3.0 %terms.3 = (f32[32,88,128]{2,1,0:T(8,128)S(1)}, bf16[512,1024]{1,0:T(8,128)(2,1)S(1)}) custom-call(bf16[512,768]{1,0:T(8,128)(2,1)S(1)} %collective-permute-done.rows_ref, bf16[1024,768]{1,0:T(8,128)(2,1)S(1)} %copy-done.1, f32[1,1024]{1,0:T(1,128)S(1)} %bitcast.11, bf16[3072,512]{1,0:T(8,128)(2,1)S(1)} %get-tuple-element.16.w_ref, ...), custom_call_target="tpu_custom_call" | custom-call | flops 24159191040 | bytes 6291456 | tf_op jit(solution)/shard_map/terms/pallas_call | solution.py:150
  28.7 0.2 collective-permute-done.1.b_ref
  28.9 0.4 code.1
  29.3 0.1 convert_element_type.25
  29.4 19.0 %all_to_all.21 = f16[32,88,128]{2,1,0:T(8,128)(2,1)S(1)} all-to-all(f16[32,88,128]{2,1,0:T(8,128)(2,1)S(1)} %convert_element_type.25), channel_id=1, replica_groups=mesh['xl'=2,'y'=4,'zh'=4,'zl'=2,'xh'=2,'c'=2] {'xl','y','xh','zl'}, dimensions={0} | all-to-all | bytes 1441792 | tf_op jit(solution)/shard_map/all_to_all | solution.py:482
  48.4 0.1 convert_element_type.26.x_ref
  48.5 0.3 recode.1
  48.9 14.1 %all_to_all.22 = f16[4,88,128]{2,1,0:T(8,128)(2,1)S(1)} all-to-all(f16[4,88,128]{2,1,0:T(8,128)(2,1)S(1)} %broadcast_in_dim.4), channel_id=1, replica_groups=mesh['xl'=2,'y'=4,'zh'=4,'zl'=2,'xh'=2,'c'=2] {'zh'}, dimensions={0} | all-to-all | bytes 180224 | tf_op jit(solution)/shard_map/all_to_all | solution.py:485
  63.1 0.4 pack.1
  63.4 0.1 convert_element_type.29
  63.6 14.2 %all_to_all.23 = f16[32,88,128]{2,1,0:T(8,128)(2,1)S(1)} all-to-all(f16[32,88,128]{2,1,0:T(8,128)(2,1)S(1)} %convert_element_type.29), channel_id=1, replica_groups=mesh['xl'=2,'y'=4,'zh'=4,'zl'=2,'xh'=2,'c'=2] {'xl','y','xh','zl'}, dimensions={0} | all-to-all | bytes 1441792 | tf_op jit(solution)/shard_map/all_to_all | solution.py:488
  77.8 4.4 %collective-permute-start.2 = (f16[32,88,128]{2,1,0:T(8,128)(2,1)S(1)}, f16[32,88,128]{2,1,0:T(8,128)(2,1)S(1)}, u32[]{:S(2)}, u32[]{:S(2)}) collective-permute-start(f16[32,88,128]{2,1,0:T(8,128)(2,1)S(1)} %all_to_all.23), channel_id=1, source_target_pairs={{0,1},{1,0},{2,3},{3,2},{4,5},{5,4},{6,7},{7,6},{8,9},{9,8},{10,11... | collective-permute-start | bytes 2162696 | tf_op jit(solution)/shard_map/ppermute | solution.py:464
  82.9 0.1 pad_maximum_fusion
  83.0 0.1 convert_element_type.31.got_ref
  83.1 1.1 %half_step.1 = (f32[64,512]{1,0:T(8,128)S(1)}, f32[1024,512]{1,0:T(8,128)S(1)}) custom-call(s32[1]{0:T(128)} %bitcast.core_ref, s32[1]{0:T(128)} %bitcast.1.blk_ref, bf16[512,1024]{1,0:T(8,128)(2,1)S(1)} %get-tuple-element.21.kern_ref, f32[32,88,128]{2,1,0:T(8,128)S(1)} %convert_element_type.31.got_ref, f32[64,256]{1,0:T(8,128)S(1)} %get-tuple-element.17.e_ref.eig_ref, ...), custom_call_target="tpu_custom_call" | custom-call | flops 5368709120 | bytes 4194304 | tf_op jit(solution)/shard_map/half_step/pallas_call | solution.py:357
  84.1 0.1 convert_element_type.30.got_ref
  84.2 2.4 %take_step.1 = (f32[128,512]{1,0:T(8,128)}, f32[1024,512]{1,0:T(8,128)}) custom-call(s32[1]{0:T(128)} %bitcast.core_ref, s32[1]{0:T(128)} %bitcast.1.blk_ref, bf16[512,1024]{1,0:T(8,128)(2,1)S(1)} %get-tuple-element.18.kern_ref, f32[32,88,128]{2,1,0:T(8,128)S(1)} %convert_element_type.30.got_ref, f32[64,256]{1,0:T(8,128)S(1)} %get-tuple-element.17.e_ref.eig_ref, ...), custom_call_target="tpu_custom_call" | custom-call | flops 536870912 | bytes 8388608 | tf_op jit(solution)/shard_map/take_step/pallas_call | solution.py:436
  (18 shorter events, 0.1 us)
Async XLA Ops:
  0.6 18.5 %copy-start.1 = (bf16[1024,768]{1,0:T(8,128)(2,1)S(1)}, bf16[1024,768]{1,0:T(8,128)(2,1)}, u32[]{:S(2)}) copy-start(bf16[1024,768]{1,0:T(8,128)(2,1)} %cen_ref.1) | copy-start | bytes 4718596
  0.7 1.0 %copy-start.3 = (bf16[128,768]{1,0:T(8,128)(2,1)S(1)}, bf16[128,768]{1,0:T(8,128)(2,1)}, u32[]{:S(2)}) copy-start(bf16[128,768]{1,0:T(8,128)(2,1)} %rows_ref.1) | copy-start | bytes 589828
  1.7 20.3 %copy-start = (f32[1024,512]{1,0:T(8,128)S(1)}, f32[1024,512]{1,0:T(8,128)}, u32[]{:S(2)}) copy-start(f32[1024,512]{1,0:T(8,128)} %w_ref.2) | copy-start | bytes 6291460
  1.8 20.3 %copy-start.4 = (f32[64,160]{1,0:T(8,128)S(1)}, f32[64,160]{1,0:T(8,128)}, u32[]{:S(2)}) copy-start(f32[64,160]{1,0:T(8,128)} %e_ref.1) | copy-start | bytes 122884
  19.5 6.2 %collective-permute-start = (bf16[512,768]{1,0:T(8,128)(2,1)S(1)}, bf16[512,768]{1,0:T(8,128)(2,1)S(1)}, u32[]{:S(2)}, u32[]{:S(2)}) collective-permute-start(bf16[512,768]{1,0:T(8,128)(2,1)S(1)} %bitcast.6), channel_id=1, source_target_pairs={{0,1},{1,0},{2,3},{3,2},{4,5},{5,4},{6,7},{7,6},{8,9},{9,8},{10,11... | collective-permute-start | bytes 2359304 | tf_op jit(solution)/shard_map/ppermute | solution.py:464
  25.6 3.3 %collective-permute-start.1 = (f32[32,88,128]{2,1,0:T(8,128)S(1)}, f32[32,88,128]{2,1,0:T(8,128)S(1)}, u32[]{:S(2)}, u32[]{:S(2)}) collective-permute-start(f32[32,88,128]{2,1,0:T(8,128)S(1)} %get-tuple-element.20), channel_id=1, source_target_pairs={{0,1},{1,0},{2,3},{3,2},{4,5},{5,4},{6,7},{7,6},{8,9},{9,8},{10,11... | collective-permute-start | bytes 4325384 | tf_op jit(solution)/shard_map/ppermute | solution.py:464
  48.5 14.5 %copy-start.2 = (f32[128,512]{1,0:T(8,128)S(1)}, f32[128,512]{1,0:T(8,128)}, u32[]{:S(2)}) copy-start(f32[128,512]{1,0:T(8,128)} %targets_ref.5) | copy-start | bytes 786436
  63.4 19.5 %copy-start.5 = (f32[160]{0:T(256)S(1)}, f32[160]{0:T(256)}, u32[]{:S(2)}) copy-start(f32[160]{0:T(256)} %param.12) | copy-start | bytes 1924
  77.8 6.3 %collective-permute-start.2 = (f16[32,88,128]{2,1,0:T(8,128)(2,1)S(1)}, f16[32,88,128]{2,1,0:T(8,128)(2,1)S(1)}, u32[]{:S(2)}, u32[]{:S(2)}) collective-permute-start(f16[32,88,128]{2,1,0:T(8,128)(2,1)S(1)} %all_to_all.23), channel_id=1, source_target_pairs={{0,1},{1,0},{2,3},{3,2},{4,5},{5,4},{6,7},{7,6},{8,9},{9,8},{10,11... | collective-permute-start | bytes 2162696 | tf_op jit(solution)/shard_map/ppermute | solution.py:464

commit v7 on v6

--- a/solution.py
+++ b/solution.py
@@ -85,30 +85,7 @@
     )(core, sub, blk, batch)
 
 
-def weights_kernel(w_ref, e_ref, out_ref, e_out):
-    count = w_ref.shape[0]
-    e_out[...] = widen(e_ref[...])
-    high, low = split(w_ref[...])
-    out_ref[:count] = high
-    out_ref[count : 2 * count] = low
-    out_ref[2 * count :] = high
-
-
-def split_weights(weights, eig):
-    count, c_dim = weights.shape
-    return pl.pallas_call(
-        weights_kernel,
-        out_shape=(
-            jax.ShapeDtypeStruct((3 * count, c_dim), BF16),
-            jax.ShapeDtypeStruct((HALF, 2 * LANES), F32),
-        ),
-        compiler_params=params(12),
-        cost_estimate=pl.CostEstimate(flops=0, bytes_accessed=5 << 20, transcendentals=0),
-        name="split_weights",
-    )(weights, eig)
-
-
-def terms_kernel(rows_ref, cen_ref, cs_ref, w_ref, e_ref, out_ref, kern_ref, kern3):
+def terms_body(rows_ref, cen_ref, cs_ref, eig, weights3, out_ref, kern_ref, kern3):
     n, d = rows_ref.shape
     count = cen_ref.shape[0]
     tile = 512
@@ -126,7 +103,7 @@
         kern_ref[:, cols] = high
         kern3[:, 2 * count + at : 2 * count + at + tile] = low
         if at == 0:
-            coef = dot3(kern[:, :HALF], e_ref[...], NN)
+            coef = dot3(kern[:, :HALF], eig, NN)
             group = lane_group((8, LANES))
             for b in range(SUBS):
                 block = coef[b * SUB : (b + 1) * SUB]
@@ -135,7 +112,7 @@
                 out_ref[b, MAIN:CODED, :] = jnp.where(
                     group == 0, tail[:8], jnp.where(group == 1, tail[8:], 0.0)
                 )
-    value = lax.dot_general(kern3[...], w_ref[...], NN, preferred_element_type=F32)
+    value = lax.dot_general(kern3[...], weights3(), NN, preferred_element_type=F32)
     for b in range(SUBS):
         for j in range(4):
             out_ref[b, j * SUB : (j + 1) * SUB, :] = value[
@@ -143,23 +120,45 @@
             ]
 
 
-def terms(rows, centers, cs, weights3, eig):
+def first_kernel(rows_ref, cen_ref, cs_ref, w_ref, e_ref, out_ref, kern_ref, w3_ref, e_out, kern3):
+    eig = widen(e_ref[...])
+    e_out[...] = eig
+
+    def weights3():
+        count = w_ref.shape[0]
+        high, low = split(w_ref[...])
+        w3_ref[:count] = high
+        w3_ref[count : 2 * count] = low
+        w3_ref[2 * count :] = high
+        return w3_ref[...]
+
+    terms_body(rows_ref, cen_ref, cs_ref, eig, weights3, out_ref, kern_ref, kern3)
+
+
+def second_kernel(rows_ref, cen_ref, cs_ref, w3_ref, e_ref, out_ref, kern_ref, kern3):
+    terms_body(
+        rows_ref, cen_ref, cs_ref, e_ref[...], lambda: w3_ref[...], out_ref, kern_ref, kern3
+    )
+
+
+def terms(kernel, rows, centers, cs, weights, eig, extra=()):
     n, d = rows.shape
     count = centers.shape[0]
-    c_dim = weights3.shape[1]
-    return pl.pallas_call(
-        terms_kernel,
+    c_dim = weights.shape[1]
+    return pl.pallas_call(
+        kernel,
         out_shape=(
             jax.ShapeDtypeStruct((SUBS, CODED, LANES), F32),
             jax.ShapeDtypeStruct((n, count), BF16),
-        ),
+        )
+        + extra,
         scratch_shapes=[pltpu.VMEM((n, 3 * count), BF16)],
         compiler_params=params(24),
         cost_estimate=pl.CostEstimate(
             flops=20 * n * count * (d + 3 * c_dim), bytes_accessed=6 << 20, transcendentals=n * count
         ),
         name="terms",
-    )(rows, centers, cs, weights3, eig)
+    )(rows, centers, cs, weights, eig)
 
 
 def scaled(part):
@@ -474,9 +473,15 @@
     first, held, to_split = lax.optimization_barrier((first, centers, weights))
     second = swap_cores(first)
     cs = sq_norm(held)[None, :]
-    weights3, eig = split_weights(to_split, eigvec)
-    sent, kern_first = terms(first, held, cs, weights3, eig)
-    kept, kern_second = terms(second, held, cs, weights3, eig)
+    count, c_dim = weights.shape
+    extra = (
+        jax.ShapeDtypeStruct((3 * count, c_dim), BF16),
+        jax.ShapeDtypeStruct((HALF, 2 * LANES), F32),
+    )
+    sent, kern_first, weights3, eig = terms(
+        first_kernel, first, held, cs, to_split, eigvec, extra
+    )
+    kept, kern_second = terms(second_kernel, second, held, cs, weights3, eig)
     coded = code(kept, swap_cores(sent)).astype(F16)
 
     got = lax.all_to_all(coded, NEAR, 0, 0, tiled=True).astype(F32)

time: 86.9 us -> 86.3 us (level)
    pallas_call x3 -> x2, Pallas kernels: 6.55 us -> 5.95 us  [terms(): pl.pallas_call(kernel, out_shape=(jax.ShapeDtypeStruct((SUBS, CODED, LANE...]
  transfers between devices with their start and end apart: 3 -> 3, of which waited for: 1 -> 1; matrix products, arithmetic and copies ran while one was open for 0% -> 0% of each run, Pallas kernels for 9% -> 8%
where the time goes in v7:
time: 86.3 us; the launch traced here: 86 us
  blocking collectives  64.7 us (75%)
  Pallas kernels  10.5 us (12%)
  starting transfers between devices  7.06 us (8%)
  between operations  1.48 us (2%)
  local copies, waits for them, and re-layouts  1.08 us (1%)
  other arithmetic  0.95 us (1%)
    all_to_all x1, blocking collectives, local(): got = lax.all_to_all(coded, NEAR, 0, 0, tiled=True).astype(F32)  19 us
    all_to_all x1, blocking collectives, local(): lax.all_to_all(fan(core, sub, blk, batch), BLK, 0, 0, tiled=True)  17.4 us
    all_to_all x1, blocking collectives, local(): got_second = lax.all_to_all(packed, NEAR, 0, 0, tiled=True)  14.2 us
    all_to_all x1, blocking collectives, local(): far = lax.all_to_all(partial, FAR, 0, 0, tiled=True).astype(F32)  14.1 us
    ppermute x3, starting transfers between devices, swap_cores(): return lax.ppermute(value, 'c', [(0, 1), (1, 0)])  7.06 us
    pallas_call x2, Pallas kernels, terms(): pl.pallas_call(kernel, out_shape=(jax.ShapeDtypeStruct((SUBS, CODED, LANE...  5.95 us
    pallas_call x1, Pallas kernels, take_step(): pl.pallas_call(step_kernel, in_specs=[smem] * 2 + [vmem] * 7, out_specs=[...  2.36 us
  transfers between devices with their start and end apart: 3, of which 1 were waited for; matrix products, arithmetic and copies ran while one was open for 0% of the time, Pallas kernels for 8%

profile of v7, /device:TPU:1, one launch (start us, length us, event | category | flops | bytes accessed | tf_op | source)
XLA Modules:
  0.0 86.0 jit_solution(10958155156473243780)
XLA Ops:
  0.7 1.0 %copy-done.2 = bf16[128,768]{1,0:T(8,128)(2,1)S(1)} copy-done((bf16[128,768]{1,0:T(8,128)(2,1)S(1)}, bf16[128,768]{1,0:T(8,128)(2,1)}, u32[]{:S(2)}) %copy-start.2) | copy-done | bytes 196632
  1.7 0.1 fan.1
  1.8 17.4 %all_to_all.20 = bf16[8,64,768]{2,1,0:T(8,128)(2,1)S(1)} all-to-all(bf16[8,64,768]{2,1,0:T(8,128)(2,1)S(1)} %fan.1), channel_id=1, replica_groups=mesh['xl'=2,'y'=4,'zh'=4,'zl'=2,'xh'=2,'c'=2] {'xl','y'}, dimensions={0} | all-to-all | bytes 1572864 | tf_op jit(solution)/shard_map/all_to_all | solution.py:472
  19.1 0.4 multiply_reduce_fusion
  19.5 2.5 %collective-permute-start = (bf16[512,768]{1,0:T(8,128)(2,1)S(1)}, bf16[512,768]{1,0:T(8,128)(2,1)S(1)}, u32[]{:S(2)}, u32[]{:S(2)}) collective-permute-start(bf16[512,768]{1,0:T(8,128)(2,1)S(1)} %bitcast.6), channel_id=1, source_target_pairs={{0,1},{1,0},{2,3},{3,2},{4,5},{5,4},{6,7},{7,6},{8,9},{9,8},{10,11... | collective-permute-start | bytes 2359304 | tf_op jit(solution)/shard_map/ppermute | solution.py:463
  22.0 3.0 %terms.2 = (f32[32,88,128]{2,1,0:T(8,128)S(1)}, bf16[512,1024]{1,0:T(8,128)(2,1)S(1)}, bf16[3072,512]{1,0:T(8,128)(2,1)S(1)}, f32[64,256]{1,0:T(8,128)S(1)}) custom-call(bf16[512,768]{1,0:T(8,128)(2,1)S(1)} %bitcast.7, bf16[1024,768]{1,0:T(8,128)(2,1)S(1)} %copy-done, f32[1,1024]{1,0:T(1,128)S(1)} %bitcast.10, f32[1024,512]{1,0:T(8,128)S(1)} %copy-done.3, ...), custom_call_target="tpu_custom_call" | custom-call | flops 24159191040 | bytes 6291456 | tf_op jit(solution)/shard_map/terms/pallas_call | solution.py:148
  25.0 0.1 collective-permute-start.1
  25.2 2.9 %terms.3 = (f32[32,88,128]{2,1,0:T(8,128)S(1)}, bf16[512,1024]{1,0:T(8,128)(2,1)S(1)}) custom-call(bf16[512,768]{1,0:T(8,128)(2,1)S(1)} %collective-permute-done.rows_ref, bf16[1024,768]{1,0:T(8,128)(2,1)S(1)} %copy-done, f32[1,1024]{1,0:T(1,128)S(1)} %bitcast.11, bf16[3072,512]{1,0:T(8,128)(2,1)S(1)} %get-tuple-element.17.w3_ref, ...), custom_call_target="tpu_custom_call" | custom-call | flops 24159191040 | bytes 6291456 | tf_op jit(solution)/shard_map/terms/pallas_call | solution.py:148
  28.1 0.2 collective-permute-done.1.b_ref
  28.3 0.4 code.1
  28.7 0.1 convert_element_type.25
  28.8 19.0 %all_to_all.21 = f16[32,88,128]{2,1,0:T(8,128)(2,1)S(1)} all-to-all(f16[32,88,128]{2,1,0:T(8,128)(2,1)S(1)} %convert_element_type.25), channel_id=1, replica_groups=mesh['xl'=2,'y'=4,'zh'=4,'zl'=2,'xh'=2,'c'=2] {'xl','y','xh','zl'}, dimensions={0} | all-to-all | bytes 1441792 | tf_op jit(solution)/shard_map/all_to_all | solution.py:487
  47.9 0.1 convert_element_type.26.x_ref
  48.0 0.3 recode.1
  48.4 14.1 %all_to_all.22 = f16[4,88,128]{2,1,0:T(8,128)(2,1)S(1)} all-to-all(f16[4,88,128]{2,1,0:T(8,128)(2,1)S(1)} %broadcast_in_dim.4), channel_id=1, replica_groups=mesh['xl'=2,'y'=4,'zh'=4,'zl'=2,'xh'=2,'c'=2] {'zh'}, dimensions={0} | all-to-all | bytes 180224 | tf_op jit(solution)/shard_map/all_to_all | solution.py:490
  62.5 0.4 pack.1
  62.9 0.1 convert_element_type.29
  63.0 14.2 %all_to_all.23 = f16[32,88,128]{2,1,0:T(8,128)(2,1)S(1)} all-to-all(f16[32,88,128]{2,1,0:T(8,128)(2,1)S(1)} %convert_element_type.29), channel_id=1, replica_groups=mesh['xl'=2,'y'=4,'zh'=4,'zl'=2,'xh'=2,'c'=2] {'xl','y','xh','zl'}, dimensions={0} | all-to-all | bytes 1441792 | tf_op jit(solution)/shard_map/all_to_all | solution.py:493
  77.2 4.4 %collective-permute-start.2 = (f16[32,88,128]{2,1,0:T(8,128)(2,1)S(1)}, f16[32,88,128]{2,1,0:T(8,128)(2,1)S(1)}, u32[]{:S(2)}, u32[]{:S(2)}) collective-permute-start(f16[32,88,128]{2,1,0:T(8,128)(2,1)S(1)} %all_to_all.23), channel_id=1, source_target_pairs={{0,1},{1,0},{2,3},{3,2},{4,5},{5,4},{6,7},{7,6},{8,9},{9,8},{10,11... | collective-permute-start | bytes 2162696 | tf_op jit(solution)/shard_map/ppermute | solution.py:463
  82.3 0.1 pad_maximum_fusion
  82.4 0.1 convert_element_type.31.got_ref
  82.5 1.0 %half_step.1 = (f32[64,512]{1,0:T(8,128)S(1)}, f32[1024,512]{1,0:T(8,128)S(1)}) custom-call(s32[1]{0:T(128)} %bitcast.core_ref, s32[1]{0:T(128)} %bitcast.1.blk_ref, bf16[512,1024]{1,0:T(8,128)(2,1)S(1)} %get-tuple-element.21.kern_ref, f32[32,88,128]{2,1,0:T(8,128)S(1)} %convert_element_type.31.got_ref, f32[64,256]{1,0:T(8,128)S(1)} %get-tuple-element.18.e_ref.eig_ref, ...), custom_call_target="tpu_custom_call" | custom-call | flops 5368709120 | bytes 4194304 | tf_op jit(solution)/shard_map/half_step/pallas_call | solution.py:356
  83.6 0.1 convert_element_type.30.got_ref
  83.7 2.4 %take_step.1 = (f32[128,512]{1,0:T(8,128)}, f32[1024,512]{1,0:T(8,128)}) custom-call(s32[1]{0:T(128)} %bitcast.core_ref, s32[1]{0:T(128)} %bitcast.1.blk_ref, bf16[512,1024]{1,0:T(8,128)(2,1)S(1)} %get-tuple-element.16.kern_ref, f32[32,88,128]{2,1,0:T(8,128)S(1)} %convert_element_type.30.got_ref, f32[64,256]{1,0:T(8,128)S(1)} %get-tuple-element.18.e_ref.eig_ref, ...), custom_call_target="tpu_custom_call" | custom-call | flops 536870912 | bytes 8388608 | tf_op jit(solution)/shard_map/take_step/pallas_call | solution.py:435
  (17 shorter events, 0.1 us)
Async XLA Ops:
  0.6 18.5 %copy-start = (bf16[1024,768]{1,0:T(8,128)(2,1)S(1)}, bf16[1024,768]{1,0:T(8,128)(2,1)}, u32[]{:S(2)}) copy-start(bf16[1024,768]{1,0:T(8,128)(2,1)} %cen_ref.1) | copy-start | bytes 4718596
  0.7 1.0 %copy-start.2 = (bf16[128,768]{1,0:T(8,128)(2,1)S(1)}, bf16[128,768]{1,0:T(8,128)(2,1)}, u32[]{:S(2)}) copy-start(bf16[128,768]{1,0:T(8,128)(2,1)} %rows_ref.1) | copy-start | bytes 589828
  1.7 20.3 %copy-start.3 = (f32[1024,512]{1,0:T(8,128)S(1)}, f32[1024,512]{1,0:T(8,128)}, u32[]{:S(2)}) copy-start(f32[1024,512]{1,0:T(8,128)} %w_ref.2) | copy-start | bytes 6291460
  1.8 20.3 %copy-start.4 = (f32[64,160]{1,0:T(8,128)S(1)}, f32[64,160]{1,0:T(8,128)}, u32[]{:S(2)}) copy-start(f32[64,160]{1,0:T(8,128)} %e_ref.1) | copy-start | bytes 122884
  19.5 5.6 %collective-permute-start = (bf16[512,768]{1,0:T(8,128)(2,1)S(1)}, bf16[512,768]{1,0:T(8,128)(2,1)S(1)}, u32[]{:S(2)}, u32[]{:S(2)}) collective-permute-start(bf16[512,768]{1,0:T(8,128)(2,1)S(1)} %bitcast.6), channel_id=1, source_target_pairs={{0,1},{1,0},{2,3},{3,2},{4,5},{5,4},{6,7},{7,6},{8,9},{9,8},{10,11... | collective-permute-start | bytes 2359304 | tf_op jit(solution)/shard_map/ppermute | solution.py:463
  25.0 3.3 %collective-permute-start.1 = (f32[32,88,128]{2,1,0:T(8,128)S(1)}, f32[32,88,128]{2,1,0:T(8,128)S(1)}, u32[]{:S(2)}, u32[]{:S(2)}) collective-permute-start(f32[32,88,128]{2,1,0:T(8,128)S(1)} %get-tuple-element.20), channel_id=1, source_target_pairs={{0,1},{1,0},{2,3},{3,2},{4,5},{5,4},{6,7},{7,6},{8,9},{9,8},{10,11... | collective-permute-start | bytes 4325384 | tf_op jit(solution)/shard_map/ppermute | solution.py:463
  48.0 14.5 %copy-start.1 = (f32[128,512]{1,0:T(8,128)S(1)}, f32[128,512]{1,0:T(8,128)}, u32[]{:S(2)}) copy-start(f32[128,512]{1,0:T(8,128)} %targets_ref.5) | copy-start | bytes 786436
  62.9 19.4 %copy-start.5 = (f32[160]{0:T(256)S(1)}, f32[160]{0:T(256)}, u32[]{:S(2)}) copy-start(f32[160]{0:T(256)} %param.12) | copy-start | bytes 1924
  77.2 6.3 %collective-permute-start.2 = (f16[32,88,128]{2,1,0:T(8,128)(2,1)S(1)}, f16[32,88,128]{2,1,0:T(8,128)(2,1)S(1)}, u32[]{:S(2)}, u32[]{:S(2)}) collective-permute-start(f16[32,88,128]{2,1,0:T(8,128)(2,1)S(1)} %all_to_all.23), channel_id=1, source_target_pairs={{0,1},{1,0},{2,3},{3,2},{4,5},{5,4},{6,7},{7,6},{8,9},{9,8},{10,11... | collective-permute-start | bytes 2162696 | tf_op jit(solution)/shard_map/ppermute | solution.py:463

commit v8 on v7

--- a/solution.py
+++ b/solution.py
@@ -10,7 +10,7 @@
 AXES = ("xl", "y", "zh", "zl", "xh", "c")
 BLK = ("xl", "y")
 SUB_AXES = ("xh", "zl")
-NEAR = BLK + SUB_AXES
+NEAR = ("xh", "xl", "zl", "y")
 FAR = "zh"
 ALL = P(AXES, None)
 F32 = jnp.float32
@@ -30,6 +30,10 @@
 MAIN = VALUE + SUB
 CODED = MAIN + 8
 FAR_SIZE = 4
+
+
+def slot(blk, sub):
+    return sub // 2 * 16 + blk // 4 * 8 + sub % 2 * 4 + blk % 4
 
 
 def params(mib):
@@ -107,15 +111,17 @@
             group = lane_group((8, LANES))
             for b in range(SUBS):
                 block = coef[b * SUB : (b + 1) * SUB]
-                out_ref[b, VALUE:MAIN, :] = block[:, :LANES]
+                at_b = slot(b // PER_BLOCK, b % PER_BLOCK)
+                out_ref[at_b, VALUE:MAIN, :] = block[:, :LANES]
                 tail = block[:, LANES:]
-                out_ref[b, MAIN:CODED, :] = jnp.where(
+                out_ref[at_b, MAIN:CODED, :] = jnp.where(
                     group == 0, tail[:8], jnp.where(group == 1, tail[8:], 0.0)
                 )
     value = lax.dot_general(kern3[...], weights3(), NN, preferred_element_type=F32)
     for b in range(SUBS):
+        at_b = slot(b // PER_BLOCK, b % PER_BLOCK)
         for j in range(4):
-            out_ref[b, j * SUB : (j + 1) * SUB, :] = value[
+            out_ref[at_b, j * SUB : (j + 1) * SUB, :] = value[
                 b * SUB : (b + 1) * SUB, j * LANES : (j + 1) * LANES
             ]
 
@@ -249,7 +255,7 @@
         out_ref[b, MAIN:CODED, :] = tile
     _, tile = with_powers(coef, value_power, coef_power)
     for h in range(PER_BLOCK):
-        b = blk_ref[0] * PER_BLOCK + h
+        b = slot(blk_ref[0], h)
         out_ref[b, :VALUE, :] = value
         out_ref[b, MAIN:CODED, :] = tile
 
@@ -273,22 +279,24 @@
     group = lane_group((8, LANES))
     coefs = []
     for b in range(SUBS):
-        value_scale, coef_scale = unscale(got_ref, b)
+        at_b = slot(b // PER_BLOCK, b % PER_BLOCK)
+        value_scale, coef_scale = unscale(got_ref, at_b)
         for j in range(4):
             resid[b * SUB : (b + 1) * SUB, j * LANES : (j + 1) * LANES] = (
-                got_ref[b, j * SUB : (j + 1) * SUB, :] * value_scale
+                got_ref[at_b, j * SUB : (j + 1) * SUB, :] * value_scale
             ).astype(BF16)
-        main = got_ref[b, VALUE:MAIN, :] * coef_scale
-        tile_rows = got_ref[b, MAIN:CODED, :] * coef_scale
+        main = got_ref[at_b, VALUE:MAIN, :] * coef_scale
+        tile_rows = got_ref[at_b, MAIN:CODED, :] * coef_scale
         tails = [jnp.where(group == t, tile_rows, 0.0) for t in range(2)]
         coefs.append(jnp.concatenate([main, jnp.concatenate(tails, axis=0)], axis=1).astype(BF16))
     for h in range(PER_BLOCK):
         b = blk * PER_BLOCK + h
-        value_scale, _ = unscale(got_ref, b)
+        at_b = slot(blk, h)
+        value_scale, _ = unscale(got_ref, at_b)
         row = pl.multiple_of(half * HALF + h * SUB, SUB)
         for j in range(4):
             lanes = slice(j * LANES, (j + 1) * LANES)
-            value = got_ref[b, j * SUB : (j + 1) * SUB, :] * value_scale
+            value = got_ref[at_b, j * SUB : (j + 1) * SUB, :] * value_scale
             pred_ref[h * SUB : (h + 1) * SUB, lanes] = value
             target = targets_ref[pl.ds(row, SUB), lanes]
             resid[pl.ds(pl.multiple_of(b * SUB, SUB), SUB), lanes] = (value - target).astype(BF16)

time: 86.3 us -> 85.3 us (0.988)
  blocking collectives: 64.7 us -> 63.8 us
    all_to_all x1, blocking collectives: 19 us -> 18 us  [local(): got = lax.all_to_all(coded, NEAR, 0, 0, tiled=True).astype(F32)]
where the time goes in v8:
time: 85.3 us; the launch traced here: 85 us
  blocking collectives  63.8 us (75%)
  Pallas kernels  10.5 us (12%)
  starting transfers between devices  6.97 us (8%)
  between operations  1.48 us (2%)
  local copies, waits for them, and re-layouts  1.08 us (1%)
  other arithmetic  0.95 us (1%)
    all_to_all x1, blocking collectives, local(): got = lax.all_to_all(coded, NEAR, 0, 0, tiled=True).astype(F32)  18 us
    all_to_all x1, blocking collectives, local(): lax.all_to_all(fan(core, sub, blk, batch), BLK, 0, 0, tiled=True)  17.4 us
    all_to_all x1, blocking collectives, local(): got_second = lax.all_to_all(packed, NEAR, 0, 0, tiled=True)  14.3 us
    all_to_all x1, blocking collectives, local(): far = lax.all_to_all(partial, FAR, 0, 0, tiled=True).astype(F32)  14.1 us
    ppermute x3, starting transfers between devices, swap_cores(): return lax.ppermute(value, 'c', [(0, 1), (1, 0)])  6.97 us
    pallas_call x2, Pallas kernels, terms(): pl.pallas_call(kernel, out_shape=(jax.ShapeDtypeStruct((SUBS, CODED, LANE...  5.95 us
    pallas_call x1, Pallas kernels, take_step(): pl.pallas_call(step_kernel, in_specs=[smem] * 2 + [vmem] * 7, out_specs=[...  2.37 us
  transfers between devices with their start and end apart: 3, of which 1 were waited for; matrix products, arithmetic and copies ran while one was open for 0% of the time, Pallas kernels for 8%

profile of v8, /device:TPU:1, one launch (start us, length us, event | category | flops | bytes accessed | tf_op | source)
XLA Modules:
  0.0 85.0 jit_solution(12442149828600918079)
XLA Ops:
  0.7 1.0 %copy-done.2 = bf16[128,768]{1,0:T(8,128)(2,1)S(1)} copy-done((bf16[128,768]{1,0:T(8,128)(2,1)S(1)}, bf16[128,768]{1,0:T(8,128)(2,1)}, u32[]{:S(2)}) %copy-start.2) | copy-done | bytes 196632
  1.7 0.1 fan.1
  1.8 17.4 %all_to_all.20 = bf16[8,64,768]{2,1,0:T(8,128)(2,1)S(1)} all-to-all(bf16[8,64,768]{2,1,0:T(8,128)(2,1)S(1)} %fan.1), channel_id=1, replica_groups=mesh['xl'=2,'y'=4,'zh'=4,'zl'=2,'xh'=2,'c'=2] {'xl','y'}, dimensions={0} | all-to-all | bytes 1572864 | tf_op jit(solution)/shard_map/all_to_all | solution.py:480
  19.1 0.4 multiply_reduce_fusion
  19.5 2.5 %collective-permute-start = (bf16[512,768]{1,0:T(8,128)(2,1)S(1)}, bf16[512,768]{1,0:T(8,128)(2,1)S(1)}, u32[]{:S(2)}, u32[]{:S(2)}) collective-permute-start(bf16[512,768]{1,0:T(8,128)(2,1)S(1)} %bitcast.6), channel_id=1, source_target_pairs={{0,1},{1,0},{2,3},{3,2},{4,5},{5,4},{6,7},{7,6},{8,9},{9,8},{10,11... | collective-permute-start | bytes 2359304 | tf_op jit(solution)/shard_map/ppermute | solution.py:471
  22.0 3.0 %terms.2 = (f32[32,88,128]{2,1,0:T(8,128)S(1)}, bf16[512,1024]{1,0:T(8,128)(2,1)S(1)}, bf16[3072,512]{1,0:T(8,128)(2,1)S(1)}, f32[64,256]{1,0:T(8,128)S(1)}) custom-call(bf16[512,768]{1,0:T(8,128)(2,1)S(1)} %bitcast.7, bf16[1024,768]{1,0:T(8,128)(2,1)S(1)} %copy-done, f32[1,1024]{1,0:T(1,128)S(1)} %bitcast.10, f32[1024,512]{1,0:T(8,128)S(1)} %copy-done.3, ...), custom_call_target="tpu_custom_call" | custom-call | flops 24159191040 | bytes 6291456 | tf_op jit(solution)/shard_map/terms/pallas_call | solution.py:154
  25.0 0.1 collective-permute-start.1
  25.2 2.9 %terms.3 = (f32[32,88,128]{2,1,0:T(8,128)S(1)}, bf16[512,1024]{1,0:T(8,128)(2,1)S(1)}) custom-call(bf16[512,768]{1,0:T(8,128)(2,1)S(1)} %collective-permute-done.rows_ref, bf16[1024,768]{1,0:T(8,128)(2,1)S(1)} %copy-done, f32[1,1024]{1,0:T(1,128)S(1)} %bitcast.11, bf16[3072,512]{1,0:T(8,128)(2,1)S(1)} %get-tuple-element.17.w3_ref, ...), custom_call_target="tpu_custom_call" | custom-call | flops 24159191040 | bytes 6291456 | tf_op jit(solution)/shard_map/terms/pallas_call | solution.py:154
  28.1 0.2 collective-permute-done.1.b_ref
  28.3 0.4 code.1
  28.7 0.1 convert_element_type.25
  28.8 18.0 %all_to_all.21 = f16[32,88,128]{2,1,0:T(8,128)(2,1)S(1)} all-to-all(f16[32,88,128]{2,1,0:T(8,128)(2,1)S(1)} %convert_element_type.25), channel_id=1, replica_groups=mesh['xl'=2,'y'=4,'zh'=4,'zl'=2,'xh'=2,'c'=2] {'xh','xl','zl','y'}, dimensions={0} | all-to-all | bytes 1441792 | tf_op jit(solution)/shard_map/all_to_all | solution.py:495
  46.9 0.1 convert_element_type.26.x_ref
  47.0 0.3 recode.1
  47.4 14.1 %all_to_all.22 = f16[4,88,128]{2,1,0:T(8,128)(2,1)S(1)} all-to-all(f16[4,88,128]{2,1,0:T(8,128)(2,1)S(1)} %broadcast_in_dim.4), channel_id=1, replica_groups=mesh['xl'=2,'y'=4,'zh'=4,'zl'=2,'xh'=2,'c'=2] {'zh'}, dimensions={0} | all-to-all | bytes 180224 | tf_op jit(solution)/shard_map/all_to_all | solution.py:498
  61.5 0.4 pack.1
  61.9 0.1 convert_element_type.29
  62.0 14.3 %all_to_all.23 = f16[32,88,128]{2,1,0:T(8,128)(2,1)S(1)} all-to-all(f16[32,88,128]{2,1,0:T(8,128)(2,1)S(1)} %convert_element_type.29), channel_id=1, replica_groups=mesh['xl'=2,'y'=4,'zh'=4,'zl'=2,'xh'=2,'c'=2] {'xh','xl','zl','y'}, dimensions={0} | all-to-all | bytes 1441792 | tf_op jit(solution)/shard_map/all_to_all | solution.py:501
  76.3 4.4 %collective-permute-start.2 = (f16[32,88,128]{2,1,0:T(8,128)(2,1)S(1)}, f16[32,88,128]{2,1,0:T(8,128)(2,1)S(1)}, u32[]{:S(2)}, u32[]{:S(2)}) collective-permute-start(f16[32,88,128]{2,1,0:T(8,128)(2,1)S(1)} %all_to_all.23), channel_id=1, source_target_pairs={{0,1},{1,0},{2,3},{3,2},{4,5},{5,4},{6,7},{7,6},{8,9},{9,8},{10,11... | collective-permute-start | bytes 2162696 | tf_op jit(solution)/shard_map/ppermute | solution.py:471
  81.3 0.1 pad_maximum_fusion
  81.4 0.1 convert_element_type.31.got_ref
  81.5 1.0 %half_step.1 = (f32[64,512]{1,0:T(8,128)S(1)}, f32[1024,512]{1,0:T(8,128)S(1)}) custom-call(s32[1]{0:T(128)} %bitcast.core_ref, s32[1]{0:T(128)} %bitcast.1.blk_ref, bf16[512,1024]{1,0:T(8,128)(2,1)S(1)} %get-tuple-element.21.kern_ref, f32[32,88,128]{2,1,0:T(8,128)S(1)} %convert_element_type.31.got_ref, f32[64,256]{1,0:T(8,128)S(1)} %get-tuple-element.18.e_ref.eig_ref, ...), custom_call_target="tpu_custom_call" | custom-call | flops 5368709120 | bytes 4194304 | tf_op jit(solution)/shard_map/half_step/pallas_call | solution.py:364
  82.5 0.1 convert_element_type.30.got_ref
  82.6 2.4 %take_step.1 = (f32[128,512]{1,0:T(8,128)}, f32[1024,512]{1,0:T(8,128)}) custom-call(s32[1]{0:T(128)} %bitcast.core_ref, s32[1]{0:T(128)} %bitcast.1.blk_ref, bf16[512,1024]{1,0:T(8,128)(2,1)S(1)} %get-tuple-element.16.kern_ref, f32[32,88,128]{2,1,0:T(8,128)S(1)} %convert_element_type.30.got_ref, f32[64,256]{1,0:T(8,128)S(1)} %get-tuple-element.18.e_ref.eig_ref, ...), custom_call_target="tpu_custom_call" | custom-call | flops 536870912 | bytes 8388608 | tf_op jit(solution)/shard_map/take_step/pallas_call | solution.py:443
  (17 shorter events, 0.1 us)
Async XLA Ops:
  0.6 18.5 %copy-start = (bf16[1024,768]{1,0:T(8,128)(2,1)S(1)}, bf16[1024,768]{1,0:T(8,128)(2,1)}, u32[]{:S(2)}) copy-start(bf16[1024,768]{1,0:T(8,128)(2,1)} %cen_ref.1) | copy-start | bytes 4718596
  0.7 1.0 %copy-start.2 = (bf16[128,768]{1,0:T(8,128)(2,1)S(1)}, bf16[128,768]{1,0:T(8,128)(2,1)}, u32[]{:S(2)}) copy-start(bf16[128,768]{1,0:T(8,128)(2,1)} %rows_ref.1) | copy-start | bytes 589828
  1.7 20.3 %copy-start.3 = (f32[1024,512]{1,0:T(8,128)S(1)}, f32[1024,512]{1,0:T(8,128)}, u32[]{:S(2)}) copy-start(f32[1024,512]{1,0:T(8,128)} %w_ref.2) | copy-start | bytes 6291460
  1.8 20.3 %copy-start.4 = (f32[64,160]{1,0:T(8,128)S(1)}, f32[64,160]{1,0:T(8,128)}, u32[]{:S(2)}) copy-start(f32[64,160]{1,0:T(8,128)} %e_ref.1) | copy-start | bytes 122884
  19.5 5.6 %collective-permute-start = (bf16[512,768]{1,0:T(8,128)(2,1)S(1)}, bf16[512,768]{1,0:T(8,128)(2,1)S(1)}, u32[]{:S(2)}, u32[]{:S(2)}) collective-permute-start(bf16[512,768]{1,0:T(8,128)(2,1)S(1)} %bitcast.6), channel_id=1, source_target_pairs={{0,1},{1,0},{2,3},{3,2},{4,5},{5,4},{6,7},{7,6},{8,9},{9,8},{10,11... | collective-permute-start | bytes 2359304 | tf_op jit(solution)/shard_map/ppermute | solution.py:471
  25.0 3.3 %collective-permute-start.1 = (f32[32,88,128]{2,1,0:T(8,128)S(1)}, f32[32,88,128]{2,1,0:T(8,128)S(1)}, u32[]{:S(2)}, u32[]{:S(2)}) collective-permute-start(f32[32,88,128]{2,1,0:T(8,128)S(1)} %get-tuple-element.20), channel_id=1, source_target_pairs={{0,1},{1,0},{2,3},{3,2},{4,5},{5,4},{6,7},{7,6},{8,9},{9,8},{10,11... | collective-permute-start | bytes 4325384 | tf_op jit(solution)/shard_map/ppermute | solution.py:471
  47.0 14.5 %copy-start.1 = (f32[128,512]{1,0:T(8,128)S(1)}, f32[128,512]{1,0:T(8,128)}, u32[]{:S(2)}) copy-start(f32[128,512]{1,0:T(8,128)} %targets_ref.5) | copy-start | bytes 786436
  61.9 19.4 %copy-start.5 = (f32[160]{0:T(256)S(1)}, f32[160]{0:T(256)}, u32[]{:S(2)}) copy-start(f32[160]{0:T(256)} %param.12) | copy-start | bytes 1924
  76.3 6.2 %collective-permute-start.2 = (f16[32,88,128]{2,1,0:T(8,128)(2,1)S(1)}, f16[32,88,128]{2,1,0:T(8,128)(2,1)S(1)}, u32[]{:S(2)}, u32[]{:S(2)}) collective-permute-start(f16[32,88,128]{2,1,0:T(8,128)(2,1)S(1)} %all_to_all.23), channel_id=1, source_target_pairs={{0,1},{1,0},{2,3},{3,2},{4,5},{5,4},{6,7},{7,6},{8,9},{9,8},{10,11... | collective-permute-start | bytes 2162696 | tf_op jit(solution)/shard_map/ppermute | solution.py:471

commit v9 on v8

--- a/solution.py
+++ b/solution.py
@@ -186,12 +186,21 @@
     return value, coef
 
 
+def unscale_all(ref):
+    powers = jnp.concatenate([ref[b, MAIN : MAIN + 1, :] for b in range(ref.shape[0])], axis=0)
+    shape = powers.shape
+    value = jnp.exp2(jnp.broadcast_to(powers[:, 64:65], shape) - 14.0)
+    coef = jnp.exp2(jnp.broadcast_to(powers[:, 96:97], shape) - 14.0)
+    return [(value[b : b + 1], coef[b : b + 1]) for b in range(shape[0])]
+
+
 def sum_blocks(ref):
     value = jnp.zeros((VALUE, LANES), F32)
     main = jnp.zeros((SUB, LANES), F32)
     tile = jnp.zeros((8, LANES), F32)
+    scales = unscale_all(ref)
     for b in range(ref.shape[0]):
-        value_scale, coef_scale = unscale(ref, b)
+        value_scale, coef_scale = scales[b]
         value += ref[b, :VALUE, :] * value_scale
         main += ref[b, VALUE:MAIN, :] * coef_scale
         tile += ref[b, MAIN:CODED, :] * coef_scale
@@ -278,9 +287,10 @@
     count = kern_ref.shape[1]
     group = lane_group((8, LANES))
     coefs = []
+    scales = unscale_all(got_ref)
     for b in range(SUBS):
         at_b = slot(b // PER_BLOCK, b % PER_BLOCK)
-        value_scale, coef_scale = unscale(got_ref, at_b)
+        value_scale, coef_scale = scales[at_b]
         for j in range(4):
             resid[b * SUB : (b + 1) * SUB, j * LANES : (j + 1) * LANES] = (
                 got_ref[at_b, j * SUB : (j + 1) * SUB, :] * value_scale
@@ -308,7 +318,9 @@
     head[:, :HALF] = (kern_ref[:, :HALF].astype(F32) - corr).astype(BF16)
     for at in [*range(tile, count, tile), 0]:
         if at == 0:
-            kern = jnp.concatenate([head[...], kern_ref[:, LANES:tile]], axis=1)
+            kern = head[...]
+            if tile > LANES:
+                kern = jnp.concatenate([kern, kern_ref[:, LANES:tile]], axis=1)
         else:
             kern = kern_ref[:, at : at + tile]
         add(
@@ -421,7 +433,7 @@
         other,
         resid,
         head,
-        256,
+        128,
         add,
     )
     other_copy = pltpu.make_async_copy(
@@ -452,7 +464,7 @@
         + [
             pltpu.VMEM((HALF, c_dim), F32),
             pltpu.VMEM(base.shape, F32),
-            pltpu.SemaphoreType.DMA((4,)),
+            pltpu.SemaphoreType.DMA((8,)),
             pltpu.SemaphoreType.DMA((2,)),
         ],
         compiler_params=params(16),

time: 85.3 us -> 85.1 us (level)
  no operation moved by 1% of the time
where the time goes in v9:
time: 85.1 us; the launch traced here: 84.9 us
  blocking collectives  63.8 us (75%)
  Pallas kernels  10.4 us (12%)
  starting transfers between devices  6.97 us (8%)
  between operations  1.47 us (2%)
  local copies, waits for them, and re-layouts  1.08 us (1%)
  other arithmetic  0.95 us (1%)
    all_to_all x1, blocking collectives, local(): got = lax.all_to_all(coded, NEAR, 0, 0, tiled=True).astype(F32)  18 us
    all_to_all x1, blocking collectives, local(): lax.all_to_all(fan(core, sub, blk, batch), BLK, 0, 0, tiled=True)  17.4 us
    all_to_all x1, blocking collectives, local(): got_second = lax.all_to_all(packed, NEAR, 0, 0, tiled=True)  14.3 us
    all_to_all x1, blocking collectives, local(): far = lax.all_to_all(partial, FAR, 0, 0, tiled=True).astype(F32)  14.1 us
    ppermute x3, starting transfers between devices, swap_cores(): return lax.ppermute(value, 'c', [(0, 1), (1, 0)])  6.97 us
    pallas_call x2, Pallas kernels, terms(): pl.pallas_call(kernel, out_shape=(jax.ShapeDtypeStruct((SUBS, CODED, LANE...  5.95 us
    pallas_call x1, Pallas kernels, take_step(): pl.pallas_call(step_kernel, in_specs=[smem] * 2 + [vmem] * 7, out_specs=[...  2.32 us
  transfers between devices with their start and end apart: 3, of which 1 were waited for; matrix products, arithmetic and copies ran while one was open for 0% of the time, Pallas kernels for 8%

profile of v9, /device:TPU:1, one launch (start us, length us, event | category | flops | bytes accessed | tf_op | source)
XLA Modules:
  0.0 84.9 jit_solution(7075964613296890706)
XLA Ops:
  0.7 1.0 %copy-done.2 = bf16[128,768]{1,0:T(8,128)(2,1)S(1)} copy-done((bf16[128,768]{1,0:T(8,128)(2,1)S(1)}, bf16[128,768]{1,0:T(8,128)(2,1)}, u32[]{:S(2)}) %copy-start.2) | copy-done | bytes 196632
  1.7 0.1 fan.1
  1.8 17.4 %all_to_all.20 = bf16[8,64,768]{2,1,0:T(8,128)(2,1)S(1)} all-to-all(bf16[8,64,768]{2,1,0:T(8,128)(2,1)S(1)} %fan.1), channel_id=1, replica_groups=mesh['xl'=2,'y'=4,'zh'=4,'zl'=2,'xh'=2,'c'=2] {'xl','y'}, dimensions={0} | all-to-all | bytes 1572864 | tf_op jit(solution)/shard_map/all_to_all | solution.py:492
  19.1 0.4 multiply_reduce_fusion
  19.5 2.5 %collective-permute-start = (bf16[512,768]{1,0:T(8,128)(2,1)S(1)}, bf16[512,768]{1,0:T(8,128)(2,1)S(1)}, u32[]{:S(2)}, u32[]{:S(2)}) collective-permute-start(bf16[512,768]{1,0:T(8,128)(2,1)S(1)} %bitcast.6), channel_id=1, source_target_pairs={{0,1},{1,0},{2,3},{3,2},{4,5},{5,4},{6,7},{7,6},{8,9},{9,8},{10,11... | collective-permute-start | bytes 2359304 | tf_op jit(solution)/shard_map/ppermute | solution.py:483
  22.0 3.0 %terms.2 = (f32[32,88,128]{2,1,0:T(8,128)S(1)}, bf16[512,1024]{1,0:T(8,128)(2,1)S(1)}, bf16[3072,512]{1,0:T(8,128)(2,1)S(1)}, f32[64,256]{1,0:T(8,128)S(1)}) custom-call(bf16[512,768]{1,0:T(8,128)(2,1)S(1)} %bitcast.7, bf16[1024,768]{1,0:T(8,128)(2,1)S(1)} %copy-done, f32[1,1024]{1,0:T(1,128)S(1)} %bitcast.10, f32[1024,512]{1,0:T(8,128)S(1)} %copy-done.3, ...), custom_call_target="tpu_custom_call" | custom-call | flops 24159191040 | bytes 6291456 | tf_op jit(solution)/shard_map/terms/pallas_call | solution.py:154
  25.0 0.1 collective-permute-start.1
  25.2 2.9 %terms.3 = (f32[32,88,128]{2,1,0:T(8,128)S(1)}, bf16[512,1024]{1,0:T(8,128)(2,1)S(1)}) custom-call(bf16[512,768]{1,0:T(8,128)(2,1)S(1)} %collective-permute-done.rows_ref, bf16[1024,768]{1,0:T(8,128)(2,1)S(1)} %copy-done, f32[1,1024]{1,0:T(1,128)S(1)} %bitcast.11, bf16[3072,512]{1,0:T(8,128)(2,1)S(1)} %get-tuple-element.17.w3_ref, ...), custom_call_target="tpu_custom_call" | custom-call | flops 24159191040 | bytes 6291456 | tf_op jit(solution)/shard_map/terms/pallas_call | solution.py:154
  28.1 0.2 collective-permute-done.1.b_ref
  28.3 0.4 code.1
  28.7 0.1 convert_element_type.25
  28.8 18.0 %all_to_all.21 = f16[32,88,128]{2,1,0:T(8,128)(2,1)S(1)} all-to-all(f16[32,88,128]{2,1,0:T(8,128)(2,1)S(1)} %convert_element_type.25), channel_id=1, replica_groups=mesh['xl'=2,'y'=4,'zh'=4,'zl'=2,'xh'=2,'c'=2] {'xh','xl','zl','y'}, dimensions={0} | all-to-all | bytes 1441792 | tf_op jit(solution)/shard_map/all_to_all | solution.py:507
  46.9 0.1 convert_element_type.26.x_ref
  47.0 0.3 recode.1
  47.3 14.1 %all_to_all.22 = f16[4,88,128]{2,1,0:T(8,128)(2,1)S(1)} all-to-all(f16[4,88,128]{2,1,0:T(8,128)(2,1)S(1)} %broadcast_in_dim.4), channel_id=1, replica_groups=mesh['xl'=2,'y'=4,'zh'=4,'zl'=2,'xh'=2,'c'=2] {'zh'}, dimensions={0} | all-to-all | bytes 180224 | tf_op jit(solution)/shard_map/all_to_all | solution.py:510
  61.5 0.3 pack.1
  61.8 0.1 convert_element_type.29
  61.9 14.3 %all_to_all.23 = f16[32,88,128]{2,1,0:T(8,128)(2,1)S(1)} all-to-all(f16[32,88,128]{2,1,0:T(8,128)(2,1)S(1)} %convert_element_type.29), channel_id=1, replica_groups=mesh['xl'=2,'y'=4,'zh'=4,'zl'=2,'xh'=2,'c'=2] {'xh','xl','zl','y'}, dimensions={0} | all-to-all | bytes 1441792 | tf_op jit(solution)/shard_map/all_to_all | solution.py:513
  76.2 4.4 %collective-permute-start.2 = (f16[32,88,128]{2,1,0:T(8,128)(2,1)S(1)}, f16[32,88,128]{2,1,0:T(8,128)(2,1)S(1)}, u32[]{:S(2)}, u32[]{:S(2)}) collective-permute-start(f16[32,88,128]{2,1,0:T(8,128)(2,1)S(1)} %all_to_all.23), channel_id=1, source_target_pairs={{0,1},{1,0},{2,3},{3,2},{4,5},{5,4},{6,7},{7,6},{8,9},{9,8},{10,11... | collective-permute-start | bytes 2162696 | tf_op jit(solution)/shard_map/ppermute | solution.py:483
  81.2 0.1 pad_maximum_fusion
  81.3 0.1 convert_element_type.31.got_ref
  81.4 1.0 %half_step.1 = (f32[64,512]{1,0:T(8,128)S(1)}, f32[1024,512]{1,0:T(8,128)S(1)}) custom-call(s32[1]{0:T(128)} %bitcast.core_ref, s32[1]{0:T(128)} %bitcast.1.blk_ref, bf16[512,1024]{1,0:T(8,128)(2,1)S(1)} %get-tuple-element.21.kern_ref, f32[32,88,128]{2,1,0:T(8,128)S(1)} %convert_element_type.31.got_ref, f32[64,256]{1,0:T(8,128)S(1)} %get-tuple-element.18.e_ref.eig_ref, ...), custom_call_target="tpu_custom_call" | custom-call | flops 5368709120 | bytes 4194304 | tf_op jit(solution)/shard_map/half_step/pallas_call | solution.py:376
  82.5 0.1 convert_element_type.30.got_ref
  82.6 2.3 %take_step.1 = (f32[128,512]{1,0:T(8,128)}, f32[1024,512]{1,0:T(8,128)}) custom-call(s32[1]{0:T(128)} %bitcast.core_ref, s32[1]{0:T(128)} %bitcast.1.blk_ref, bf16[512,1024]{1,0:T(8,128)(2,1)S(1)} %get-tuple-element.16.kern_ref, f32[32,88,128]{2,1,0:T(8,128)S(1)} %convert_element_type.30.got_ref, f32[64,256]{1,0:T(8,128)S(1)} %get-tuple-element.18.e_ref.eig_ref, ...), custom_call_target="tpu_custom_call" | custom-call | flops 536870912 | bytes 8388608 | tf_op jit(solution)/shard_map/take_step/pallas_call | solution.py:455
  (17 shorter events, 0.1 us)
Async XLA Ops:
  0.6 18.5 %copy-start = (bf16[1024,768]{1,0:T(8,128)(2,1)S(1)}, bf16[1024,768]{1,0:T(8,128)(2,1)}, u32[]{:S(2)}) copy-start(bf16[1024,768]{1,0:T(8,128)(2,1)} %cen_ref.1) | copy-start | bytes 4718596
  0.7 1.0 %copy-start.2 = (bf16[128,768]{1,0:T(8,128)(2,1)S(1)}, bf16[128,768]{1,0:T(8,128)(2,1)}, u32[]{:S(2)}) copy-start(bf16[128,768]{1,0:T(8,128)(2,1)} %rows_ref.1) | copy-start | bytes 589828
  1.7 20.3 %copy-start.3 = (f32[1024,512]{1,0:T(8,128)S(1)}, f32[1024,512]{1,0:T(8,128)}, u32[]{:S(2)}) copy-start(f32[1024,512]{1,0:T(8,128)} %w_ref.2) | copy-start | bytes 6291460
  1.8 20.3 %copy-start.4 = (f32[64,160]{1,0:T(8,128)S(1)}, f32[64,160]{1,0:T(8,128)}, u32[]{:S(2)}) copy-start(f32[64,160]{1,0:T(8,128)} %e_ref.1) | copy-start | bytes 122884
  19.5 5.6 %collective-permute-start = (bf16[512,768]{1,0:T(8,128)(2,1)S(1)}, bf16[512,768]{1,0:T(8,128)(2,1)S(1)}, u32[]{:S(2)}, u32[]{:S(2)}) collective-permute-start(bf16[512,768]{1,0:T(8,128)(2,1)S(1)} %bitcast.6), channel_id=1, source_target_pairs={{0,1},{1,0},{2,3},{3,2},{4,5},{5,4},{6,7},{7,6},{8,9},{9,8},{10,11... | collective-permute-start | bytes 2359304 | tf_op jit(solution)/shard_map/ppermute | solution.py:483
  25.0 3.3 %collective-permute-start.1 = (f32[32,88,128]{2,1,0:T(8,128)S(1)}, f32[32,88,128]{2,1,0:T(8,128)S(1)}, u32[]{:S(2)}, u32[]{:S(2)}) collective-permute-start(f32[32,88,128]{2,1,0:T(8,128)S(1)} %get-tuple-element.20), channel_id=1, source_target_pairs={{0,1},{1,0},{2,3},{3,2},{4,5},{5,4},{6,7},{7,6},{8,9},{9,8},{10,11... | collective-permute-start | bytes 4325384 | tf_op jit(solution)/shard_map/ppermute | solution.py:483
  47.0 14.5 %copy-start.1 = (f32[128,512]{1,0:T(8,128)S(1)}, f32[128,512]{1,0:T(8,128)}, u32[]{:S(2)}) copy-start(f32[128,512]{1,0:T(8,128)} %targets_ref.5) | copy-start | bytes 786436
  61.8 19.4 %copy-start.5 = (f32[160]{0:T(256)S(1)}, f32[160]{0:T(256)}, u32[]{:S(2)}) copy-start(f32[160]{0:T(256)} %param.12) | copy-start | bytes 1924
  76.2 6.2 %collective-permute-start.2 = (f16[32,88,128]{2,1,0:T(8,128)(2,1)S(1)}, f16[32,88,128]{2,1,0:T(8,128)(2,1)S(1)}, u32[]{:S(2)}, u32[]{:S(2)}) collective-permute-start(f16[32,88,128]{2,1,0:T(8,128)(2,1)S(1)} %all_to_all.23), channel_id=1, source_target_pairs={{0,1},{1,0},{2,3},{3,2},{4,5},{5,4},{6,7},{7,6},{8,9},{9,8},{10,11... | collective-permute-start | bytes 2162696 | tf_op jit(solution)/shard_map/ppermute | solution.py:483

commit v10 on v9

--- a/solution.py
+++ b/solution.py
@@ -107,7 +107,9 @@
         kern_ref[:, cols] = high
         kern3[:, 2 * count + at : 2 * count + at + tile] = low
         if at == 0:
-            coef = dot3(kern[:, :HALF], eig, NN)
+            coef = jnp.zeros((n, eig.shape[1]), F32)
+            for part in split(eig):
+                coef += lax.dot_general(high[:, :HALF], part, NN, preferred_element_type=F32)
             group = lane_group((8, LANES))
             for b in range(SUBS):
                 block = coef[b * SUB : (b + 1) * SUB]

time: 85.1 us -> 85.2 us (level)
  no operation moved by 1% of the time
where the time goes in v10:
time: 85.2 us; the launch traced here: 84.9 us
  blocking collectives  63.9 us (75%)
  Pallas kernels  10.2 us (12%)
  starting transfers between devices  6.96 us (8%)
  between operations  1.47 us (2%)
  local copies, waits for them, and re-layouts  1.08 us (1%)
  other arithmetic  0.95 us (1%)
    all_to_all x1, blocking collectives, local(): got = lax.all_to_all(coded, NEAR, 0, 0, tiled=True).astype(F32)  18.1 us
    all_to_all x1, blocking collectives, local(): lax.all_to_all(fan(core, sub, blk, batch), BLK, 0, 0, tiled=True)  17.4 us
    all_to_all x1, blocking collectives, local(): far = lax.all_to_all(partial, FAR, 0, 0, tiled=True).astype(F32)  14.3 us
    all_to_all x1, blocking collectives, local(): got_second = lax.all_to_all(packed, NEAR, 0, 0, tiled=True)  14.1 us
    ppermute x3, starting transfers between devices, swap_cores(): return lax.ppermute(value, 'c', [(0, 1), (1, 0)])  6.96 us
    pallas_call x2, Pallas kernels, terms(): pl.pallas_call(kernel, out_shape=(jax.ShapeDtypeStruct((SUBS, CODED, LANE...  5.83 us
    pallas_call x1, Pallas kernels, take_step(): pl.pallas_call(step_kernel, in_specs=[smem] * 2 + [vmem] * 7, out_specs=[...  2.32 us
  transfers between devices with their start and end apart: 3, of which 1 were waited for; matrix products, arithmetic and copies ran while one was open for 0% of the time, Pallas kernels for 8%

profile of v10, /device:TPU:1, one launch (start us, length us, event | category | flops | bytes accessed | tf_op | source)
XLA Modules:
  0.0 84.9 jit_solution(8366065376819350786)
XLA Ops:
  0.7 1.0 %copy-done.2 = bf16[128,768]{1,0:T(8,128)(2,1)S(1)} copy-done((bf16[128,768]{1,0:T(8,128)(2,1)S(1)}, bf16[128,768]{1,0:T(8,128)(2,1)}, u32[]{:S(2)}) %copy-start.2) | copy-done | bytes 196632
  1.7 0.1 fan.1
  1.8 17.4 %all_to_all.20 = bf16[8,64,768]{2,1,0:T(8,128)(2,1)S(1)} all-to-all(bf16[8,64,768]{2,1,0:T(8,128)(2,1)S(1)} %fan.1), channel_id=1, replica_groups=mesh['xl'=2,'y'=4,'zh'=4,'zl'=2,'xh'=2,'c'=2] {'xl','y'}, dimensions={0} | all-to-all | bytes 1572864 | tf_op jit(solution)/shard_map/all_to_all | solution.py:494
  19.1 0.4 multiply_reduce_fusion
  19.5 2.5 %collective-permute-start = (bf16[512,768]{1,0:T(8,128)(2,1)S(1)}, bf16[512,768]{1,0:T(8,128)(2,1)S(1)}, u32[]{:S(2)}, u32[]{:S(2)}) collective-permute-start(bf16[512,768]{1,0:T(8,128)(2,1)S(1)} %bitcast.6), channel_id=1, source_target_pairs={{0,1},{1,0},{2,3},{3,2},{4,5},{5,4},{6,7},{7,6},{8,9},{9,8},{10,11... | collective-permute-start | bytes 2359304 | tf_op jit(solution)/shard_map/ppermute | solution.py:485
  22.0 3.0 %terms.2 = (f32[32,88,128]{2,1,0:T(8,128)S(1)}, bf16[512,1024]{1,0:T(8,128)(2,1)S(1)}, bf16[3072,512]{1,0:T(8,128)(2,1)S(1)}, f32[64,256]{1,0:T(8,128)S(1)}) custom-call(bf16[512,768]{1,0:T(8,128)(2,1)S(1)} %bitcast.7, bf16[1024,768]{1,0:T(8,128)(2,1)S(1)} %copy-done, f32[1,1024]{1,0:T(1,128)S(1)} %bitcast.10, f32[1024,512]{1,0:T(8,128)S(1)} %copy-done.3, ...), custom_call_target="tpu_custom_call" | custom-call | flops 24159191040 | bytes 6291456 | tf_op jit(solution)/shard_map/terms/pallas_call | solution.py:156
  25.0 0.1 collective-permute-start.1
  25.1 2.9 %terms.3 = (f32[32,88,128]{2,1,0:T(8,128)S(1)}, bf16[512,1024]{1,0:T(8,128)(2,1)S(1)}) custom-call(bf16[512,768]{1,0:T(8,128)(2,1)S(1)} %collective-permute-done.rows_ref, bf16[1024,768]{1,0:T(8,128)(2,1)S(1)} %copy-done, f32[1,1024]{1,0:T(1,128)S(1)} %bitcast.11, bf16[3072,512]{1,0:T(8,128)(2,1)S(1)} %get-tuple-element.17.w3_ref, ...), custom_call_target="tpu_custom_call" | custom-call | flops 24159191040 | bytes 6291456 | tf_op jit(solution)/shard_map/terms/pallas_call | solution.py:156
  28.0 0.3 collective-permute-done.1.b_ref
  28.3 0.4 code.1
  28.7 0.1 convert_element_type.25
  28.8 18.1 %all_to_all.21 = f16[32,88,128]{2,1,0:T(8,128)(2,1)S(1)} all-to-all(f16[32,88,128]{2,1,0:T(8,128)(2,1)S(1)} %convert_element_type.25), channel_id=1, replica_groups=mesh['xl'=2,'y'=4,'zh'=4,'zl'=2,'xh'=2,'c'=2] {'xh','xl','zl','y'}, dimensions={0} | all-to-all | bytes 1441792 | tf_op jit(solution)/shard_map/all_to_all | solution.py:509
  46.9 0.1 convert_element_type.26.x_ref
  47.0 0.3 recode.1
  47.4 14.3 %all_to_all.22 = f16[4,88,128]{2,1,0:T(8,128)(2,1)S(1)} all-to-all(f16[4,88,128]{2,1,0:T(8,128)(2,1)S(1)} %broadcast_in_dim.4), channel_id=1, replica_groups=mesh['xl'=2,'y'=4,'zh'=4,'zl'=2,'xh'=2,'c'=2] {'zh'}, dimensions={0} | all-to-all | bytes 180224 | tf_op jit(solution)/shard_map/all_to_all | solution.py:512
  61.7 0.3 pack.1
  62.1 0.1 convert_element_type.29
  62.2 14.1 %all_to_all.23 = f16[32,88,128]{2,1,0:T(8,128)(2,1)S(1)} all-to-all(f16[32,88,128]{2,1,0:T(8,128)(2,1)S(1)} %convert_element_type.29), channel_id=1, replica_groups=mesh['xl'=2,'y'=4,'zh'=4,'zl'=2,'xh'=2,'c'=2] {'xh','xl','zl','y'}, dimensions={0} | all-to-all | bytes 1441792 | tf_op jit(solution)/shard_map/all_to_all | solution.py:515
  76.3 4.4 %collective-permute-start.2 = (f16[32,88,128]{2,1,0:T(8,128)(2,1)S(1)}, f16[32,88,128]{2,1,0:T(8,128)(2,1)S(1)}, u32[]{:S(2)}, u32[]{:S(2)}) collective-permute-start(f16[32,88,128]{2,1,0:T(8,128)(2,1)S(1)} %all_to_all.23), channel_id=1, source_target_pairs={{0,1},{1,0},{2,3},{3,2},{4,5},{5,4},{6,7},{7,6},{8,9},{9,8},{10,11... | collective-permute-start | bytes 2162696 | tf_op jit(solution)/shard_map/ppermute | solution.py:485
  81.3 0.1 pad_maximum_fusion
  81.4 0.1 convert_element_type.31.got_ref
  81.5 1.0 %half_step.1 = (f32[64,512]{1,0:T(8,128)S(1)}, f32[1024,512]{1,0:T(8,128)S(1)}) custom-call(s32[1]{0:T(128)} %bitcast.core_ref, s32[1]{0:T(128)} %bitcast.1.blk_ref, bf16[512,1024]{1,0:T(8,128)(2,1)S(1)} %get-tuple-element.21.kern_ref, f32[32,88,128]{2,1,0:T(8,128)S(1)} %convert_element_type.31.got_ref, f32[64,256]{1,0:T(8,128)S(1)} %get-tuple-element.18.e_ref.eig_ref, ...), custom_call_target="tpu_custom_call" | custom-call | flops 5368709120 | bytes 4194304 | tf_op jit(solution)/shard_map/half_step/pallas_call | solution.py:378
  82.5 0.1 convert_element_type.30.got_ref
  82.6 2.3 %take_step.1 = (f32[128,512]{1,0:T(8,128)}, f32[1024,512]{1,0:T(8,128)}) custom-call(s32[1]{0:T(128)} %bitcast.core_ref, s32[1]{0:T(128)} %bitcast.1.blk_ref, bf16[512,1024]{1,0:T(8,128)(2,1)S(1)} %get-tuple-element.16.kern_ref, f32[32,88,128]{2,1,0:T(8,128)S(1)} %convert_element_type.30.got_ref, f32[64,256]{1,0:T(8,128)S(1)} %get-tuple-element.18.e_ref.eig_ref, ...), custom_call_target="tpu_custom_call" | custom-call | flops 536870912 | bytes 8388608 | tf_op jit(solution)/shard_map/take_step/pallas_call | solution.py:457
  (17 shorter events, 0.1 us)
Async XLA Ops:
  0.6 18.5 %copy-start = (bf16[1024,768]{1,0:T(8,128)(2,1)S(1)}, bf16[1024,768]{1,0:T(8,128)(2,1)}, u32[]{:S(2)}) copy-start(bf16[1024,768]{1,0:T(8,128)(2,1)} %cen_ref.1) | copy-start | bytes 4718596
  0.7 1.0 %copy-start.2 = (bf16[128,768]{1,0:T(8,128)(2,1)S(1)}, bf16[128,768]{1,0:T(8,128)(2,1)}, u32[]{:S(2)}) copy-start(bf16[128,768]{1,0:T(8,128)(2,1)} %rows_ref.1) | copy-start | bytes 589828
  1.7 20.3 %copy-start.3 = (f32[1024,512]{1,0:T(8,128)S(1)}, f32[1024,512]{1,0:T(8,128)}, u32[]{:S(2)}) copy-start(f32[1024,512]{1,0:T(8,128)} %w_ref.2) | copy-start | bytes 6291460
  1.8 20.3 %copy-start.4 = (f32[64,160]{1,0:T(8,128)S(1)}, f32[64,160]{1,0:T(8,128)}, u32[]{:S(2)}) copy-start(f32[64,160]{1,0:T(8,128)} %e_ref.1) | copy-start | bytes 122884
  19.5 5.6 %collective-permute-start = (bf16[512,768]{1,0:T(8,128)(2,1)S(1)}, bf16[512,768]{1,0:T(8,128)(2,1)S(1)}, u32[]{:S(2)}, u32[]{:S(2)}) collective-permute-start(bf16[512,768]{1,0:T(8,128)(2,1)S(1)} %bitcast.6), channel_id=1, source_target_pairs={{0,1},{1,0},{2,3},{3,2},{4,5},{5,4},{6,7},{7,6},{8,9},{9,8},{10,11... | collective-permute-start | bytes 2359304 | tf_op jit(solution)/shard_map/ppermute | solution.py:485
  25.0 3.3 %collective-permute-start.1 = (f32[32,88,128]{2,1,0:T(8,128)S(1)}, f32[32,88,128]{2,1,0:T(8,128)S(1)}, u32[]{:S(2)}, u32[]{:S(2)}) collective-permute-start(f32[32,88,128]{2,1,0:T(8,128)S(1)} %get-tuple-element.20), channel_id=1, source_target_pairs={{0,1},{1,0},{2,3},{3,2},{4,5},{5,4},{6,7},{7,6},{8,9},{9,8},{10,11... | collective-permute-start | bytes 4325384 | tf_op jit(solution)/shard_map/ppermute | solution.py:485
  47.0 14.7 %copy-start.1 = (f32[128,512]{1,0:T(8,128)S(1)}, f32[128,512]{1,0:T(8,128)}, u32[]{:S(2)}) copy-start(f32[128,512]{1,0:T(8,128)} %targets_ref.5) | copy-start | bytes 786436
  62.1 19.2 %copy-start.5 = (f32[160]{0:T(256)S(1)}, f32[160]{0:T(256)}, u32[]{:S(2)}) copy-start(f32[160]{0:T(256)} %param.12) | copy-start | bytes 1924
  76.3 6.2 %collective-permute-start.2 = (f16[32,88,128]{2,1,0:T(8,128)(2,1)S(1)}, f16[32,88,128]{2,1,0:T(8,128)(2,1)S(1)}, u32[]{:S(2)}, u32[]{:S(2)}) collective-permute-start(f16[32,88,128]{2,1,0:T(8,128)(2,1)S(1)} %all_to_all.23), channel_id=1, source_target_pairs={{0,1},{1,0},{2,3},{3,2},{4,5},{5,4},{6,7},{7,6},{8,9},{9,8},{10,11... | collective-permute-start | bytes 2162696 | tf_op jit(solution)/shard_map/ppermute | solution.py:485
